TPU v7x, 256 devices: a whole 4x4x8 slice. The times are simulated.
256 devices in a mesh: enc: 16 (over x, y), blk: 16 (over z, core).
Axes of the slice: x: 4, y: 4, z: 8, core: 2. Of those that a mesh axis runs over, the one named last changes fastest.
Arguments:
- observations: bfloat16 [131072, 128], P(('enc', 'blk')), may hold values from -6 to 6
- lon_index: int32 [256, 512], P(('enc', 'blk')), may hold values from 0 to 1439
- live_count: int32 [256, 256], P(('enc', 'blk')), may hold values from 0 to 2, as said below
- w_in: bfloat16 [128, 512], replicated, may hold values from -0.5 to 0.5
- w_out: bfloat16 [512, 512], replicated, may hold values from -0.25 to 0.25
- w_spec: float32 [256, 512], replicated, may hold values from -4 to 4
- north: float32 [256, 512], P(('enc', 'blk')), may hold values from -0.8 to 0.8
- south: float32 [256, 512], P(('enc', 'blk')), may hold values from -0.8 to 0.8
- w_mix: bfloat16 [512, 512], replicated, may hold values from -0.25 to 0.25
- loss_sensitivity: bfloat16 [256, 1440, 512], P(('enc', 'blk')), may hold values from -6 to 6
Outputs:
- predicted_state: bfloat16 [256, 1440, 512], P(('enc', 'blk'))
- entry_matrix_slope: float32 [128, 512], replicated
- exit_matrix_slope: float32 [512, 512], replicated
- blend_matrix_slope: float32 [512, 512], replicated
- observation_slope: bfloat16 [131072, 128], P(('enc', 'blk'))
Inputs may be any that keep to these rules, and one draw needn't show every extreme that they name: In every draw some cycle r has live_count[r, s] = 2 for every source s.
All inputs are finite; a program needn't handle non-finite values.
Results may differ from a plain program's by a relative error of at most 0.0095.
Values may be sent and summed in bfloat16 or wider, within the bound.
No kernel may reach another device: no remote copies, remote signals or barrier semaphores. Data moves between devices by JAX's collectives and lax.ppermute only.
A program may use at most 64 MiB of HBM per device.

v0:
```python
import math

import jax
import jax.numpy as jnp
from jax import lax
from jax.sharding import PartitionSpec as P

CODE_BREADTH = 512
LON = 1440
MODES = 128
CAP = 2


def extended(block, sides, width):
    for axis, dim in sides:
        count = lax.axis_size(axis)
        forward = [(i, i + 1) for i in range(count - 1)]
        backward = [(target, source) for source, target in forward]
        low = lax.ppermute(
            lax.slice_in_dim(block, block.shape[dim] - width, None, axis=dim), axis, forward
        )
        high = lax.ppermute(lax.slice_in_dim(block, 0, width, axis=dim), axis, backward)
        block = jnp.concatenate([low, block, high], axis=dim)
    return block


def from_behind(value, axis, steps):
    count = lax.axis_size(axis)
    initial, last = (max(0, -steps), min(count, count - steps))
    return lax.ppermute(value, axis, [(source, source + steps) for source in range(initial, last)])


def tables():
    wavenum = jnp.arange(MODES, dtype=jnp.int32)
    lon_pos = jnp.arange(LON, dtype=jnp.int32)
    phases = (wavenum[:, None] * lon_pos[None, :] % LON).astype(jnp.float32) * (2.0 * math.pi / LON)
    forward = jnp.concatenate([jnp.cos(phases), -jnp.sin(phases)], 0).astype(jnp.bfloat16)
    weight = jnp.where(wavenum == 0, 1.0, 2.0).astype(jnp.float32) / LON
    inverse = jnp.concatenate(
        [jnp.cos(phases) * weight[:, None], -jnp.sin(phases) * weight[:, None]], 0
    ).T.astype(jnp.bfloat16)
    return (forward, inverse)


def silu_grad(values):
    logistic = jax.nn.sigmoid(values)
    return logistic * (1.0 + values * (1.0 - logistic))


def cell_table(lon_row, count_row):
    is_live = (jnp.arange(CAP, dtype=jnp.int32)[None, :] < count_row[:, None]).reshape(-1)
    matches = (lon_row[None, :] == jnp.arange(LON, dtype=jnp.int32)[:, None]) & is_live[None, :]
    return (matches.astype(jnp.bfloat16), jnp.sum(matches.astype(jnp.float32), axis=1))


def encode(rows, w_in, w_out):
    pre1 = jnp.dot(rows, w_in, preferred_element_type=jnp.float32)
    hidden = jax.nn.silu(pre1).astype(jnp.bfloat16)
    latent = jnp.dot(hidden, w_out, preferred_element_type=jnp.float32).astype(jnp.bfloat16)
    return (pre1, hidden, latent)


def encoder_grads(rows, pre1, hidden, grad_latent, w_in, w_out):
    out_local = jnp.dot(hidden.T, grad_latent, preferred_element_type=jnp.float32)
    grad_hidden = jnp.dot(grad_latent, w_out.T, preferred_element_type=jnp.float32)
    grad_pre1 = (grad_hidden * silu_grad(pre1)).astype(jnp.bfloat16)
    in_local = jnp.dot(rows.T, grad_pre1, preferred_element_type=jnp.float32)
    row_grads = jnp.dot(grad_pre1, w_in.T, preferred_element_type=jnp.float32).astype(jnp.bfloat16)
    return (in_local, out_local, row_grads)


def shards(
    observations, lon_index, live_count, w_in, w_out, w_spec, north, south, w_mix, loss_sensitivity
):
    enc_count = lax.axis_size("enc")
    blk_count = lax.axis_size("blk")
    devices = enc_count * blk_count
    slot_total = observations.shape[0]
    forward, inverse = tables()
    pre1, hidden, latent = encode(observations, w_in, w_out)
    outgoing = latent.reshape(enc_count, blk_count, CAP, CODE_BREADTH)
    arrived = lax.all_to_all(
        lax.all_to_all(outgoing, "enc", split_axis=0, concat_axis=0, tiled=True),
        "blk",
        split_axis=1,
        concat_axis=1,
        tiled=True,
    )
    lat_rows = arrived.reshape(slot_total, CODE_BREADTH)
    onehot, occupancy = cell_table(lon_index[0], live_count[0])
    denom = jnp.maximum(occupancy, 1.0)[:, None]
    grid_sum = jnp.dot(onehot, lat_rows, preferred_element_type=jnp.float32)
    resampled_field = (grid_sum / denom).astype(jnp.bfloat16)
    spectrum = jnp.dot(forward, resampled_field, preferred_element_type=jnp.float32)
    border = extended(resampled_field[None], ((("enc", "blk"), 0),), 1)
    spec_prev = jnp.dot(forward, border[0], preferred_element_type=jnp.float32)
    spec_next = jnp.dot(forward, border[2], preferred_element_type=jnp.float32)
    north_row = north[0][None, :]
    south_row = south[0][None, :]
    blended_fourier_modes = (
        spectrum * w_spec + north_row * spec_prev + south_row * spec_next
    ).astype(jnp.bfloat16)
    azimuth = jnp.dot(inverse, blended_fourier_modes, preferred_element_type=jnp.float32).astype(
        jnp.bfloat16
    )
    before_nonlinearity = jnp.dot(azimuth, w_mix, preferred_element_type=jnp.float32)
    predicted_state = (
        resampled_field.astype(jnp.float32) + jax.nn.silu(before_nonlinearity)
    ).astype(jnp.bfloat16)
    grad_pre = (loss_sensitivity[0].astype(jnp.float32) * silu_grad(before_nonlinearity)).astype(
        jnp.bfloat16
    )
    mix_local = jnp.dot(azimuth.T, grad_pre, preferred_element_type=jnp.float32)
    gridding_factor = 1.0 / math.sqrt(devices * LON)
    grad_az = jnp.dot(grad_pre, w_mix.T, preferred_element_type=jnp.float32).astype(jnp.bfloat16)
    blend_matrix_slope_local = jnp.dot(inverse.T, grad_az, preferred_element_type=jnp.float32)
    from_next = from_behind(north_row * blend_matrix_slope_local, ("enc", "blk"), -1)
    from_prev = from_behind(south_row * blend_matrix_slope_local, ("enc", "blk"), 1)
    grad_spec = (w_spec * blend_matrix_slope_local + from_next + from_prev).astype(jnp.bfloat16)
    grad_grid = loss_sensitivity[0].astype(jnp.float32) + jnp.dot(
        forward.T, grad_spec, preferred_element_type=jnp.float32
    )
    scaled = (grad_grid / denom).astype(jnp.bfloat16)
    grad_rows = jnp.dot(onehot.T, scaled, preferred_element_type=jnp.float32).astype(jnp.bfloat16)
    returned = lax.all_to_all(
        lax.all_to_all(
            grad_rows.reshape(enc_count, blk_count, CAP, CODE_BREADTH),
            "enc",
            split_axis=0,
            concat_axis=0,
            tiled=True,
        ),
        "blk",
        split_axis=1,
        concat_axis=1,
        tiled=True,
    )
    grad_latent = returned.reshape(slot_total, CODE_BREADTH)
    in_local, out_local, observation_slope = encoder_grads(
        observations, pre1, hidden, grad_latent, w_in, w_out
    )
    observed_factor = 1.0 / math.sqrt(devices * slot_total)
    input_gradient_total, output_gradient_total, blend_matrix_slope_summed = lax.psum(
        (in_local, out_local, mix_local), ("enc", "blk")
    )
    return (
        predicted_state[None],
        input_gradient_total * observed_factor,
        output_gradient_total * observed_factor,
        blend_matrix_slope_summed * gridding_factor,
        observation_slope,
    )


def solution(mesh):
    placed = (
        P(("enc", "blk"), None),
        P(("enc", "blk"), None),
        P(("enc", "blk"), None),
        P(),
        P(),
        P(),
        P(("enc", "blk"), None),
        P(("enc", "blk"), None),
        P(),
        P(("enc", "blk"), None, None),
    )
    return jax.shard_map(
        shards,
        mesh=mesh,
        in_specs=placed,
        out_specs=(P(("enc", "blk"), None, None), P(), P(), P(), P(("enc", "blk"), None)),
        check_vma=False,
    )
```

profile of v0, /device:TPU:1, one launch (start us, length us, event | category | flops | bytes accessed | tf_op | source)
XLA Modules:
  0.0 426.2 jit_solution(8997733929521939271)
XLA Ops:
  7.2 1.3 fusion.52
  9.5 1.5 convolution_convert_fusion.2
  11.2 17.7 %all_to_all.20 = bf16[16,16,2,512]{3,2,1,0:T(2,128)(2,1)S(1)} all-to-all(bf16[16,16,2,512]{3,2,1,0:T(2,128)(2,1)S(1)} %reshape.48), channel_id=1, replica_groups=mesh['enc'=16,'blk'=16] {'enc'}, dimensions={0} | all-to-all | bytes 1048576 | tf_op jit(solution)/shard_map/all_to_all | solution.py:83
  28.9 1.3 copy.30
  30.2 10.6 %all-to-all-start.1 = ((bf16[16,16,2,512]{3,2,0,1:T(2,128)(2,1)}), bf16[16,16,2,512]{3,2,0,1:T(2,128)(2,1)S(1)}, u32[]{:S(2)}, u32[]{:S(2)}) async-start(bf16[16,16,2,512]{3,2,0,1:T(2,128)(2,1)} %copy.30), calls=%async_computation.1 | async-start | bytes 1048576 | tf_op jit(solution)/shard_map/all_to_all | solution.py:82
  41.6 16.5 %all-to-all-done.1 = bf16[16,16,2,512]{3,2,0,1:T(2,128)(2,1)S(1)} async-done(((bf16[16,16,2,512]{3,2,0,1:T(2,128)(2,1)}), bf16[16,16,2,512]{3,2,0,1:T(2,128)(2,1)S(1)}, u32[]{:S(2)}, u32[]{:S(2)}) %all-to-all-start.1) | async-done | bytes 524320 | tf_op jit(solution)/shard_map/all_to_all | solution.py:82
  59.9 2.1 collective-permute-start.1
  61.9 3.6 collective-permute-start
  65.6 3.5 fusion.44
  69.1 4.1 multiply_convert_fusion.2
  73.2 1.4 convolution_multiply_fusion.1
  74.5 6.1 %collective-permute-done.1 = bf16[1,1440,512]{2,1,0:T(8,128)(2,1)S(1)} collective-permute-done((bf16[1,1440,512]{2,1,0:T(8,128)(2,1)S(1)}, bf16[1,1440,512]{2,1,0:T(8,128)(2,1)S(1)}, u32[]{:S(2)}, u32[]{:S(2)}) %collective-permute-start.1) | collective-permute-done | bytes 1474592 | tf_op jit(solution)/shard_map/ppermute | solution.py:22
  80.7 1.4 fusion.24
  82.0 1.1 copy-done.13
  83.2 2.9 convolution_convert_fusion.1
  86.1 5.2 %fusion = (bf16[1440,512]{1,0:T(8,128)(2,1)S(1)}, bf16[1,1440,512]{2,1,0:T(8,128)(2,1)}) fusion(bf16[1,1440,512]{2,1,0:T(8,128)(2,1)} %param.19, bf16[1440,512]{1,0:T(8,128)(2,1)} %copy-done.12, bf16[1440,512]{1,0:T(8,128)(2,1)S(1)} %convolution_convert_fusion.1, bf16[512,512]{1,0:T(8,128)(2,1)S(1)} %copy-done), kind=kOutput, calls=%fused_computation.4 | convolution fusion | flops 765296640 | bytes 7897088 | tf_op jit(solution)/shard_map/dot_general | solution.py:106
  91.3 4.2 broadcast_multiply_fusion.3
  95.5 1.9 collective-permute-start.2
  97.4 4.4 %collective-permute-start.3 = (f32[256,512]{1,0:T(8,128)}, f32[256,512]{1,0:T(8,128)S(1)}, u32[]{:S(2)}, u32[]{:S(2)}) collective-permute-start(f32[256,512]{1,0:T(8,128)} %get-tuple-element.41), channel_id=1, source_target_pairs={{0,1},{1,2},{2,3},{3,4},{4,5},{5,6},{6,7},{7,8},{8,9},{9,10},{10,1... | collective-permute-start | bytes 1572872 | tf_op jit(solution)/shard_map/ppermute | solution.py:30
  101.8 5.0 %collective-permute-done.2 = f32[256,512]{1,0:T(8,128)S(1)} collective-permute-done((f32[256,512]{1,0:T(8,128)}, f32[256,512]{1,0:T(8,128)S(1)}, u32[]{:S(2)}, u32[]{:S(2)}) %collective-permute-start.2) | collective-permute-done | bytes 524320 | tf_op jit(solution)/shard_map/ppermute | solution.py:30
  106.7 1.3 collective-permute-done.3
  108.8 3.9 fusion.17
  112.9 12.9 %all_to_all.21 = bf16[16,16,2,512]{3,2,1,0:T(2,128)(2,1)S(1)} all-to-all(bf16[16,16,2,512]{3,2,1,0:T(2,128)(2,1)S(1)} %reshape.50), channel_id=1, replica_groups=mesh['enc'=16,'blk'=16] {'enc'}, dimensions={0} | all-to-all | bytes 1048576 | tf_op jit(solution)/shard_map/all_to_all | solution.py:126
  125.8 1.3 copy.32
  127.1 11.4 %all-to-all-start.3 = ((bf16[16,16,2,512]{3,2,0,1:T(2,128)(2,1)}), bf16[16,16,2,512]{3,2,0,1:T(2,128)(2,1)S(1)}, u32[]{:S(2)}, u32[]{:S(2)}) async-start(bf16[16,16,2,512]{3,2,0,1:T(2,128)(2,1)} %copy.32), calls=%async_computation.3 | async-start | bytes 1048576 | tf_op jit(solution)/shard_map/all_to_all | solution.py:125
  138.5 3.3 fusion.53
  141.9 14.0 %all-to-all-done.3 = bf16[16,16,2,512]{3,2,0,1:T(2,128)(2,1)S(1)} async-done(((bf16[16,16,2,512]{3,2,0,1:T(2,128)(2,1)}), bf16[16,16,2,512]{3,2,0,1:T(2,128)(2,1)S(1)}, u32[]{:S(2)}, u32[]{:S(2)}) %all-to-all-start.3) | async-done | bytes 524320 | tf_op jit(solution)/shard_map/all_to_all | solution.py:125
  156.6 2.0 fusion.20
  158.5 1.5 fusion.51
  162.0 253.2 %all-reduce.3.cloned.1.call-done = (f32[128,512]{0,1:T(8,128)}, f32[512,512]{1,0:T(8,128)}, f32[512,512]{1,0:T(8,128)}) async-done(((f32[128,512]{0,1:T(8,128)}, f32[512,512]{1,0:T(8,128)}, f32[512,512]{1,0:T(8,128)}), (f32[128,512]{0,1:T(8,128)}, f32[512,512]{1,0:T(8,128)}, f32[512,512]{1,0:T(8,128)})) %all-reduce.3.cloned.1.call-update) | async-done | bytes 2359312 | tf_op jit(solution)/shard_map/psum | solution.py:143
  415.3 1.1 broadcast_multiply_fusion.4
  417.2 1.1 broadcast_multiply_fusion.1
  (58 shorter events, 9.4 us)
Async XLA Ops:
  7.2 78.9 %copy-start = (bf16[512,512]{1,0:T(8,128)(2,1)S(1)}, bf16[512,512]{1,0:T(8,128)(2,1)}, u32[]{:S(2)}) copy-start(bf16[512,512]{1,0:T(8,128)(2,1)} %param.18) | copy-start | bytes 1572868
  8.5 1.0 copy-start.2
  11.2 29.6 %copy-start.11 = (s32[1,256]{1,0:T(1,128)S(1)}, s32[1,256]{1,0:T(1,128)}, u32[]{:S(2)}) copy-start(s32[1,256]{1,0:T(1,128)} %param.12) | copy-start | bytes 3076
  11.2 29.9 %copy-start.19 = (s32[1,512]{1,0:T(1,128)S(1)}, s32[1,512]{1,0:T(1,128)}, u32[]{:S(2)}) copy-start(s32[1,512]{1,0:T(1,128)} %param.11) | copy-start | bytes 6148
  30.2 27.9 %all-to-all-start.1 = ((bf16[16,16,2,512]{3,2,0,1:T(2,128)(2,1)}), bf16[16,16,2,512]{3,2,0,1:T(2,128)(2,1)S(1)}, u32[]{:S(2)}, u32[]{:S(2)}) async-start(bf16[16,16,2,512]{3,2,0,1:T(2,128)(2,1)} %copy.30), calls=%async_computation.1 | async-start | bytes 1048576 | tf_op jit(solution)/shard_map/all_to_all | solution.py:82
  59.8 14.7 %copy-start.12 = (bf16[1440,512]{1,0:T(8,128)(2,1)}, bf16[1440,512]{1,0:T(8,128)(2,1)S(1)}, u32[]{:S(2)}) copy-start(bf16[1440,512]{1,0:T(8,128)(2,1)S(1)} %divide_convert_fusion.1) | copy-start | bytes 4423684
  59.8 13.3 %copy-start.14 = (f32[256,512]{1,0:T(8,128)S(1)}, f32[256,512]{1,0:T(8,128)}, u32[]{:S(2)}) copy-start(f32[256,512]{1,0:T(8,128)} %param.15) | copy-start | bytes 1572868
  59.9 20.8 %collective-permute-start.1 = (bf16[1,1440,512]{2,1,0:T(8,128)(2,1)S(1)}, bf16[1,1440,512]{2,1,0:T(8,128)(2,1)S(1)}, u32[]{:S(2)}, u32[]{:S(2)}) collective-permute-start(bf16[1,1440,512]{2,1,0:T(8,128)(2,1)S(1)} %bitcast.52), channel_id=1, source_target_pairs={{1,0},{2,1},{3,2},{4,3},{5,4},{6,5},{7,6},{8,7},{9,8},{10,9},{11,1... | collective-permute-start | bytes 4423688 | tf_op jit(solution)/shard_map/ppermute | solution.py:22
  61.9 20.1 %collective-permute-start = (bf16[1,1440,512]{2,1,0:T(8,128)(2,1)S(1)}, bf16[1,1440,512]{2,1,0:T(8,128)(2,1)S(1)}, u32[]{:S(2)}, u32[]{:S(2)}) collective-permute-start(bf16[1,1440,512]{2,1,0:T(8,128)(2,1)S(1)} %bitcast.53), channel_id=1, source_target_pairs={{0,1},{1,2},{2,3},{3,4},{4,5},{5,6},{6,7},{7,8},{8,9},{9,10},{10,1... | collective-permute-start | bytes 4423688 | tf_op jit(solution)/shard_map/ppermute | solution.py:19
  69.1 14.1 %copy-start.8 = (bf16[128,1440]{1,0:T(8,128)(2,1)}, bf16[128,1440]{1,0:T(8,128)(2,1)S(1)}, u32[]{:S(2)}) copy-start(bf16[128,1440]{1,0:T(8,128)(2,1)S(1)} %get-tuple-element.45) | copy-start | bytes 1105924
  69.1 14.1 %copy-start.9 = (bf16[128,1440]{1,0:T(8,128)(2,1)}, bf16[128,1440]{1,0:T(8,128)(2,1)S(1)}, u32[]{:S(2)}) copy-start(bf16[128,1440]{1,0:T(8,128)(2,1)S(1)} %get-tuple-element.46) | copy-start | bytes 1105924
  73.2 10.0 %copy-start.10 = (bf16[128,1440]{1,0:T(8,128)(2,1)}, bf16[128,1440]{1,0:T(8,128)(2,1)S(1)}, u32[]{:S(2)}) copy-start(bf16[128,1440]{1,0:T(8,128)(2,1)S(1)} %get-tuple-element.42) | copy-start | bytes 1105924
  73.2 7.5 %copy-start.17 = (f32[1,512]{1,0:T(1,128)S(1)}, f32[1,512]{1,0:T(1,128)}, u32[]{:S(2)}) copy-start(f32[1,512]{1,0:T(1,128)} %param.17) | copy-start | bytes 6148
  80.7 2.5 copy-start.18
  82.0 1.1 copy-start.13
  91.3 4.2 copy-start.1
  95.5 11.3 %collective-permute-start.2 = (f32[256,512]{1,0:T(8,128)}, f32[256,512]{1,0:T(8,128)S(1)}, u32[]{:S(2)}, u32[]{:S(2)}) collective-permute-start(f32[256,512]{1,0:T(8,128)} %get-tuple-element.40), channel_id=1, source_target_pairs={{1,0},{2,1},{3,2},{4,3},{5,4},{6,5},{7,6},{8,7},{9,8},{10,9},{11,1... | collective-permute-start | bytes 1572872 | tf_op jit(solution)/shard_map/ppermute | solution.py:30
  97.4 10.6 %collective-permute-start.3 = (f32[256,512]{1,0:T(8,128)}, f32[256,512]{1,0:T(8,128)S(1)}, u32[]{:S(2)}, u32[]{:S(2)}) collective-permute-start(f32[256,512]{1,0:T(8,128)} %get-tuple-element.41), channel_id=1, source_target_pairs={{0,1},{1,2},{2,3},{3,4},{4,5},{5,6},{6,7},{7,8},{8,9},{9,10},{10,1... | collective-permute-start | bytes 1572872 | tf_op jit(solution)/shard_map/ppermute | solution.py:30
  108.0 0.8 copy-start.16
  127.1 28.7 %all-to-all-start.3 = ((bf16[16,16,2,512]{3,2,0,1:T(2,128)(2,1)}), bf16[16,16,2,512]{3,2,0,1:T(2,128)(2,1)S(1)}, u32[]{:S(2)}, u32[]{:S(2)}) async-start(bf16[16,16,2,512]{3,2,0,1:T(2,128)(2,1)} %copy.32), calls=%async_computation.3 | async-start | bytes 1048576 | tf_op jit(solution)/shard_map/all_to_all | solution.py:125
  138.5 276.8 %all-reduce.3.cloned.1.call-start = ((), (), s32[]{:S(2)}) async-start(), calls=%async_computation.4 | async-start | bytes 4718592 | tf_op jit(solution)/shard_map/psum | solution.py:143
  141.9 14.7 %copy-start.15 = (bf16[512,512]{1,0:T(8,128)(2,1)S(1)}, bf16[512,512]{1,0:T(8,128)(2,1)}, u32[]{:S(2)}) copy-start(bf16[512,512]{1,0:T(8,128)(2,1)} %param.14) | copy-start | bytes 1572868
  156.5 2.0 copy-start.3
  158.5 1.5 copy-start.6
  160.0 1.1 copy-start.7
  415.3 2.0 copy-start.5
  415.3 3.1 copy-start.4
Sparse Core Ops, SparseCore 0:
  161.2 254.0 all-reduce.2
where the time goes:
time: 428 us; the launch traced here: 426 us
  waiting for transfers between devices  296 us (69%)
  starting transfers between devices  34 us (8%)
  matrix products  31.5 us (7%)
  blocking collectives  30.6 us (7%)
  between operations  14.3 us (3%)
  other arithmetic  11.5 us (3%)
  local copies, waits for them, and re-layouts  8.33 us (2%)
    psum x1, waiting for transfers between devices, shards(): lax.psum((in_local, out_local, mix_local), ('enc', 'blk'))  253 us
    all_to_all x1, blocking collectives, shards(): lax.all_to_all(outgoing, 'enc', split_axis=0, concat_axis=0, tiled=True)  17.7 us
    all_to_all x1, waiting for transfers between devices, shards(): lax.all_to_all(lax.all_to_all(outgoing, 'enc', split_axis=0, concat_axis=...  16.5 us
    all_to_all x1, waiting for transfers between devices, shards(): lax.all_to_all(lax.all_to_all(grad_rows.reshape(enc_count, blk_count, CAP...  14 us
    all_to_all x1, blocking collectives, shards(): lax.all_to_all(grad_rows.reshape(enc_count, blk_count, CAP, CODE_BREADTH)...  12.9 us
    all_to_all x1, starting transfers between devices, shards(): lax.all_to_all(lax.all_to_all(grad_rows.reshape(enc_count, blk_count, CAP...  11.4 us
    all_to_all x1, starting transfers between devices, shards(): lax.all_to_all(lax.all_to_all(outgoing, 'enc', split_axis=0, concat_axis=...  10.6 us
  transfers between devices with their start and end apart: 7, of which 6 were waited for; matrix products, arithmetic and copies ran while one was open for 4% of the time, Pallas kernels for 0%

commit v1 on v0

v1 whole, which is shorter than its diff:
```python
import math

import jax
import jax.numpy as jnp
from jax import lax
from jax.sharding import PartitionSpec as P

LON = 1440
MODES = 128
CAP = 2
BOTH = ("enc", "blk")
BF16 = jnp.bfloat16
F32 = jnp.float32


def dot(a, b):
    return jnp.dot(a, b, preferred_element_type=F32)


def dot_ta(a, b):
    return lax.dot_general(a, b, (((0,), (0,)), ((), ())), preferred_element_type=F32)


def dot_tb(a, b):
    return lax.dot_general(a, b, (((1,), (1,)), ((), ())), preferred_element_type=F32)


def fourier_table():
    wavenum = jnp.arange(MODES, dtype=jnp.int32)
    lon_pos = jnp.arange(LON, dtype=jnp.int32)
    phases = (wavenum[:, None] * lon_pos[None, :] % LON).astype(F32) * (2.0 * math.pi / LON)
    return jnp.concatenate([jnp.cos(phases), -jnp.sin(phases)], 0).astype(BF16)


def silu_grad(values):
    logistic = jax.nn.sigmoid(values)
    return logistic * (1.0 + values * (1.0 - logistic))


def exchange(rows, enc_count, blk_count):
    blocks = rows.reshape(enc_count * blk_count, CAP, rows.shape[-1])
    out = lax.all_to_all(blocks, BOTH, split_axis=0, concat_axis=0, tiled=True)
    return out.reshape(rows.shape)


def neighbour(value, count, step):
    pairs = [(i, i + step) for i in range(count) if 0 <= i + step < count]
    return lax.ppermute(value, BOTH, pairs)


def reduce_all(total, enc_count, blk_count):
    rows, width = total.shape
    half = width // 2
    swap = [(j, j ^ 1) for j in range(blk_count)]
    core = lax.axis_index("blk") % 2
    mine = lax.dynamic_slice(total, (0, core * half), (rows, half))
    other = lax.dynamic_slice(total, (0, (1 - core) * half), (rows, half))
    summed = mine + lax.ppermute(other.astype(BF16), "blk", swap).astype(F32)
    parts = lax.all_to_all(
        summed.astype(BF16).reshape(enc_count, rows // enc_count, half), "enc", split_axis=0, concat_axis=0, tiled=True
    )
    block = jnp.sum(parts.astype(F32), axis=0).astype(BF16)
    step = 2
    while step < blk_count:
        partner = lax.ppermute(block, "blk", [(j, j ^ step) for j in range(blk_count)])
        block = (block.astype(F32) + partner.astype(F32)).astype(BF16)
        step *= 2
    whole = lax.all_to_all(
        jnp.broadcast_to(block[None], (enc_count,) + block.shape), "enc", split_axis=0, concat_axis=0, tiled=True
    ).reshape(rows, half)
    theirs = lax.ppermute(whole, "blk", swap)
    low = jnp.where(core == 0, whole, theirs)
    high = jnp.where(core == 0, theirs, whole)
    return jnp.concatenate([low, high], axis=1).astype(F32)


def shards(
    observations, lon_index, live_count, w_in, w_out, w_spec, north, south, w_mix, loss_sensitivity
):
    enc_count = lax.axis_size("enc")
    blk_count = lax.axis_size("blk")
    devices = enc_count * blk_count
    slots = observations.shape[0]
    rows = exchange(observations, enc_count, blk_count)

    lon = lon_index[0]
    live = (jnp.arange(CAP, dtype=jnp.int32)[None, :] < live_count[0][:, None]).reshape(-1)
    cell = jnp.where(live, lon, -1)
    onehot = (cell[None, :] == jnp.arange(LON, dtype=jnp.int32)[:, None]).astype(BF16)
    shared = jnp.sum((lon[:, None] == cell[None, :]).astype(F32), axis=1)
    share = (1.0 / jnp.maximum(shared, 1.0))[:, None]
    table = fourier_table()
    weight = (jnp.where(jnp.arange(2 * MODES) % MODES == 0, 1.0, 2.0).astype(F32) / LON)[:, None]
    cotangent = loss_sensitivity[0]
    slot_modes = dot(table, onehot).astype(BF16)
    slot_cot = dot_ta(onehot, cotangent).astype(BF16)

    pre1 = dot(rows, w_in)
    hidden = jax.nn.silu(pre1).astype(BF16)
    latent = (dot(hidden, w_out) * share).astype(BF16)
    spectrum = dot(slot_modes, latent)
    sent = spectrum.astype(BF16)
    prev = neighbour(sent, devices, 1).astype(F32)
    following = neighbour(sent, devices, -1).astype(F32)
    mix = (spectrum * w_spec + north * prev + south * following).astype(BF16)
    coeffs = (dot(mix, w_mix) * weight).astype(BF16)
    pre_act = dot_ta(table, coeffs)
    predicted_state = (dot(onehot, latent) + jax.nn.silu(pre_act)).astype(BF16)
    grad_pre = (cotangent.astype(F32) * silu_grad(pre_act)).astype(BF16)
    grad_coeffs = (dot(table, grad_pre) * weight).astype(BF16)
    blend_local = dot_ta(mix, grad_coeffs)
    grad_mix = dot_tb(grad_coeffs, w_mix)
    from_next = neighbour((north * grad_mix).astype(BF16), devices, -1).astype(F32)
    from_prev = neighbour((south * grad_mix).astype(BF16), devices, 1).astype(F32)
    grad_spec = (w_spec * grad_mix + from_next + from_prev).astype(BF16)
    grad_latent = ((slot_cot.astype(F32) + dot_ta(slot_modes, grad_spec)) * share).astype(BF16)
    grad_pre1 = (dot_tb(grad_latent, w_out) * silu_grad(pre1)).astype(BF16)
    row_slope = dot_tb(grad_pre1, w_in).astype(BF16)
    observation_slope = exchange(row_slope, enc_count, blk_count)

    exit_local = dot_ta(hidden, grad_latent)
    entry_local = dot_ta(rows, grad_pre1)
    total = reduce_all(jnp.concatenate([exit_local, blend_local, entry_local], 0), enc_count, blk_count)
    observed_factor = 1.0 / math.sqrt(devices * slots)
    gridding_factor = 1.0 / math.sqrt(devices * LON)
    hid = exit_local.shape[0]
    code = blend_local.shape[0]
    return (
        predicted_state[None],
        total[hid + code :] * observed_factor,
        total[:hid] * observed_factor,
        total[hid : hid + code] * gridding_factor,
        observation_slope,
    )


def solution(mesh):
    placed = (
        P(BOTH, None),
        P(BOTH, None),
        P(BOTH, None),
        P(),
        P(),
        P(),
        P(BOTH, None),
        P(BOTH, None),
        P(),
        P(BOTH, None, None),
    )
    return jax.shard_map(
        shards,
        mesh=mesh,
        in_specs=placed,
        out_specs=(P(BOTH, None, None), P(), P(), P(), P(BOTH, None)),
        check_vma=False,
    )
```

time: 428 us -> 151 us (0.35)
  waiting for transfers between devices: 296 us -> 39.8 us
  starting transfers between devices: 34 us -> 47.6 us
  between operations: 14.3 us -> 1.09 us
  matrix products: 31.5 us -> 19.4 us
  blocking collectives: 30.6 us -> 25.7 us
    psum x1 -> x0, waiting for transfers between devices: 253 us -> none  [shards(): lax.psum((in_local, out_local, mix_local), ('enc', 'blk'))]
    dot_general x14 -> x15, matrix products: 31.5 us -> 19.4 us  [the longest x6 10.9 us: dot(): return jnp.dot(a, b, preferred_element_type=F32)]
    all_to_all x2 -> x3, starting transfers between devices: 22 us -> 32.5 us  [the longest x2 28.3 us: exchange(): out = lax.all_to_all(blocks, BOTH, split_axis=0, concat_axis=0, tiled=True)]
    all_to_all x2 -> x3, waiting for transfers between devices: 30.4 us -> 20 us  [the longest x2 12.6 us: exchange(): out = lax.all_to_all(blocks, BOTH, split_axis=0, concat_axis=0, tiled=True)]
    ppermute x4 -> x9, waiting for transfers between devices: 12.4 us -> 19.8 us  [the longest x3 13.3 us: reduce_all(): lax.ppermute(block, 'blk', [(j, j ^ step) for j in range(blk_count)])]
    all_to_all x2 -> x1, blocking collectives: 30.6 us -> 25.7 us  [reduce_all(): lax.all_to_all(summed.astype(BF16).reshape(enc_count, rows // enc_count,...]
    ppermute x4 -> x9, starting transfers between devices: 12 us -> 15 us  [the longest x4 12.1 us: neighbour(): return lax.ppermute(value, BOTH, pairs)]
  transfers between devices with their start and end apart: 7 -> 12, of which waited for: 6 -> 11; matrix products, arithmetic and copies ran while one was open for 4% -> 10% of each run, Pallas kernels for 0% -> 0%
where the time goes in v1:
time: 151 us; the launch traced here: 150 us
  starting transfers between devices  47.6 us (32%)
  waiting for transfers between devices  39.8 us (26%)
  blocking collectives  25.7 us (17%)
  matrix products  19.4 us (13%)
  other arithmetic  12.1 us (8%)
  local copies, waits for them, and re-layouts  4.6 us (3%)
    all_to_all x2, starting transfers between devices, exchange(): out = lax.all_to_all(blocks, BOTH, split_axis=0, concat_axis=0, tiled=True)  28.3 us
    all_to_all x1, blocking collectives, reduce_all(): lax.all_to_all(summed.astype(BF16).reshape(enc_count, rows // enc_count,...  25.7 us
    ppermute x3, waiting for transfers between devices, reduce_all(): lax.ppermute(block, 'blk', [(j, j ^ step) for j in range(blk_count)])  13.3 us
    all_to_all x2, waiting for transfers between devices, exchange(): out = lax.all_to_all(blocks, BOTH, split_axis=0, concat_axis=0, tiled=True)  12.6 us
    ppermute x4, starting transfers between devices, neighbour(): return lax.ppermute(value, BOTH, pairs)  12.1 us
    dot_general x6, matrix products, dot(): return jnp.dot(a, b, preferred_element_type=F32)  10.9 us
    all_to_all x1, waiting for transfers between devices, reduce_all(): lax.all_to_all(jnp.broadcast_to(block[None], (enc_count,) + block.shape),...  7.4 us
    dot_general x6, matrix products, dot_ta(): lax.dot_general(a, b, (((0,), (0,)), ((), ())), preferred_element_type=F32)  5.52 us
  transfers between devices with their start and end apart: 12, of which 11 were waited for; matrix products, arithmetic and copies ran while one was open for 10% of the time, Pallas kernels for 0%

profile of v1, /device:TPU:1, one launch (start us, length us, event | category | flops | bytes accessed | tf_op | source)
XLA Modules:
  0.0 150.2 jit_solution(13170756189042332446)
XLA Ops:
  0.7 15.7 %all-to-all-start = ((bf16[256,2,128]{2,1,0:T(2,128)(2,1)}), bf16[256,2,128]{2,1,0:T(2,128)(2,1)S(1)}, u32[]{:S(2)}, u32[]{:S(2)}) async-start(bf16[256,2,128]{2,1,0:T(2,128)(2,1)} %bitcast.54), calls=%async_computation | async-start | bytes 262144 | tf_op jit(solution)/shard_map/all_to_all | solution.py:42
  16.3 3.5 %negate_convert_fusion = (bf16[128,1440]{1,0:T(8,128)(2,1)S(1)}, bf16[128,1440]{1,0:T(8,128)(2,1)S(1)}) fusion(), kind=kLoop, calls=%fused_computation.42 | loop fusion | flops 2211840 | bytes 737280 | tf_op jit(solution)/shard_map/convert.2
  21.5 0.9 convert_reduce_fusion
  23.2 6.0 %all-to-all-done = bf16[256,2,128]{2,1,0:T(2,128)(2,1)S(1)} async-done(((bf16[256,2,128]{2,1,0:T(2,128)(2,1)}), bf16[256,2,128]{2,1,0:T(2,128)(2,1)S(1)}, u32[]{:S(2)}, u32[]{:S(2)}) %all-to-all-start) | async-done | bytes 131104 | tf_op jit(solution)/shard_map/all_to_all | solution.py:42
  29.5 1.9 %fusion.17 = bf16[512,512]{1,0:T(8,128)(2,1)S(1)} fusion(bf16[512,512]{1,0:T(8,128)(2,1)} %param.14, f32[512]{0:T(512)S(1)} %maximum_divide_fusion, f32[512,512]{1,0:T(8,128)S(1)} %fusion.37), kind=kOutput, calls=%fused_computation.21 | convolution fusion | flops 270270464 | bytes 2099200 | tf_op jit(solution)/shard_map/dot_general | solution.py:17
  32.3 2.9 %collective-permute-start.1 = (bf16[256,512]{1,0:T(8,128)(2,1)S(1)}, bf16[256,512]{1,0:T(8,128)(2,1)S(1)}, u32[]{:S(2)}, u32[]{:S(2)}) collective-permute-start(bf16[256,512]{1,0:T(8,128)(2,1)S(1)} %get-tuple-element.11), channel_id=1, source_target_pairs={{1,0},{2,1},{3,2},{4,3},{5,4},{6,5},{7,6},{8,7},{9,8},{10,9},{11,1... | collective-permute-start | bytes 786440 | tf_op jit(solution)/shard_map/ppermute | solution.py:48
  35.1 2.8 %collective-permute-start = (bf16[256,512]{1,0:T(8,128)(2,1)S(1)}, bf16[256,512]{1,0:T(8,128)(2,1)S(1)}, u32[]{:S(2)}, u32[]{:S(2)}) collective-permute-start(bf16[256,512]{1,0:T(8,128)(2,1)S(1)} %get-tuple-element.11), channel_id=1, source_target_pairs={{0,1},{1,2},{2,3},{3,4},{4,5},{5,6},{6,7},{7,8},{8,9},{9,10},{10,1... | collective-permute-start | bytes 786440 | tf_op jit(solution)/shard_map/ppermute | solution.py:48
  38.0 2.0 %fusion.14 = f32[512,512]{1,0:T(8,128)} fusion(bf16[1,1440,512]{2,1,0:T(8,128)(2,1)S(1)} %copy-done.20, s32[512]{0:T(512)S(1)} %bitcast.62), kind=kOutput, calls=%fused_computation.20 | convolution fusion | flops 756236288 | bytes 2525184 | tf_op jit(solution)/shard_map/dot_general | solution.py:21
  40.1 1.2 collective-permute-done
  42.1 2.0 %fusion.23 = f32[1440,512]{1,0:T(8,128)S(1)} fusion(bf16[256,512]{1,0:T(8,128)(2,1)} %add_convert_fusion.2, bf16[512,512]{1,0:T(8,128)(2,1)S(1)} %copy-done, f32[256]{0:T(256)S(1)} %fusion.30, bf16[128,1440]{1,0:T(8,128)(2,1)} %copy-done.7, bf16[128,1440]{1,0:T(8,128)(2,1)} %copy-done.8), kind=kOutput, calls=%fused_computation.31 | convolution fusion | flops 513441792 | bytes 4473856 | tf_op jit(solution)/shard_map/dot_general | solution.py:21
  44.2 4.1 %fusion.20 = bf16[256,512]{1,0:T(8,128)(2,1)S(1)} fusion(f32[1440,512]{1,0:T(8,128)S(1)} %fusion.23, bf16[1,1440,512]{2,1,0:T(8,128)(2,1)} %param.19, f32[256]{0:T(256)S(1)} %fusion.30, bf16[128,1440]{1,0:T(8,128)(2,1)} %copy-done.7, bf16[128,1440]{1,0:T(8,128)(2,1)} %copy-done.8), kind=kOutput, calls=%fused_computation.25 | convolution fusion | flops 386596864 | bytes 5424128 | tf_op jit(solution)/shard_map/dot_general | solution.py:17
  48.7 2.1 %collective-permute-start.2 = (bf16[256,512]{1,0:T(8,128)(2,1)S(1)}, bf16[256,512]{1,0:T(8,128)(2,1)S(1)}, u32[]{:S(2)}, u32[]{:S(2)}) collective-permute-start(bf16[256,512]{1,0:T(8,128)(2,1)S(1)} %get-tuple-element.9), channel_id=1, source_target_pairs={{1,0},{2,1},{3,2},{4,3},{5,4},{6,5},{7,6},{8,7},{9,8},{10,9},{11,1... | collective-permute-start | bytes 786440 | tf_op jit(solution)/shard_map/ppermute | solution.py:48
  50.8 4.4 %collective-permute-start.3 = (bf16[256,512]{1,0:T(8,128)(2,1)S(1)}, bf16[256,512]{1,0:T(8,128)(2,1)S(1)}, u32[]{:S(2)}, u32[]{:S(2)}) collective-permute-start(bf16[256,512]{1,0:T(8,128)(2,1)S(1)} %get-tuple-element.10), channel_id=1, source_target_pairs={{0,1},{1,2},{2,3},{3,4},{4,5},{5,6},{6,7},{7,8},{8,9},{9,10},{10,1... | collective-permute-start | bytes 786440 | tf_op jit(solution)/shard_map/ppermute | solution.py:48
  55.5 1.8 %collective-permute-done.2 = bf16[256,512]{1,0:T(8,128)(2,1)S(1)} collective-permute-done((bf16[256,512]{1,0:T(8,128)(2,1)S(1)}, bf16[256,512]{1,0:T(8,128)(2,1)S(1)}, u32[]{:S(2)}, u32[]{:S(2)}) %collective-permute-start.2) | collective-permute-done | bytes 262176 | tf_op jit(solution)/shard_map/ppermute | solution.py:48
  57.3 1.2 collective-permute-done.3
  61.1 0.9 dynamic-slice_convert_fusion
  62.0 2.2 %collective-permute-done.4 = bf16[1152,256]{1,0:T(8,128)(2,1)S(1)} collective-permute-done((bf16[1152,256]{1,0:T(8,128)(2,1)}, bf16[1152,256]{1,0:T(8,128)(2,1)S(1)}, u32[]{:S(2)}, u32[]{:S(2)}) %collective-permute-start.4) | collective-permute-done | bytes 589856 | tf_op jit(solution)/shard_map/ppermute | solution.py:58
  64.5 25.7 %all_to_all.20 = bf16[16,72,256]{2,1,0:T(8,128)(2,1)} all-to-all(bf16[16,72,256]{2,1,0:T(8,128)(2,1)S(1)} %bitcast.50), channel_id=1, replica_groups=mesh['enc'=16,'blk'=16] {'enc'}, dimensions={0} | all-to-all | bytes 1179648 | tf_op jit(solution)/shard_map/all_to_all | solution.py:59
  90.2 1.2 reduce_sum.22
  91.4 2.8 %collective-permute-done.5 = bf16[72,256]{1,0:T(8,128)(2,1)S(1)} collective-permute-done((bf16[72,256]{1,0:T(8,128)(2,1)S(1)}, bf16[72,256]{1,0:T(8,128)(2,1)S(1)}, u32[]{:S(2)}, u32[]{:S(2)}) %collective-permute-start.5) | collective-permute-done | bytes 36896 | tf_op jit(solution)/shard_map/ppermute | solution.py:65
  94.3 3.8 %collective-permute-done.6 = bf16[72,256]{1,0:T(8,128)(2,1)S(1)} collective-permute-done((bf16[72,256]{1,0:T(8,128)(2,1)S(1)}, bf16[72,256]{1,0:T(8,128)(2,1)S(1)}, u32[]{:S(2)}, u32[]{:S(2)}) %collective-permute-start.6) | collective-permute-done | bytes 36896 | tf_op jit(solution)/shard_map/ppermute | solution.py:65
  98.4 6.7 %collective-permute-done.7 = bf16[72,256]{1,0:T(8,128)(2,1)S(1)} collective-permute-done((bf16[72,256]{1,0:T(8,128)(2,1)S(1)}, bf16[72,256]{1,0:T(8,128)(2,1)S(1)}, u32[]{:S(2)}, u32[]{:S(2)}) %collective-permute-start.7) | collective-permute-done | bytes 36896 | tf_op jit(solution)/shard_map/ppermute | solution.py:65
  106.0 4.3 %all-to-all-start.2 = ((bf16[16,72,256]{2,1,0:T(8,128)(2,1)}), bf16[16,72,256]{2,1,0:T(8,128)(2,1)}, u32[]{:S(2)}, u32[]{:S(2)}) async-start(bf16[16,72,256]{2,1,0:T(8,128)(2,1)} %broadcast_in_dim.33), calls=%async_computation.2 | async-start | bytes 1179648 | tf_op jit(solution)/shard_map/all_to_all | solution.py:68
  110.3 2.0 %convolution_convert_fusion = bf16[512,128]{1,0:T(8,128)(2,1)} fusion(bf16[512,512]{1,0:T(8,128)(2,1)} %copy-done.4, bf16[128,512]{1,0:T(8,128)(2,1)} %param.13), kind=kOutput, calls=%fused_computation.33 | convolution fusion | flops 67174400 | bytes 786432 | tf_op jit(solution)/shard_map/dot_general | solution.py:25
  112.3 7.4 %all-to-all-done.2 = bf16[16,72,256]{2,1,0:T(8,128)(2,1)} async-done(((bf16[16,72,256]{2,1,0:T(8,128)(2,1)}), bf16[16,72,256]{2,1,0:T(8,128)(2,1)}, u32[]{:S(2)}, u32[]{:S(2)}) %all-to-all-start.2) | async-done | bytes 589856 | tf_op jit(solution)/shard_map/all_to_all | solution.py:68
  119.7 12.6 %all-to-all-start.3 = ((bf16[256,2,128]{2,1,0:T(2,128)(2,1)}), bf16[256,2,128]{2,1,0:T(2,128)(2,1)}, u32[]{:S(2)}, u32[]{:S(2)}) async-start(bf16[256,2,128]{2,1,0:T(2,128)(2,1)} %bitcast.53), calls=%async_computation.3 | async-start | bytes 262144 | tf_op jit(solution)/shard_map/all_to_all | solution.py:42
  132.3 2.4 %collective-permute-start.8 = (bf16[1152,256]{1,0:T(8,128)(2,1)}, bf16[1152,256]{1,0:T(8,128)(2,1)}, u32[]{:S(2)}, u32[]{:S(2)}) collective-permute-start(bf16[1152,256]{1,0:T(8,128)(2,1)} %bitcast.11), channel_id=1, source_target_pairs={{0,1},{1,0},{2,3},{3,2},{4,5},{5,4},{6,7},{7,6},{8,9},{9,8},{10,11... | collective-permute-start | bytes 1769480 | tf_op jit(solution)/shard_map/ppermute | solution.py:71
  134.8 3.5 %fusion.3 = bf16[1,1440,512]{2,1,0:T(8,128)(2,1)} fusion(f32[1440,512]{1,0:T(8,128)S(1)} %copy-done.2, bf16[512,512]{1,0:T(8,128)(2,1)} %copy-done.16, s32[512]{0:T(512)S(1)} %bitcast.63), kind=kOutput, calls=%fused_computation.7 | convolution fusion | flops 760135680 | bytes 4950016 | tf_op jit(solution)/shard_map/dot_general | solution.py:17
  138.3 6.7 %all-to-all-done.3 = bf16[256,2,128]{2,1,0:T(2,128)(2,1)} async-done(((bf16[256,2,128]{2,1,0:T(2,128)(2,1)}), bf16[256,2,128]{2,1,0:T(2,128)(2,1)}, u32[]{:S(2)}, u32[]{:S(2)}) %all-to-all-start.3) | async-done | bytes 131104 | tf_op jit(solution)/shard_map/all_to_all | solution.py:42
  144.9 1.3 broadcast_select_fusion.1
  147.0 1.6 %convert_multiply_fusion.1 = (f32[512,512]{1,0:T(8,128)}, f32[512,512]{1,0:T(8,128)}) fusion(bf16[1152,256]{1,0:T(8,128)(2,1)S(1)} %get-tuple-element.8, bf16[1152,256]{1,0:T(8,128)(2,1)S(1)} %get-tuple-element.7), kind=kLoop, calls=%fused_computation.35 | loop fusion | flops 2621440 | bytes 3276800 | tf_op jit(solution)/shard_map/mul | solution.py:132
  148.6 1.6 %copy.16 = bf16[512,128]{1,0:T(8,128)(2,1)} copy(bf16[512,128]{1,0:T(8,128)(2,1)} %bitcast.13) | data formatting | bytes 262144
  (72 shorter events, 10.1 us)
Async XLA Ops:
  0.6 41.5 %copy-start = (bf16[512,512]{1,0:T(8,128)(2,1)S(1)}, bf16[512,512]{1,0:T(8,128)(2,1)}, u32[]{:S(2)}) copy-start(bf16[512,512]{1,0:T(8,128)(2,1)} %param.18) | copy-start | bytes 1572868
  0.6 28.6 %copy-start.17 = (bf16[128,512]{1,0:T(8,128)(2,1)S(1)}, bf16[128,512]{1,0:T(8,128)(2,1)}, u32[]{:S(2)}) copy-start(bf16[128,512]{1,0:T(8,128)(2,1)} %param.13) | copy-start | bytes 393220
  0.7 28.5 %all-to-all-start = ((bf16[256,2,128]{2,1,0:T(2,128)(2,1)}), bf16[256,2,128]{2,1,0:T(2,128)(2,1)S(1)}, u32[]{:S(2)}, u32[]{:S(2)}) async-start(bf16[256,2,128]{2,1,0:T(2,128)(2,1)} %bitcast.54), calls=%async_computation | async-start | bytes 262144 | tf_op jit(solution)/shard_map/all_to_all | solution.py:42
  19.8 11.6 %copy-start.7 = (bf16[128,1440]{1,0:T(8,128)(2,1)}, bf16[128,1440]{1,0:T(8,128)(2,1)S(1)}, u32[]{:S(2)}) copy-start(bf16[128,1440]{1,0:T(8,128)(2,1)S(1)} %get-tuple-element.14) | copy-start | bytes 1105924
  19.8 11.6 %copy-start.8 = (bf16[128,1440]{1,0:T(8,128)(2,1)}, bf16[128,1440]{1,0:T(8,128)(2,1)S(1)}, u32[]{:S(2)}) copy-start(bf16[128,1440]{1,0:T(8,128)(2,1)S(1)} %get-tuple-element.15) | copy-start | bytes 1105924
  23.2 8.2 %copy-start.14 = (bf16[256,512]{1,0:T(8,128)(2,1)}, bf16[256,512]{1,0:T(8,128)(2,1)S(1)}, u32[]{:S(2)}) copy-start(bf16[256,512]{1,0:T(8,128)(2,1)S(1)} %fusion.22) | copy-start | bytes 786436
  29.2 2.2 %copy-start.9 = (bf16[256,2,128]{2,1,0:T(2,128)(2,1)}, bf16[256,2,128]{2,1,0:T(2,128)(2,1)S(1)}, u32[]{:S(2)}) copy-start(bf16[256,2,128]{2,1,0:T(2,128)(2,1)S(1)} %all-to-all-done) | copy-start | bytes 393220
  29.5 2.0 %copy-start.12 = (f32[512,512]{1,0:T(8,128)}, f32[512,512]{1,0:T(8,128)S(1)}, u32[]{:S(2)}) copy-start(f32[512,512]{1,0:T(8,128)S(1)} %fusion.37) | copy-start | bytes 3145732
  29.5 8.5 %copy-start.20 = (bf16[1,1440,512]{2,1,0:T(8,128)(2,1)S(1)}, bf16[1,1440,512]{2,1,0:T(8,128)(2,1)}, u32[]{:S(2)}) copy-start(bf16[1,1440,512]{2,1,0:T(8,128)(2,1)} %param.19) | copy-start | bytes 4423684
  32.3 9.0 %copy-start.5 = (f32[256,512]{1,0:T(8,128)S(1)}, f32[256,512]{1,0:T(8,128)}, u32[]{:S(2)}) copy-start(f32[256,512]{1,0:T(8,128)} %param.15) | copy-start | bytes 1572868
  32.3 9.0 %copy-start.18 = (f32[1,512]{1,0:T(1,128)S(1)}, f32[1,512]{1,0:T(1,128)}, u32[]{:S(2)}) copy-start(f32[1,512]{1,0:T(1,128)} %param.17) | copy-start | bytes 6148
  32.3 9.0 %copy-start.19 = (f32[1,512]{1,0:T(1,128)S(1)}, f32[1,512]{1,0:T(1,128)}, u32[]{:S(2)}) copy-start(f32[1,512]{1,0:T(1,128)} %param.16) | copy-start | bytes 6148
  32.3 7.8 %collective-permute-start.1 = (bf16[256,512]{1,0:T(8,128)(2,1)S(1)}, bf16[256,512]{1,0:T(8,128)(2,1)S(1)}, u32[]{:S(2)}, u32[]{:S(2)}) collective-permute-start(bf16[256,512]{1,0:T(8,128)(2,1)S(1)} %get-tuple-element.11), channel_id=1, source_target_pairs={{1,0},{2,1},{3,2},{4,3},{5,4},{6,5},{7,6},{8,7},{9,8},{10,9},{11,1... | collective-permute-start | bytes 786440 | tf_op jit(solution)/shard_map/ppermute | solution.py:48
  35.1 6.1 %collective-permute-start = (bf16[256,512]{1,0:T(8,128)(2,1)S(1)}, bf16[256,512]{1,0:T(8,128)(2,1)S(1)}, u32[]{:S(2)}, u32[]{:S(2)}) collective-permute-start(bf16[256,512]{1,0:T(8,128)(2,1)S(1)} %get-tuple-element.11), channel_id=1, source_target_pairs={{0,1},{1,2},{2,3},{3,4},{4,5},{5,6},{6,7},{7,8},{8,9},{9,10},{10,1... | collective-permute-start | bytes 786440 | tf_op jit(solution)/shard_map/ppermute | solution.py:48
  44.2 4.1 %copy-start.1 = (f32[1440,512]{1,0:T(8,128)}, f32[1440,512]{1,0:T(8,128)S(1)}, u32[]{:S(2)}) copy-start(f32[1440,512]{1,0:T(8,128)S(1)} %fusion.23) | copy-start | bytes 8847364
  44.2 11.0 %copy-start.3 = (bf16[256,512]{1,0:T(8,128)(2,1)S(1)}, bf16[256,512]{1,0:T(8,128)(2,1)}, u32[]{:S(2)}) copy-start(bf16[256,512]{1,0:T(8,128)(2,1)} %add_convert_fusion.2) | copy-start | bytes 786436
  48.3 10.2 %copy-start.6 = (f32[256,512]{1,0:T(8,128)S(1)}, f32[256,512]{1,0:T(8,128)}, u32[]{:S(2)}) copy-start(f32[256,512]{1,0:T(8,128)} %param.15) | copy-start | bytes 1572868
  48.3 10.1 %copy-start.11 = (f32[512,512]{1,0:T(8,128)S(1)}, f32[512,512]{1,0:T(8,128)}, u32[]{:S(2)}) copy-start(f32[512,512]{1,0:T(8,128)} %fusion.14) | copy-start | bytes 3145732
  48.3 10.1 %copy-start.15 = (bf16[256,512]{1,0:T(8,128)(2,1)S(1)}, bf16[256,512]{1,0:T(8,128)(2,1)}, u32[]{:S(2)}) copy-start(bf16[256,512]{1,0:T(8,128)(2,1)} %copy-done.14) | copy-start | bytes 786436
  48.7 10.2 %copy-start.13 = (f32[512,512]{1,0:T(8,128)S(1)}, f32[512,512]{1,0:T(8,128)}, u32[]{:S(2)}) copy-start(f32[512,512]{1,0:T(8,128)} %copy-done.12) | copy-start | bytes 3145732
  48.7 10.2 %copy-start.21 = (bf16[512,512]{1,0:T(8,128)(2,1)S(1)}, bf16[512,512]{1,0:T(8,128)(2,1)}, u32[]{:S(2)}) copy-start(bf16[512,512]{1,0:T(8,128)(2,1)} %param.14) | copy-start | bytes 1572868
  48.7 8.6 %collective-permute-start.2 = (bf16[256,512]{1,0:T(8,128)(2,1)S(1)}, bf16[256,512]{1,0:T(8,128)(2,1)S(1)}, u32[]{:S(2)}, u32[]{:S(2)}) collective-permute-start(bf16[256,512]{1,0:T(8,128)(2,1)S(1)} %get-tuple-element.9), channel_id=1, source_target_pairs={{1,0},{2,1},{3,2},{4,3},{5,4},{6,5},{7,6},{8,7},{9,8},{10,9},{11,1... | collective-permute-start | bytes 786440 | tf_op jit(solution)/shard_map/ppermute | solution.py:48
  50.8 7.7 %collective-permute-start.3 = (bf16[256,512]{1,0:T(8,128)(2,1)S(1)}, bf16[256,512]{1,0:T(8,128)(2,1)S(1)}, u32[]{:S(2)}, u32[]{:S(2)}) collective-permute-start(bf16[256,512]{1,0:T(8,128)(2,1)S(1)} %get-tuple-element.10), channel_id=1, source_target_pairs={{0,1},{1,2},{2,3},{3,4},{4,5},{5,6},{6,7},{7,8},{8,9},{9,10},{10,1... | collective-permute-start | bytes 786440 | tf_op jit(solution)/shard_map/ppermute | solution.py:48
  59.6 1.0 copy-start.10
  62.0 2.2 %collective-permute-start.4 = (bf16[1152,256]{1,0:T(8,128)(2,1)}, bf16[1152,256]{1,0:T(8,128)(2,1)S(1)}, u32[]{:S(2)}, u32[]{:S(2)}) collective-permute-start(bf16[1152,256]{1,0:T(8,128)(2,1)} %dynamic-slice_convert_fusion), channel_id=1, source_target_pairs={{0,1},{1,0},{2,3},{3,2},{4,5},{5,4},{6,7},{7,6},{8,9},{9,8},{10,11... | collective-permute-start | bytes 1769480 | tf_op jit(solution)/shard_map/ppermute | solution.py:58
  64.4 70.3 %copy-start.2 = (f32[1440,512]{1,0:T(8,128)S(1)}, f32[1440,512]{1,0:T(8,128)}, u32[]{:S(2)}) copy-start(f32[1440,512]{1,0:T(8,128)} %copy-done.1) | copy-start | bytes 8847364
  91.3 2.9 %collective-permute-start.5 = (bf16[72,256]{1,0:T(8,128)(2,1)S(1)}, bf16[72,256]{1,0:T(8,128)(2,1)S(1)}, u32[]{:S(2)}, u32[]{:S(2)}) collective-permute-start(bf16[72,256]{1,0:T(8,128)(2,1)S(1)} %reduce_sum.22), channel_id=1, source_target_pairs={{0,2},{1,3},{2,0},{3,1},{4,6},{5,7},{6,4},{7,5},{8,10},{9,11},{10,... | collective-permute-start | bytes 110600 | tf_op jit(solution)/shard_map/ppermute | solution.py:65
  94.2 3.9 %collective-permute-start.6 = (bf16[72,256]{1,0:T(8,128)(2,1)S(1)}, bf16[72,256]{1,0:T(8,128)(2,1)S(1)}, u32[]{:S(2)}, u32[]{:S(2)}) collective-permute-start(bf16[72,256]{1,0:T(8,128)(2,1)S(1)} %add_convert_fusion.6), channel_id=1, source_target_pairs={{0,4},{1,5},{2,6},{3,7},{4,0},{5,1},{6,2},{7,3},{8,12},{9,13},{10,... | collective-permute-start | bytes 110600 | tf_op jit(solution)/shard_map/ppermute | solution.py:65
  98.1 7.0 %collective-permute-start.7 = (bf16[72,256]{1,0:T(8,128)(2,1)S(1)}, bf16[72,256]{1,0:T(8,128)(2,1)S(1)}, u32[]{:S(2)}, u32[]{:S(2)}) collective-permute-start(bf16[72,256]{1,0:T(8,128)(2,1)S(1)} %add_convert_fusion.5), channel_id=1, source_target_pairs={{0,8},{1,9},{2,10},{3,11},{4,12},{5,13},{6,14},{7,15},{8,0},{9,1},... | collective-permute-start | bytes 110600 | tf_op jit(solution)/shard_map/ppermute | solution.py:65
  106.0 13.7 %all-to-all-start.2 = ((bf16[16,72,256]{2,1,0:T(8,128)(2,1)}), bf16[16,72,256]{2,1,0:T(8,128)(2,1)}, u32[]{:S(2)}, u32[]{:S(2)}) async-start(bf16[16,72,256]{2,1,0:T(8,128)(2,1)} %broadcast_in_dim.33), calls=%async_computation.2 | async-start | bytes 1179648 | tf_op jit(solution)/shard_map/all_to_all | solution.py:68
  119.7 25.3 %all-to-all-start.3 = ((bf16[256,2,128]{2,1,0:T(2,128)(2,1)}), bf16[256,2,128]{2,1,0:T(2,128)(2,1)}, u32[]{:S(2)}, u32[]{:S(2)}) async-start(bf16[256,2,128]{2,1,0:T(2,128)(2,1)} %bitcast.53), calls=%async_computation.3 | async-start | bytes 262144 | tf_op jit(solution)/shard_map/all_to_all | solution.py:42
  132.3 12.6 %collective-permute-start.8 = (bf16[1152,256]{1,0:T(8,128)(2,1)}, bf16[1152,256]{1,0:T(8,128)(2,1)}, u32[]{:S(2)}, u32[]{:S(2)}) collective-permute-start(bf16[1152,256]{1,0:T(8,128)(2,1)} %bitcast.11), channel_id=1, source_target_pairs={{0,1},{1,0},{2,3},{3,2},{4,5},{5,4},{6,7},{7,6},{8,9},{9,8},{10,11... | collective-permute-start | bytes 1769480 | tf_op jit(solution)/shard_map/ppermute | solution.py:71
  (2 other events, 1.6 us)

commit v2 on v1

v2 whole, which is shorter than its diff:
```python
import math

import jax
import jax.numpy as jnp
import numpy as np
from jax import lax
from jax.experimental import pallas as pl
from jax.experimental.pallas import tpu as pltpu
from jax.sharding import PartitionSpec as P

LON = 1440
MODES = 128
CAP = 2
LANES = 128
BOTH = ("enc", "blk")
BF16 = jnp.bfloat16
F32 = jnp.float32
TILES = ((0, 384), (384, 384), (768, 384), (1152, 288))


def dot(a, b):
    return jnp.dot(a, b, preferred_element_type=F32)


def dot_ta(a, b):
    return lax.dot_general(a, b, (((0,), (0,)), ((), ())), preferred_element_type=F32)


def dot_tb(a, b):
    return lax.dot_general(a, b, (((1,), (1,)), ((), ())), preferred_element_type=F32)


def logistic(values):
    return 0.5 * jnp.tanh(0.5 * values) + 0.5


def local_kernel(body, out_shape, flops, moved, *operands, smem=(), room=6):
    vmem = pl.BlockSpec(memory_space=pltpu.VMEM)
    in_specs = [pl.BlockSpec(memory_space=pltpu.SMEM) if i in smem else vmem for i in range(len(operands))]
    single = not isinstance(out_shape, (tuple, list))
    return pl.pallas_call(
        body,
        out_shape=out_shape,
        in_specs=in_specs,
        out_specs=vmem if single else [vmem] * len(out_shape),
        compiler_params=pltpu.CompilerParams(vmem_limit_bytes=room * 1024 * 1024),
        cost_estimate=pl.CostEstimate(flops=flops, bytes_accessed=moved, transcendentals=0),
    )(*operands)


def shape(dims, dtype):
    return jax.ShapeDtypeStruct(dims, dtype)


def mix_body(
    spectrum, prev, following, w_spec, north, south, w_mix, weight, table_t, table, onehot, latent, cotangent,
    state, mix_out, coeffs_out, own, to_prev, to_next,
):
    north_row, south_row = north[...], south[...]
    scale = weight[...]
    mix = (
        spectrum[...] * w_spec[...] + north_row * prev[...].astype(F32) + south_row * following[...].astype(F32)
    ).astype(BF16)
    mix_out[...] = mix
    coeffs = (dot(mix, w_mix[...]) * scale).astype(BF16)
    total = jnp.zeros(spectrum.shape, F32)
    for low, size in TILES:
        part = pl.ds(low, size)
        pre_act = dot(table_t[part, :], coeffs)
        gate = logistic(pre_act)
        silu = pre_act * gate
        state[part, :] = (dot(onehot[part, :], latent[...]) + silu).astype(BF16)
        grad_pre = (cotangent[part, :].astype(F32) * (gate + silu * (1.0 - gate))).astype(BF16)
        total += dot(table[:, part], grad_pre)
    grad_coeffs = (total * scale).astype(BF16)
    coeffs_out[...] = grad_coeffs
    grad_mix = dot_tb(grad_coeffs, w_mix[...])
    own[...] = w_spec[...] * grad_mix
    to_prev[...] = (north_row * grad_mix).astype(BF16)
    to_next[...] = (south_row * grad_mix).astype(BF16)


def back_body(
    core, own, from_next, from_prev, slot_cot, slot_modes, share, w_out, pre1, hidden, rows, w_in, order, mix, coeffs,
    sent, mine, kept,
):
    first = core[0] == 0
    grad_spec = (own[...] + from_next[...].astype(F32) + from_prev[...].astype(F32)).astype(BF16)
    grad_latent = ((slot_cot[...].astype(F32) + dot_ta(slot_modes[...], grad_spec)) * share[...]).astype(BF16)
    gate = logistic(pre1[...])
    slope = gate * (1.0 + pre1[...] * (1.0 - gate))
    grad_pre1 = (dot_tb(grad_latent, w_out[...]) * slope).astype(BF16)
    row_slope = dot_tb(grad_pre1, w_in[...]).astype(BF16)
    ordered = dot(order[...], row_slope).astype(BF16)
    half = ordered.shape[0] // 2
    kept[...] = ordered[:half]
    sent[mine.shape[0] :, :] = ordered[half:]
    at = 0
    depth = mine.shape[0] // 2
    for left, right in ((hidden[...], grad_latent), (mix[...], coeffs[...]), (rows[...], grad_pre1)):
        width = right.shape[1] // 2
        low, high = right[:, :width], right[:, width:]
        near = dot_ta(left, jnp.where(first, low, high))
        far = dot_ta(left, jnp.where(first, high, low)).astype(BF16)
        size = near.shape[0]
        for piece in range(2):
            lanes = slice(piece * LANES, (piece + 1) * LANES)
            mine[piece * depth + at : piece * depth + at + size, :] = near[:, lanes]
            sent[piece * depth + at : piece * depth + at + size, :] = far[:, lanes]
        at += size


def scatter_body(mine, kept, got, out):
    count = out.shape[0]
    size = mine.shape[0] // count
    few = kept.shape[0] // count
    for i in range(count):
        out[i, :few, :] = kept[i * few : (i + 1) * few, :]
        out[i, few : 2 * few, :] = got[mine.shape[0] + i * few : mine.shape[0] + (i + 1) * few, :]
        part = slice(i * size, (i + 1) * size)
        out[i, 2 * few :, :] = (mine[part, :] + got[part, :].astype(F32)).astype(BF16)


def relay_body(got, order, out):
    sources = got.shape[0]
    count = out.shape[0]
    few = order.shape[0] // sources
    more = order.shape[0] // count
    total = got[0, few:, :].astype(F32)
    for i in range(1, sources):
        total += got[i, few:, :].astype(F32)
    total = total.astype(BF16)
    ordered = dot(order[...], jnp.concatenate([got[i, :few, :] for i in range(sources)], 0)).astype(BF16)
    for i in range(count):
        out[i, :more, :] = ordered[i * more : (i + 1) * more, :]
        out[i, more:, :] = total


def gather_body(got, order, out, slope):
    sources = got.shape[0]
    few = order.shape[0] // sources
    total = got[0, few:, :].astype(F32)
    for i in range(1, sources):
        total += got[i, few:, :].astype(F32)
    total = total.astype(BF16)
    for i in range(out.shape[0]):
        out[i, :, :] = total
    ordered = dot(order[...], jnp.concatenate([got[i, :few, :] for i in range(sources)], 0))
    slope[...] = ordered.astype(BF16)


def final_body(factors, core, whole, theirs, entry, exit_, blend):
    first = core[0] == 0
    depth = whole.shape[0] // 2
    for piece in range(2):
        at = piece * depth
        for out, factor in ((exit_, factors[0]), (blend, factors[1]), (entry, factors[0])):
            size = out.shape[0]
            ours = whole[at : at + size, :].astype(F32) * factor
            other = theirs[at : at + size, :].astype(F32) * factor
            out[:, piece * LANES : (piece + 1) * LANES] = jnp.where(first, ours, other)
            out[:, (2 + piece) * LANES : (3 + piece) * LANES] = jnp.where(first, other, ours)
            at += size


def phase_tables():
    product = np.arange(MODES)[:, None] * np.arange(LON)[None, :] % LON
    phases = product.astype(np.float64) * (2.0 * math.pi / LON)
    table = np.concatenate([np.cos(phases), -np.sin(phases)], 0)
    return jnp.asarray(table, BF16), jnp.asarray(np.ascontiguousarray(table.T), BF16)


def selection(source):
    return (source[:, None] == jnp.arange(source.shape[0], dtype=jnp.int32)[None, :]).astype(BF16)


def neighbour(value, count, step):
    pairs = [(i, i + step) for i in range(count) if 0 <= i + step < count]
    return lax.ppermute(value, BOTH, pairs)


def all_swap(blocks, axis, groups=None):
    return lax.all_to_all(blocks, axis, split_axis=0, concat_axis=0, tiled=True, axis_index_groups=groups)


def shards(
    observations, lon_index, live_count, w_in, w_out, w_spec, north, south, w_mix, loss_sensitivity
):
    encs = lax.axis_size("enc")
    blks = lax.axis_size("blk")
    deep = blks // 2
    devices = encs * blks
    slots, channels = observations.shape
    hid, code = w_out.shape
    core = lax.axis_index("blk") % 2
    core_arg = core.astype(jnp.int32).reshape(1)
    swap = [(j, j ^ 1) for j in range(blks)]
    columns = [[2 * i + k for i in range(deep)] for k in range(2)]

    rows = all_swap(observations.reshape(devices, CAP, channels), BOTH).reshape(slots, channels)

    lon = lon_index[0]
    live = (jnp.arange(CAP, dtype=jnp.int32)[None, :] < live_count[0][:, None]).reshape(-1)
    cell = jnp.where(live, lon, -1)
    onehot = (cell[None, :] == jnp.arange(LON, dtype=jnp.int32)[:, None]).astype(BF16)
    shared = jnp.sum((lon[:, None] == cell[None, :]).astype(F32), axis=1)
    share = (1.0 / jnp.maximum(shared, 1.0))[:, None]
    table, table_t = phase_tables()
    weight = jnp.asarray(np.where(np.arange(2 * MODES) % MODES == 0, 1.0, 2.0)[:, None] / LON, F32)
    cotangent = loss_sensitivity[0]
    slot_modes = dot(table, onehot).astype(BF16)
    slot_cot = dot_ta(onehot, cotangent).astype(BF16)
    at = jnp.arange(slots, dtype=jnp.int32)
    slot = at % CAP
    half = slots // 2
    enc_at, z_at = at % half // (deep * CAP), at // CAP % deep
    order1 = selection(((enc_at * deep + z_at) * 2 + (at // half + core) % 2) * CAP + slot)
    z_at, enc_core = at // (encs * 2 * CAP), at // CAP % (encs * 2)
    order2 = selection((enc_core * deep + z_at) * CAP + slot)
    enc_at, z_at, core_at = at // (deep * 2 * CAP), at // (2 * CAP) % deep, at // CAP % 2
    order3 = selection(((z_at * encs + enc_at) * 2 + (core_at + core) % 2) * CAP + slot)

    pre1 = dot(rows, w_in)
    hidden = (pre1 * logistic(pre1)).astype(BF16)
    latent = (dot(hidden, w_out) * share).astype(BF16)
    spectrum = dot(slot_modes, latent)
    outgoing = spectrum.astype(BF16)
    prev = neighbour(outgoing, devices, 1)
    following = neighbour(outgoing, devices, -1)

    modes = (2 * MODES, code)
    state, mix, coeffs, own, to_prev, to_next = local_kernel(
        mix_body,
        [
            shape((LON, code), BF16), shape(modes, BF16), shape(modes, BF16),
            shape(modes, F32), shape(modes, BF16), shape(modes, BF16),
        ],
        2 * LON * code * (4 * MODES + slots),
        8 * LON * code,
        spectrum, prev, following, w_spec, north, south, w_mix, weight, table_t, table, onehot, latent, cotangent,
        room=12,
    )
    from_next = neighbour(to_prev, devices, -1)
    from_prev = neighbour(to_next, devices, 1)
    depth = hid + code + channels
    sent, mine, kept = local_kernel(
        back_body,
        [shape((2 * depth + half, LANES), BF16), shape((2 * depth, LANES), F32), shape((half, LANES), BF16)],
        2 * slots * code * 1500,
        6 * slots * code,
        core_arg, own, from_next, from_prev, slot_cot, slot_modes, share, w_out, pre1, hidden, rows, w_in, order1, mix, coeffs,
        smem=(0,),
        room=10,
    )
    got = lax.ppermute(sent, "blk", swap)
    chunk = 2 * depth // encs
    few, more = slots // encs, slots // deep
    parts = local_kernel(
        scatter_body, shape((encs, few + chunk, LANES), BF16), depth * LANES, 16 * depth * LANES, mine, kept, got
    )
    parts = all_swap(parts, "enc")
    parts = local_kernel(
        relay_body, shape((deep, more + chunk, LANES), BF16), 10 * depth * LANES, 8 * depth * LANES, parts, order2
    )
    parts = all_swap(parts, "blk", columns)
    spread, observation_slope = local_kernel(
        gather_body,
        [shape((encs, chunk, LANES), BF16), shape((slots, LANES), BF16)],
        10 * depth * LANES,
        8 * depth * LANES,
        parts, order3,
    )
    whole = all_swap(spread, "enc").reshape(2 * depth, LANES)
    theirs = lax.ppermute(whole, "blk", swap)
    factors = jnp.array([1.0 / math.sqrt(devices * slots), 1.0 / math.sqrt(devices * LON)], F32)
    entry, exit_, blend = local_kernel(
        final_body,
        [shape((channels, hid), F32), shape((hid, code), F32), shape((code, code), F32)],
        4 * depth * code,
        6 * depth * code,
        factors, core_arg, whole, theirs,
        smem=(0, 1),
    )
    return state[None], entry, exit_, blend, observation_slope


def solution(mesh):
    placed = (
        P(BOTH, None),
        P(BOTH, None),
        P(BOTH, None),
        P(),
        P(),
        P(),
        P(BOTH, None),
        P(BOTH, None),
        P(),
        P(BOTH, None, None),
    )
    return jax.shard_map(
        shards,
        mesh=mesh,
        in_specs=placed,
        out_specs=(P(BOTH, None, None), P(), P(), P(), P(BOTH, None)),
        check_vma=False,
    )
```

time: 151 us -> 139 us (0.921)
  matrix products: 19.4 us -> 4.57 us
  Pallas kernels: 0 us -> 10.6 us
  blocking collectives: 25.7 us -> 16.3 us
  other arithmetic: 12.1 us -> 2.87 us
  waiting for transfers between devices: 39.8 us -> 44.4 us
  local copies, waits for them, and re-layouts: 4.6 us -> 8.49 us
  starting transfers between devices: 47.6 us -> 49.6 us
    all_to_all x3, waiting for transfers between devices: 20 us -> 33.5 us  [all_swap(): lax.all_to_all(blocks, axis, split_axis=0, concat_axis=0, tiled=True, axi...]
    ppermute x5 -> x2, waiting for transfers between devices: 15.5 us -> 3.71 us  [the longest x1 2.08 us: shards(): got = lax.ppermute(sent, 'blk', swap)]
    pallas_call x0 -> x6, Pallas kernels: none -> 10.6 us  [local_kernel(): pl.pallas_call(body, out_shape=out_shape, in_specs=in_specs, out_specs=vm...]
    all_to_all x1, blocking collectives: 25.7 us -> 16.3 us  [all_swap(): lax.all_to_all(blocks, axis, split_axis=0, concat_axis=0, tiled=True, axi...]
    dot_general x6 -> x4, matrix products: 10.9 us -> 2.74 us  [dot(): return jnp.dot(a, b, preferred_element_type=F32)]
    unnamed x45 -> x42, local copies, waits for them, and re-layouts: 2.69 us -> 8.19 us
    dot_general x6 -> x1, matrix products: 5.52 us -> 1.83 us  [dot_ta(): lax.dot_general(a, b, (((0,), (0,)), ((), ())), preferred_element_type=F32)]
    another operation x1 -> x0, other arithmetic: 3.46 us -> none
  transfers between devices with their start and end apart: 12 -> 9, of which waited for: 11 -> 8; matrix products, arithmetic and copies ran while one was open for 10% -> 4% of each run, Pallas kernels for 0% -> 0%
where the time goes in v2:
time: 139 us; the launch traced here: 138 us
  starting transfers between devices  49.6 us (36%)
  waiting for transfers between devices  44.4 us (32%)
  blocking collectives  16.3 us (12%)
  Pallas kernels  10.6 us (8%)
  local copies, waits for them, and re-layouts  8.49 us (6%)
  matrix products  4.57 us (3%)
  other arithmetic  2.87 us (2%)
    all_to_all x3, starting transfers between devices, all_swap(): lax.all_to_all(blocks, axis, split_axis=0, concat_axis=0, tiled=True, axi...  35.3 us
    all_to_all x3, waiting for transfers between devices, all_swap(): lax.all_to_all(blocks, axis, split_axis=0, concat_axis=0, tiled=True, axi...  33.5 us
    all_to_all x1, blocking collectives, all_swap(): lax.all_to_all(blocks, axis, split_axis=0, concat_axis=0, tiled=True, axi...  16.3 us
    ppermute x4, starting transfers between devices, neighbour(): return lax.ppermute(value, BOTH, pairs)  11.1 us
    pallas_call x6, Pallas kernels, local_kernel(): pl.pallas_call(body, out_shape=out_shape, in_specs=in_specs, out_specs=vm...  10.6 us
    unnamed x42, local copies, waits for them, and re-layouts  8.19 us
    ppermute x4, waiting for transfers between devices, neighbour(): return lax.ppermute(value, BOTH, pairs)  7.2 us
    ppermute x1, starting transfers between devices, shards(): theirs = lax.ppermute(whole, 'blk', swap)  3.11 us
  transfers between devices with their start and end apart: 9, of which 8 were waited for; matrix products, arithmetic and copies ran while one was open for 4% of the time, Pallas kernels for 0%

profile of v2, /device:TPU:1, one launch (start us, length us, event | category | flops | bytes accessed | tf_op | source)
XLA Modules:
  0.0 137.8 jit_solution(11977254929323868908)
XLA Ops:
  0.7 15.7 %all-to-all-start = ((bf16[256,2,128]{2,1,0:T(2,128)(2,1)}), bf16[256,2,128]{2,1,0:T(2,128)(2,1)S(1)}, u32[]{:S(2)}, u32[]{:S(2)}) async-start(bf16[256,2,128]{2,1,0:T(2,128)(2,1)} %bitcast.26), calls=%async_computation | async-start | bytes 262144 | tf_op jit(solution)/shard_map/all_to_all | solution.py:183
  19.6 9.6 %all-to-all-done = bf16[256,2,128]{2,1,0:T(2,128)(2,1)S(1)} async-done(((bf16[256,2,128]{2,1,0:T(2,128)(2,1)}), bf16[256,2,128]{2,1,0:T(2,128)(2,1)S(1)}, u32[]{:S(2)}, u32[]{:S(2)}) %all-to-all-start) | async-done | bytes 131104 | tf_op jit(solution)/shard_map/all_to_all | solution.py:183
  29.2 1.3 multiply_convert_fusion
  31.4 3.6 %collective-permute-start = (bf16[256,512]{1,0:T(8,128)(2,1)S(1)}, bf16[256,512]{1,0:T(8,128)(2,1)S(1)}, u32[]{:S(2)}, u32[]{:S(2)}) collective-permute-start(bf16[256,512]{1,0:T(8,128)(2,1)S(1)} %get-tuple-element.35), channel_id=1, source_target_pairs={{0,1},{1,2},{2,3},{3,4},{4,5},{5,6},{6,7},{7,8},{8,9},{9,10},{10,1... | collective-permute-start | bytes 786440 | tf_op jit(solution)/shard_map/ppermute | solution.py:179
  35.0 1.9 %collective-permute-start.1 = (bf16[256,512]{1,0:T(8,128)(2,1)S(1)}, bf16[256,512]{1,0:T(8,128)(2,1)S(1)}, u32[]{:S(2)}, u32[]{:S(2)}) collective-permute-start(bf16[256,512]{1,0:T(8,128)(2,1)S(1)} %get-tuple-element.35), channel_id=1, source_target_pairs={{1,0},{2,1},{3,2},{4,3},{5,4},{6,5},{7,6},{8,7},{9,8},{10,9},{11,1... | collective-permute-start | bytes 786440 | tf_op jit(solution)/shard_map/ppermute | solution.py:179
  36.9 1.8 %fusion.5.slot_cot = bf16[512,512]{1,0:T(8,128)(2,1)} fusion(s32[512]{0:T(512)S(1)} %bitcast.30, bf16[1,1440,512]{2,1,0:T(8,128)(2,1)S(1)} %copy-done), kind=kOutput, calls=%fused_computation.7 | convolution fusion | flops 755974144 | bytes 2000896 | tf_op jit(solution)/shard_map/dot_general | solution.py:26
  38.8 3.9 %collective-permute-done.1.following = bf16[256,512]{1,0:T(8,128)(2,1)S(1)} collective-permute-done((bf16[256,512]{1,0:T(8,128)(2,1)S(1)}, bf16[256,512]{1,0:T(8,128)(2,1)S(1)}, u32[]{:S(2)}, u32[]{:S(2)}) %collective-permute-start.1) | collective-permute-done | bytes 262176 | tf_op jit(solution)/shard_map/ppermute | solution.py:179
  42.7 3.6 %shard_map.173 = (bf16[1440,512]{1,0:T(8,128)(2,1)}, bf16[256,512]{1,0:T(8,128)(2,1)S(1)}, bf16[256,512]{1,0:T(8,128)(2,1)S(1)}, f32[256,512]{1,0:T(8,128)S(1)},...) custom-call(f32[256,512]{1,0:T(8,128)S(1)} %get-tuple-element.36.spectrum, ...), custom_call_target="tpu_custom_call" | custom-call | flops 1509949440 | bytes 5898240 | tf_op jit(solution)/shard_map/pallas_call | solution.py:41
  46.4 0.8 copy-done.10
  48.6 1.9 %collective-permute-start.2 = (bf16[256,512]{1,0:T(8,128)(2,1)}, bf16[256,512]{1,0:T(8,128)(2,1)S(1)}, u32[]{:S(2)}, u32[]{:S(2)}) collective-permute-start(bf16[256,512]{1,0:T(8,128)(2,1)} %get-tuple-element.21), channel_id=1, source_target_pairs={{1,0},{2,1},{3,2},{4,3},{5,4},{6,5},{7,6},{8,7},{9,8},{10,9},{11,1... | collective-permute-start | bytes 786440 | tf_op jit(solution)/shard_map/ppermute | solution.py:179
  50.5 3.6 %collective-permute-start.3 = (bf16[256,512]{1,0:T(8,128)(2,1)}, bf16[256,512]{1,0:T(8,128)(2,1)S(1)}, u32[]{:S(2)}, u32[]{:S(2)}) collective-permute-start(bf16[256,512]{1,0:T(8,128)(2,1)} %get-tuple-element.22), channel_id=1, source_target_pairs={{0,1},{1,2},{2,3},{3,4},{4,5},{5,6},{6,7},{7,8},{8,9},{9,10},{10,1... | collective-permute-start | bytes 786440 | tf_op jit(solution)/shard_map/ppermute | solution.py:179
  54.5 2.0 %collective-permute-done.2.from_next = bf16[256,512]{1,0:T(8,128)(2,1)S(1)} collective-permute-done((bf16[256,512]{1,0:T(8,128)(2,1)}, bf16[256,512]{1,0:T(8,128)(2,1)S(1)}, u32[]{:S(2)}, u32[]{:S(2)}) %collective-permute-start.2) | collective-permute-done | bytes 262176 | tf_op jit(solution)/shard_map/ppermute | solution.py:179
  56.5 1.3 collective-permute-done.3.from_prev
  57.8 0.9 copy-done.4
  58.7 1.0 copy-done.8
  59.7 1.0 copy-done.9
  60.7 1.0 copy-done.11
  61.8 0.9 copy-done.13
  62.7 0.9 copy-done.15
  63.7 1.8 %shard_map.174 = (bf16[2560,128]{1,0:T(8,128)(2,1)S(1)}, f32[2304,128]{1,0:T(8,128)S(1)}, bf16[256,128]{1,0:T(8,128)(2,1)S(1)}) custom-call(s32[1]{0:T(128)} %bitcast.7.core, f32[256,512]{1,0:T(8,128)S(1)} %copy-done.11, bf16[256,512]{1,0:T(8,128)(2,1)S(1)} %collective-permute-done.2.from_next, bf16[256,512]{1,0:T(8,128)(2,1)S(1)} %collective-permute-done.3.from_prev, ...), custom_call_target="tpu_custom_call" | custom-call | flops 786432000 | bytes 1572864 | tf_op jit(solution)/shard_map/pallas_call | solution.py:41
  65.6 2.1 %collective-permute-done.4.got = bf16[2560,128]{1,0:T(8,128)(2,1)S(1)} collective-permute-done((bf16[2560,128]{1,0:T(8,128)(2,1)S(1)}, bf16[2560,128]{1,0:T(8,128)(2,1)S(1)}, u32[]{:S(2)}, u32[]{:S(2)}) %collective-permute-start.4) | collective-permute-done | bytes 655392 | tf_op jit(solution)/shard_map/ppermute | solution.py:255
  67.7 1.0 shard_map.175
  68.7 16.2 %all-to-all-start.1 = ((bf16[16,176,128]{2,1,0:T(8,128)(2,1)}), bf16[16,176,128]{2,1,0:T(8,128)(2,1)S(1)}, u32[]{:S(2)}, u32[]{:S(2)}) async-start(bf16[16,176,128]{2,1,0:T(8,128)(2,1)} %shard_map.175), calls=%async_computation.1 | async-start | bytes 1441792 | tf_op jit(solution)/shard_map/all_to_all | solution.py:183
  85.0 11.9 %all-to-all-done.1.got = bf16[16,176,128]{2,1,0:T(8,128)(2,1)S(1)} async-done(((bf16[16,176,128]{2,1,0:T(8,128)(2,1)}), bf16[16,176,128]{2,1,0:T(8,128)(2,1)S(1)}, u32[]{:S(2)}, u32[]{:S(2)}) %all-to-all-start.1) | async-done | bytes 720928 | tf_op jit(solution)/shard_map/all_to_all | solution.py:183
  96.9 1.1 shard_map.176
  98.0 3.5 %all-to-all-start.2 = ((bf16[8,208,128]{2,1,0:T(8,128)(2,1)}), bf16[8,208,128]{2,1,0:T(8,128)(2,1)S(1)}, u32[]{:S(2)}, u32[]{:S(2)}) async-start(bf16[8,208,128]{2,1,0:T(8,128)(2,1)} %shard_map.176), calls=%async_computation.2 | async-start | bytes 851968 | tf_op jit(solution)/shard_map/all_to_all | solution.py:183
  101.6 12.1 %all-to-all-done.2.got = bf16[8,208,128]{2,1,0:T(8,128)(2,1)S(1)} async-done(((bf16[8,208,128]{2,1,0:T(8,128)(2,1)}), bf16[8,208,128]{2,1,0:T(8,128)(2,1)S(1)}, u32[]{:S(2)}, u32[]{:S(2)}) %all-to-all-start.2) | async-done | bytes 426016 | tf_op jit(solution)/shard_map/all_to_all | solution.py:183
  113.7 1.0 shard_map.177
  114.7 16.3 %all_to_all.20 = bf16[16,144,128]{2,1,0:T(8,128)(2,1)S(1)} all-to-all(bf16[16,144,128]{2,1,0:T(8,128)(2,1)S(1)} %get-tuple-element.28), channel_id=1, replica_groups=mesh['enc'=16,'blk'=16] {'enc'}, dimensions={0} | all-to-all | bytes 1179648 | tf_op jit(solution)/shard_map/all_to_all | solution.py:183
  131.0 3.1 %collective-permute-start.5 = (bf16[2304,128]{1,0:T(8,128)(2,1)S(1)}, bf16[2304,128]{1,0:T(8,128)(2,1)S(1)}, u32[]{:S(2)}, u32[]{:S(2)}) collective-permute-start(bf16[2304,128]{1,0:T(8,128)(2,1)S(1)} %bitcast.20), channel_id=1, source_target_pairs={{0,1},{1,0},{2,3},{3,2},{4,5},{5,4},{6,7},{7,6},{8,9},{9,8},{10,11... | collective-permute-start | bytes 1769480 | tf_op jit(solution)/shard_map/ppermute | solution.py:274
  134.1 1.6 %collective-permute-done.5.theirs = bf16[2304,128]{1,0:T(8,128)(2,1)S(1)} collective-permute-done((bf16[2304,128]{1,0:T(8,128)(2,1)S(1)}, bf16[2304,128]{1,0:T(8,128)(2,1)S(1)}, u32[]{:S(2)}, u32[]{:S(2)}) %collective-permute-start.5) | collective-permute-done | bytes 589856 | tf_op jit(solution)/shard_map/ppermute | solution.py:274
  135.7 2.1 %shard_map.178 = (f32[128,512]{1,0:T(8,128)}, f32[512,512]{1,0:T(8,128)}, f32[512,512]{1,0:T(8,128)}) custom-call(f32[2]{0:T(128)S(1)} %copy-done.19, s32[1]{0:T(128)} %bitcast.7.core, bf16[2304,128]{1,0:T(8,128)(2,1)S(1)} %bitcast.21, bf16[2304,128]{1,0:T(8,128)(2,1)S(1)} %collective-permute-done.5.theirs), custom_call_target="tpu_custom_call" | custom-call | flops 2359296 | bytes 3538944 | tf_op jit(solution)/shard_map/pallas_call | solution.py:41
  (53 shorter events, 6.2 us)
Async XLA Ops:
  0.6 18.3 %copy-start.1 = (bf16[256,1440]{1,0:T(8,128)(2,1)S(1)}, bf16[256,1440]{1,0:T(8,128)(2,1)}, u32[]{:S(2)}) copy-start(bf16[256,1440]{1,0:T(8,128)(2,1)} %constant.177.clone.table) | copy-start | bytes 2211844
  0.6 18.0 %copy-start.20 = (s32[1,512]{1,0:T(1,128)S(1)}, s32[1,512]{1,0:T(1,128)}, u32[]{:S(2)}) copy-start(s32[1,512]{1,0:T(1,128)} %param.15) | copy-start | bytes 6148
  0.7 28.5 %all-to-all-start = ((bf16[256,2,128]{2,1,0:T(2,128)(2,1)}), bf16[256,2,128]{2,1,0:T(2,128)(2,1)S(1)}, u32[]{:S(2)}, u32[]{:S(2)}) async-start(bf16[256,2,128]{2,1,0:T(2,128)(2,1)} %bitcast.26), calls=%async_computation | async-start | bytes 262144 | tf_op jit(solution)/shard_map/all_to_all | solution.py:183
  29.2 1.3 copy-start.7
  30.5 6.4 %copy-start = (bf16[1,1440,512]{2,1,0:T(8,128)(2,1)S(1)}, bf16[1,1440,512]{2,1,0:T(8,128)(2,1)}, u32[]{:S(2)}) copy-start(bf16[1,1440,512]{2,1,0:T(8,128)(2,1)} %param.23) | copy-start | bytes 4423684
  31.3 11.4 %copy-start.2 = (bf16[256,1440]{1,0:T(8,128)(2,1)S(1)}, bf16[256,1440]{1,0:T(8,128)(2,1)}, u32[]{:S(2)}) copy-start(bf16[256,1440]{1,0:T(8,128)(2,1)} %constant.177.clone.table) | copy-start | bytes 2211844
  31.3 11.4 %copy-start.3 = (bf16[1440,256]{1,0:T(8,128)(2,1)S(1)}, bf16[1440,256]{1,0:T(8,128)(2,1)}, u32[]{:S(2)}) copy-start(bf16[1440,256]{1,0:T(8,128)(2,1)} %constant.178.clone.table_t) | copy-start | bytes 2211844
  31.3 11.4 %copy-start.5 = (f32[256,512]{1,0:T(8,128)S(1)}, f32[256,512]{1,0:T(8,128)}, u32[]{:S(2)}) copy-start(f32[256,512]{1,0:T(8,128)} %w_spec.1) | copy-start | bytes 1572868
  31.3 11.4 %copy-start.6 = (bf16[512,512]{1,0:T(8,128)(2,1)S(1)}, bf16[512,512]{1,0:T(8,128)(2,1)}, u32[]{:S(2)}) copy-start(bf16[512,512]{1,0:T(8,128)(2,1)} %w_mix.1) | copy-start | bytes 1572868
  31.3 11.4 %copy-start.16 = (f32[256,1]{1,0:T(8,128)S(1)}, f32[256,1]{1,0:T(8,128)}, u32[]{:S(2)}) copy-start(f32[256,1]{1,0:T(8,128)} %constant.179.clone.weight) | copy-start | bytes 3076
  31.3 11.4 %copy-start.17 = (f32[1,512]{1,0:T(1,128)S(1)}, f32[1,512]{1,0:T(1,128)}, u32[]{:S(2)}) copy-start(f32[1,512]{1,0:T(1,128)} %north.1) | copy-start | bytes 6148
  31.3 11.4 %copy-start.18 = (f32[1,512]{1,0:T(1,128)S(1)}, f32[1,512]{1,0:T(1,128)}, u32[]{:S(2)}) copy-start(f32[1,512]{1,0:T(1,128)} %south.1) | copy-start | bytes 6148
  31.4 7.4 %collective-permute-start = (bf16[256,512]{1,0:T(8,128)(2,1)S(1)}, bf16[256,512]{1,0:T(8,128)(2,1)S(1)}, u32[]{:S(2)}, u32[]{:S(2)}) collective-permute-start(bf16[256,512]{1,0:T(8,128)(2,1)S(1)} %get-tuple-element.35), channel_id=1, source_target_pairs={{0,1},{1,2},{2,3},{3,4},{4,5},{5,6},{6,7},{7,8},{8,9},{9,10},{10,1... | collective-permute-start | bytes 786440 | tf_op jit(solution)/shard_map/ppermute | solution.py:179
  35.0 7.7 %collective-permute-start.1 = (bf16[256,512]{1,0:T(8,128)(2,1)S(1)}, bf16[256,512]{1,0:T(8,128)(2,1)S(1)}, u32[]{:S(2)}, u32[]{:S(2)}) collective-permute-start(bf16[256,512]{1,0:T(8,128)(2,1)S(1)} %get-tuple-element.35), channel_id=1, source_target_pairs={{1,0},{2,1},{3,2},{4,3},{5,4},{6,5},{7,6},{8,7},{9,8},{10,9},{11,1... | collective-permute-start | bytes 786440 | tf_op jit(solution)/shard_map/ppermute | solution.py:179
  46.4 0.8 copy-start.10
  47.2 0.7 copy-start.12
  47.9 0.7 copy-start.14
  48.6 7.9 %collective-permute-start.2 = (bf16[256,512]{1,0:T(8,128)(2,1)}, bf16[256,512]{1,0:T(8,128)(2,1)S(1)}, u32[]{:S(2)}, u32[]{:S(2)}) collective-permute-start(bf16[256,512]{1,0:T(8,128)(2,1)} %get-tuple-element.21), channel_id=1, source_target_pairs={{1,0},{2,1},{3,2},{4,3},{5,4},{6,5},{7,6},{8,7},{9,8},{10,9},{11,1... | collective-permute-start | bytes 786440 | tf_op jit(solution)/shard_map/ppermute | solution.py:179
  50.5 7.3 %collective-permute-start.3 = (bf16[256,512]{1,0:T(8,128)(2,1)}, bf16[256,512]{1,0:T(8,128)(2,1)S(1)}, u32[]{:S(2)}, u32[]{:S(2)}) collective-permute-start(bf16[256,512]{1,0:T(8,128)(2,1)} %get-tuple-element.22), channel_id=1, source_target_pairs={{0,1},{1,2},{2,3},{3,4},{4,5},{5,6},{6,7},{7,8},{8,9},{9,10},{10,1... | collective-permute-start | bytes 786440 | tf_op jit(solution)/shard_map/ppermute | solution.py:179
  57.8 0.9 copy-start.4
  58.7 1.0 copy-start.8
  59.7 1.0 copy-start.9
  60.7 1.0 copy-start.11
  61.8 0.9 copy-start.13
  62.7 0.9 copy-start.15
  65.5 2.2 %collective-permute-start.4 = (bf16[2560,128]{1,0:T(8,128)(2,1)S(1)}, bf16[2560,128]{1,0:T(8,128)(2,1)S(1)}, u32[]{:S(2)}, u32[]{:S(2)}) collective-permute-start(bf16[2560,128]{1,0:T(8,128)(2,1)S(1)} %get-tuple-element.27), channel_id=1, source_target_pairs={{0,1},{1,0},{2,3},{3,2},{4,5},{5,4},{6,7},{7,6},{8,9},{9,8},{10,11... | collective-permute-start | bytes 1966088 | tf_op jit(solution)/shard_map/ppermute | solution.py:255
  68.7 28.2 %all-to-all-start.1 = ((bf16[16,176,128]{2,1,0:T(8,128)(2,1)}), bf16[16,176,128]{2,1,0:T(8,128)(2,1)S(1)}, u32[]{:S(2)}, u32[]{:S(2)}) async-start(bf16[16,176,128]{2,1,0:T(8,128)(2,1)} %shard_map.175), calls=%async_computation.1 | async-start | bytes 1441792 | tf_op jit(solution)/shard_map/all_to_all | solution.py:183
  98.0 15.7 %all-to-all-start.2 = ((bf16[8,208,128]{2,1,0:T(8,128)(2,1)}), bf16[8,208,128]{2,1,0:T(8,128)(2,1)S(1)}, u32[]{:S(2)}, u32[]{:S(2)}) async-start(bf16[8,208,128]{2,1,0:T(8,128)(2,1)} %shard_map.176), calls=%async_computation.2 | async-start | bytes 851968 | tf_op jit(solution)/shard_map/all_to_all | solution.py:183
  101.4 34.3 %copy-start.19 = (f32[2]{0:T(128)S(1)}, f32[2]{0:T(128)}, u32[]{:S(2)}) copy-start(f32[2]{0:T(128)} %constant.180.clone.factors) | copy-start | bytes 28
  131.0 4.7 %collective-permute-start.5 = (bf16[2304,128]{1,0:T(8,128)(2,1)S(1)}, bf16[2304,128]{1,0:T(8,128)(2,1)S(1)}, u32[]{:S(2)}, u32[]{:S(2)}) collective-permute-start(bf16[2304,128]{1,0:T(8,128)(2,1)S(1)} %bitcast.20), channel_id=1, source_target_pairs={{0,1},{1,0},{2,3},{3,2},{4,5},{5,4},{6,7},{7,6},{8,9},{9,8},{10,11... | collective-permute-start | bytes 1769480 | tf_op jit(solution)/shard_map/ppermute | solution.py:274

commit v3 on v2

--- a/solution.py
+++ b/solution.py
@@ -1,3 +1,4 @@
+import functools
 import math
 
 import jax
@@ -34,34 +35,62 @@
     return 0.5 * jnp.tanh(0.5 * values) + 0.5
 
 
-def local_kernel(body, out_shape, flops, moved, *operands, smem=(), room=6):
+def local_kernel(body, out_shape, flops, moved, *operands, smem=(), hbm=(), hbm_out=(), room=6):
     vmem = pl.BlockSpec(memory_space=pltpu.VMEM)
-    in_specs = [pl.BlockSpec(memory_space=pltpu.SMEM) if i in smem else vmem for i in range(len(operands))]
+    far = pl.BlockSpec(memory_space=pltpu.HBM)
+    scalar = pl.BlockSpec(memory_space=pltpu.SMEM)
+    in_specs = [scalar if i in smem else far if i in hbm else vmem for i in range(len(operands))]
     single = not isinstance(out_shape, (tuple, list))
+    copies = len(hbm) + len(hbm_out)
+    held = [pltpu.VMEM(operands[i].shape, operands[i].dtype) for i in hbm]
+    held += [pltpu.VMEM(out_shape[i].shape, out_shape[i].dtype) for i in hbm_out]
     return pl.pallas_call(
         body,
         out_shape=out_shape,
         in_specs=in_specs,
-        out_specs=vmem if single else [vmem] * len(out_shape),
+        out_specs=vmem if single else [far if i in hbm_out else vmem for i in range(len(out_shape))],
+        scratch_shapes=held + ([pltpu.SemaphoreType.DMA((copies,))] if copies else []),
         compiler_params=pltpu.CompilerParams(vmem_limit_bytes=room * 1024 * 1024),
         cost_estimate=pl.CostEstimate(flops=flops, bytes_accessed=moved, transcendentals=0),
     )(*operands)
 
 
+def fetch(sources, held, sems):
+    copies = [pltpu.make_async_copy(source, held[i], sems.at[i]) for i, source in enumerate(sources)]
+    for copy in copies:
+        copy.start()
+
+    def get(i):
+        copies[i].wait()
+        return held[i][...]
+
+    return get
+
+
 def shape(dims, dtype):
     return jax.ShapeDtypeStruct(dims, dtype)
 
 
+def split(index, size):
+    assert size & (size - 1) == 0
+    return index >> (size.bit_length() - 1), index & (size - 1)
+
+
+def order_rows(slots, source):
+    at = lax.broadcasted_iota(jnp.int32, (slots, 1), 0)
+    return (source(at) == lax.broadcasted_iota(jnp.int32, (slots, slots), 1)).astype(BF16)
+
+
 def mix_body(
     spectrum, prev, following, w_spec, north, south, w_mix, weight, table_t, table, onehot, latent, cotangent,
-    state, mix_out, coeffs_out, own, to_prev, to_next,
+    state, pair_out, to_prev, to_next, pair, sems,
 ):
     north_row, south_row = north[...], south[...]
     scale = weight[...]
     mix = (
         spectrum[...] * w_spec[...] + north_row * prev[...].astype(F32) + south_row * following[...].astype(F32)
     ).astype(BF16)
-    mix_out[...] = mix
+    pair[: mix.shape[0], :] = mix
     coeffs = (dot(mix, w_mix[...]) * scale).astype(BF16)
     total = jnp.zeros(spectrum.shape, F32)
     for low, size in TILES:
@@ -73,31 +102,50 @@
         grad_pre = (cotangent[part, :].astype(F32) * (gate + silu * (1.0 - gate))).astype(BF16)
         total += dot(table[:, part], grad_pre)
     grad_coeffs = (total * scale).astype(BF16)
-    coeffs_out[...] = grad_coeffs
+    pair[mix.shape[0] :, :] = grad_coeffs
+    saved = pltpu.make_async_copy(pair, pair_out, sems.at[0])
+    saved.start()
     grad_mix = dot_tb(grad_coeffs, w_mix[...])
-    own[...] = w_spec[...] * grad_mix
     to_prev[...] = (north_row * grad_mix).astype(BF16)
     to_next[...] = (south_row * grad_mix).astype(BF16)
+    saved.wait()
 
 
 def back_body(
-    core, own, from_next, from_prev, slot_cot, slot_modes, share, w_out, pre1, hidden, rows, w_in, order, mix, coeffs,
-    sent, mine, kept,
+    core, from_next, from_prev, share, pair_far, w_mix_far, w_spec_far, rows_far, w_in_far, modes_far, cot_far, w_out_far,
+    sent, mine, kept, *held,
 ):
+    get = fetch(
+        (pair_far, w_mix_far, w_spec_far, rows_far, w_in_far, modes_far, cot_far, w_out_far), held[:-1], held[-1]
+    )
     first = core[0] == 0
-    grad_spec = (own[...] + from_next[...].astype(F32) + from_prev[...].astype(F32)).astype(BF16)
-    grad_latent = ((slot_cot[...].astype(F32) + dot_ta(slot_modes[...], grad_spec)) * share[...]).astype(BF16)
-    gate = logistic(pre1[...])
-    slope = gate * (1.0 + pre1[...] * (1.0 - gate))
-    grad_pre1 = (dot_tb(grad_latent, w_out[...]) * slope).astype(BF16)
-    row_slope = dot_tb(grad_pre1, w_in[...]).astype(BF16)
-    ordered = dot(order[...], row_slope).astype(BF16)
-    half = ordered.shape[0] // 2
+    pair = get(0)
+    count = pair.shape[0] // 2
+    mix, coeffs = pair[:count], pair[count:]
+    grad_mix = dot_tb(coeffs, get(1))
+    grad_spec = (get(2) * grad_mix + from_next[...].astype(F32) + from_prev[...].astype(F32)).astype(BF16)
+    rows, w_in = get(3), get(4)
+    pre1 = dot(rows, w_in)
+    gate = logistic(pre1)
+    hidden = (pre1 * gate).astype(BF16)
+    slope = gate * (1.0 + pre1 * (1.0 - gate))
+    from_modes = dot_ta(get(5), grad_spec)
+    grad_latent = ((get(6).astype(F32) + from_modes) * share[...]).astype(BF16)
+    grad_pre1 = (dot_tb(grad_latent, get(7)) * slope).astype(BF16)
+    row_slope = dot_tb(grad_pre1, w_in).astype(BF16)
+    half = row_slope.shape[0] // 2
+
+    def source(at):
+        other, rest = split(at, half)
+        block, slot = split(rest, CAP)
+        return (block * 2 + ((other + core[0]) & 1)) * CAP + slot
+
+    ordered = dot(order_rows(row_slope.shape[0], source), row_slope).astype(BF16)
     kept[...] = ordered[:half]
     sent[mine.shape[0] :, :] = ordered[half:]
     at = 0
     depth = mine.shape[0] // 2
-    for left, right in ((hidden[...], grad_latent), (mix[...], coeffs[...]), (rows[...], grad_pre1)):
+    for left, right in ((hidden, grad_latent), (mix, coeffs), (rows, grad_pre1)):
         width = right.shape[1] // 2
         low, high = right[:, :width], right[:, width:]
         near = dot_ta(left, jnp.where(first, low, high))
@@ -121,31 +169,46 @@
         out[i, 2 * few :, :] = (mine[part, :] + got[part, :].astype(F32)).astype(BF16)
 
 
-def relay_body(got, order, out):
+def relay_body(slots, got, out):
     sources = got.shape[0]
     count = out.shape[0]
-    few = order.shape[0] // sources
-    more = order.shape[0] // count
+    few = slots // sources
+    more = slots // count
+
+    def source(at):
+        z, rest = split(at, more)
+        block, slot = split(rest, CAP)
+        return (block * count + z) * CAP + slot
+
     total = got[0, few:, :].astype(F32)
     for i in range(1, sources):
         total += got[i, few:, :].astype(F32)
     total = total.astype(BF16)
-    ordered = dot(order[...], jnp.concatenate([got[i, :few, :] for i in range(sources)], 0)).astype(BF16)
+    ordered = dot(order_rows(slots, source), jnp.concatenate([got[i, :few, :] for i in range(sources)], 0)).astype(BF16)
     for i in range(count):
         out[i, :more, :] = ordered[i * more : (i + 1) * more, :]
         out[i, more:, :] = total
 
 
-def gather_body(got, order, out, slope):
+def gather_body(core, got, out, slope):
     sources = got.shape[0]
-    few = order.shape[0] // sources
+    slots = slope.shape[0]
+    few = slots // sources
+    encs = out.shape[0]
+
+    def source(at):
+        enc, rest = split(at, slots // encs)
+        z, rest = split(rest, 2 * CAP)
+        which, slot = split(rest, CAP)
+        return ((z * encs + enc) * 2 + ((which + core[0]) & 1)) * CAP + slot
+
     total = got[0, few:, :].astype(F32)
     for i in range(1, sources):
         total += got[i, few:, :].astype(F32)
     total = total.astype(BF16)
     for i in range(out.shape[0]):
         out[i, :, :] = total
-    ordered = dot(order[...], jnp.concatenate([got[i, :few, :] for i in range(sources)], 0))
+    ordered = dot(order_rows(slots, source), jnp.concatenate([got[i, :few, :] for i in range(sources)], 0))
     slope[...] = ordered.astype(BF16)
 
 
@@ -168,10 +231,6 @@
     phases = product.astype(np.float64) * (2.0 * math.pi / LON)
     table = np.concatenate([np.cos(phases), -np.sin(phases)], 0)
     return jnp.asarray(table, BF16), jnp.asarray(np.ascontiguousarray(table.T), BF16)
-
-
-def selection(source):
-    return (source[:, None] == jnp.arange(source.shape[0], dtype=jnp.int32)[None, :]).astype(BF16)
 
 
 def neighbour(value, count, step):
@@ -201,25 +260,17 @@
 
     lon = lon_index[0]
     live = (jnp.arange(CAP, dtype=jnp.int32)[None, :] < live_count[0][:, None]).reshape(-1)
-    cell = jnp.where(live, lon, -1)
-    onehot = (cell[None, :] == jnp.arange(LON, dtype=jnp.int32)[:, None]).astype(BF16)
+    cell, core_arg = lax.optimization_barrier((jnp.where(live, lon, -1), core_arg))
     shared = jnp.sum((lon[:, None] == cell[None, :]).astype(F32), axis=1)
     share = (1.0 / jnp.maximum(shared, 1.0))[:, None]
     table, table_t = phase_tables()
     weight = jnp.asarray(np.where(np.arange(2 * MODES) % MODES == 0, 1.0, 2.0)[:, None] / LON, F32)
     cotangent = loss_sensitivity[0]
+    half = slots // 2
+    modes = (2 * MODES, code)
+    onehot = (cell[None, :] == jnp.arange(LON, dtype=jnp.int32)[:, None]).astype(BF16)
     slot_modes = dot(table, onehot).astype(BF16)
     slot_cot = dot_ta(onehot, cotangent).astype(BF16)
-    at = jnp.arange(slots, dtype=jnp.int32)
-    slot = at % CAP
-    half = slots // 2
-    enc_at, z_at = at % half // (deep * CAP), at // CAP % deep
-    order1 = selection(((enc_at * deep + z_at) * 2 + (at // half + core) % 2) * CAP + slot)
-    z_at, enc_core = at // (encs * 2 * CAP), at // CAP % (encs * 2)
-    order2 = selection((enc_core * deep + z_at) * CAP + slot)
-    enc_at, z_at, core_at = at // (deep * 2 * CAP), at // (2 * CAP) % deep, at // CAP % 2
-    order3 = selection(((z_at * encs + enc_at) * 2 + (core_at + core) % 2) * CAP + slot)
-
     pre1 = dot(rows, w_in)
     hidden = (pre1 * logistic(pre1)).astype(BF16)
     latent = (dot(hidden, w_out) * share).astype(BF16)
@@ -228,16 +279,13 @@
     prev = neighbour(outgoing, devices, 1)
     following = neighbour(outgoing, devices, -1)
 
-    modes = (2 * MODES, code)
-    state, mix, coeffs, own, to_prev, to_next = local_kernel(
+    state, pair, to_prev, to_next = local_kernel(
         mix_body,
-        [
-            shape((LON, code), BF16), shape(modes, BF16), shape(modes, BF16),
-            shape(modes, F32), shape(modes, BF16), shape(modes, BF16),
-        ],
+        [shape((LON, code), BF16), shape((4 * MODES, code), BF16), shape(modes, BF16), shape(modes, BF16)],
         2 * LON * code * (4 * MODES + slots),
         8 * LON * code,
         spectrum, prev, following, w_spec, north, south, w_mix, weight, table_t, table, onehot, latent, cotangent,
+        hbm_out=(1,),
         room=12,
     )
     from_next = neighbour(to_prev, devices, -1)
@@ -248,9 +296,10 @@
         [shape((2 * depth + half, LANES), BF16), shape((2 * depth, LANES), F32), shape((half, LANES), BF16)],
         2 * slots * code * 1500,
         6 * slots * code,
-        core_arg, own, from_next, from_prev, slot_cot, slot_modes, share, w_out, pre1, hidden, rows, w_in, order1, mix, coeffs,
+        core_arg, from_next, from_prev, share, pair, w_mix, w_spec, rows, w_in, slot_modes, slot_cot, w_out,
         smem=(0,),
-        room=10,
+        hbm=(4, 5, 6, 7, 8, 9, 10, 11),
+        room=16,
     )
     got = lax.ppermute(sent, "blk", swap)
     chunk = 2 * depth // encs
@@ -260,7 +309,11 @@
     )
     parts = all_swap(parts, "enc")
     parts = local_kernel(
-        relay_body, shape((deep, more + chunk, LANES), BF16), 10 * depth * LANES, 8 * depth * LANES, parts, order2
+        functools.partial(relay_body, slots),
+        shape((deep, more + chunk, LANES), BF16),
+        10 * depth * LANES,
+        8 * depth * LANES,
+        parts,
     )
     parts = all_swap(parts, "blk", columns)
     spread, observation_slope = local_kernel(
@@ -268,7 +321,8 @@
         [shape((encs, chunk, LANES), BF16), shape((slots, LANES), BF16)],
         10 * depth * LANES,
         8 * depth * LANES,
-        parts, order3,
+        core_arg, parts,
+        smem=(0,),
     )
     whole = all_swap(spread, "enc").reshape(2 * depth, LANES)
     theirs = lax.ppermute(whole, "blk", swap)

time: 139 us -> 128 us (0.921)
  blocking collectives: 16.3 us -> 57.7 us
  waiting for transfers between devices: 44.4 us -> 19.3 us
  starting transfers between devices: 49.6 us -> 30.7 us
  local copies, waits for them, and re-layouts: 8.49 us -> 0.36 us
    all_to_all x1 -> x3, blocking collectives: 16.3 us -> 57.7 us  [all_swap(): lax.all_to_all(blocks, axis, split_axis=0, concat_axis=0, tiled=True, axi...]
    all_to_all x3 -> x1, waiting for transfers between devices: 33.5 us -> 8.23 us  [all_swap(): lax.all_to_all(blocks, axis, split_axis=0, concat_axis=0, tiled=True, axi...]
    all_to_all x3 -> x1, starting transfers between devices: 35.3 us -> 15.7 us  [all_swap(): lax.all_to_all(blocks, axis, split_axis=0, concat_axis=0, tiled=True, axi...]
    unnamed x42 -> x22, local copies, waits for them, and re-layouts: 8.19 us -> 0.07 us
  transfers between devices with their start and end apart: 9 -> 7, of which waited for: 8 -> 7; matrix products, arithmetic and copies ran while one was open for 4% -> 5% of each run, Pallas kernels for 0% -> 0%
where the time goes in v3:
time: 128 us; the launch traced here: 127 us
  blocking collectives  57.7 us (45%)
  starting transfers between devices  30.7 us (24%)
  waiting for transfers between devices  19.3 us (15%)
  Pallas kernels  11.4 us (9%)
  matrix products  3.81 us (3%)
  other arithmetic  3.05 us (2%)
    all_to_all x3, blocking collectives, all_swap(): lax.all_to_all(blocks, axis, split_axis=0, concat_axis=0, tiled=True, axi...  57.7 us
    all_to_all x1, starting transfers between devices, all_swap(): lax.all_to_all(blocks, axis, split_axis=0, concat_axis=0, tiled=True, axi...  15.7 us
    pallas_call x6, Pallas kernels, local_kernel(): pl.pallas_call(body, out_shape=out_shape, in_specs=in_specs, out_specs=vm...  11.4 us
    ppermute x4, starting transfers between devices, neighbour(): return lax.ppermute(value, BOTH, pairs)  11.1 us
    all_to_all x1, waiting for transfers between devices, all_swap(): lax.all_to_all(blocks, axis, split_axis=0, concat_axis=0, tiled=True, axi...  8.23 us
    ppermute x4, waiting for transfers between devices, neighbour(): return lax.ppermute(value, BOTH, pairs)  7.37 us
    ppermute x1, starting transfers between devices, shards(): theirs = lax.ppermute(whole, 'blk', swap)  3.86 us
    dot_general x3, matrix products, dot(): return jnp.dot(a, b, preferred_element_type=F32)  2.78 us
  transfers between devices with their start and end apart: 7, of which 7 were waited for; matrix products, arithmetic and copies ran while one was open for 5% of the time, Pallas kernels for 0%

profile of v3, /device:TPU:1, one launch (start us, length us, event | category | flops | bytes accessed | tf_op | source)
XLA Modules:
  0.0 127.2 jit_solution(12164286412907096909)
XLA Ops:
  0.6 15.7 %all-to-all-start = ((bf16[256,2,128]{2,1,0:T(2,128)(2,1)}), bf16[256,2,128]{2,1,0:T(2,128)(2,1)S(1)}, u32[]{:S(2)}, u32[]{:S(2)}) async-start(bf16[256,2,128]{2,1,0:T(2,128)(2,1)} %bitcast.24), calls=%async_computation | async-start | bytes 262144 | tf_op jit(solution)/shard_map/all_to_all | solution.py:242
  16.3 0.8 iota_compare_fusion.7
  17.1 0.1 lt.29
  17.3 0.7 broadcast_select_fusion
  17.9 0.9 convert_reduce_fusion
  18.9 0.1 copy.23.share
  19.1 1.9 %fusion.7 = bf16[512,256]{0,1:T(8,128)(2,1)S(1)} fusion(bf16[256,1440]{1,0:T(8,128)(2,1)} %constant.33.clone.table, s32[512]{0:T(512)S(1)} %broadcast_select_fusion), kind=kOutput, calls=%fused_computation.9 | convolution fusion | flops 378355712 | bytes 1001472 | tf_op jit(solution)/shard_map/dot_general | solution.py:23
  20.9 8.2 %all-to-all-done = bf16[256,2,128]{2,1,0:T(2,128)(2,1)S(1)} async-done(((bf16[256,2,128]{2,1,0:T(2,128)(2,1)}), bf16[256,2,128]{2,1,0:T(2,128)(2,1)S(1)}, u32[]{:S(2)}, u32[]{:S(2)}) %all-to-all-start) | async-done | bytes 131104 | tf_op jit(solution)/shard_map/all_to_all | solution.py:242
  29.2 0.6 fusion.6.latent
  29.9 0.3 fusion.11
  30.2 3.6 %collective-permute-start = (bf16[256,512]{1,0:T(8,128)(2,1)S(1)}, bf16[256,512]{1,0:T(8,128)(2,1)S(1)}, u32[]{:S(2)}, u32[]{:S(2)}) collective-permute-start(bf16[256,512]{1,0:T(8,128)(2,1)S(1)} %get-tuple-element.33), channel_id=1, source_target_pairs={{0,1},{1,2},{2,3},{3,4},{4,5},{5,6},{6,7},{7,8},{8,9},{9,10},{10,1... | collective-permute-start | bytes 786440 | tf_op jit(solution)/shard_map/ppermute | solution.py:238
  33.8 1.9 %collective-permute-start.1 = (bf16[256,512]{1,0:T(8,128)(2,1)S(1)}, bf16[256,512]{1,0:T(8,128)(2,1)S(1)}, u32[]{:S(2)}, u32[]{:S(2)}) collective-permute-start(bf16[256,512]{1,0:T(8,128)(2,1)S(1)} %get-tuple-element.33), channel_id=1, source_target_pairs={{1,0},{2,1},{3,2},{4,3},{5,4},{6,5},{7,6},{8,7},{9,8},{10,9},{11,1... | collective-permute-start | bytes 786440 | tf_op jit(solution)/shard_map/ppermute | solution.py:238
  35.7 0.6 fusion.1.onehot
  36.4 0.7 collective-permute-done.prev
  37.1 4.4 %collective-permute-done.1.following = bf16[256,512]{1,0:T(8,128)(2,1)S(1)} collective-permute-done((bf16[256,512]{1,0:T(8,128)(2,1)S(1)}, bf16[256,512]{1,0:T(8,128)(2,1)S(1)}, u32[]{:S(2)}, u32[]{:S(2)}) %collective-permute-start.1) | collective-permute-done | bytes 262176 | tf_op jit(solution)/shard_map/ppermute | solution.py:238
  41.6 4.2 %shard_map.173 = (bf16[1440,512]{1,0:T(8,128)(2,1)}, bf16[512,512]{1,0:T(8,128)(2,1)S(1)}, bf16[256,512]{1,0:T(8,128)(2,1)S(1)}, bf16[256,512]{1,0:T(8,128)(2,1)S(1)}) custom-call(f32[256,512]{1,0:T(8,128)S(1)} %get-tuple-element.34.spectrum, bf16[256,512]{1,0:T(8,128)(2,1)S(1)} %collective-permute-done.prev, ...), custom_call_target="tpu_custom_call" | custom-call | flops 1509949440 | bytes 5898240 | tf_op jit(solution)/shard_map/pallas_call | solution.py:47
  45.7 1.9 %collective-permute-start.2 = (bf16[256,512]{1,0:T(8,128)(2,1)S(1)}, bf16[256,512]{1,0:T(8,128)(2,1)S(1)}, u32[]{:S(2)}, u32[]{:S(2)}) collective-permute-start(bf16[256,512]{1,0:T(8,128)(2,1)S(1)} %get-tuple-element.22), channel_id=1, source_target_pairs={{1,0},{2,1},{3,2},{4,3},{5,4},{6,5},{7,6},{8,7},{9,8},{10,9},{11,1... | collective-permute-start | bytes 786440 | tf_op jit(solution)/shard_map/ppermute | solution.py:238
  47.6 3.6 %collective-permute-start.3 = (bf16[256,512]{1,0:T(8,128)(2,1)S(1)}, bf16[256,512]{1,0:T(8,128)(2,1)S(1)}, u32[]{:S(2)}, u32[]{:S(2)}) collective-permute-start(bf16[256,512]{1,0:T(8,128)(2,1)S(1)} %get-tuple-element.23), channel_id=1, source_target_pairs={{0,1},{1,2},{2,3},{3,4},{4,5},{5,6},{6,7},{7,8},{8,9},{9,10},{10,1... | collective-permute-start | bytes 786440 | tf_op jit(solution)/shard_map/ppermute | solution.py:238
  51.3 1.0 fusion.5.cot_far
  52.3 1.1 collective-permute-done.2.from_next
  53.4 1.2 collective-permute-done.3.from_prev
  54.6 3.7 %shard_map.174 = (bf16[2560,128]{1,0:T(8,128)(2,1)S(1)}, f32[2304,128]{1,0:T(8,128)S(1)}, bf16[256,128]{1,0:T(8,128)(2,1)S(1)}) custom-call(s32[1]{0:T(128)} %bitcast.2.core, bf16[256,512]{1,0:T(8,128)(2,1)S(1)} %collective-permute-done.2.from_next, bf16[256,512]{1,0:T(8,128)(2,1)S(1)} %collective-permute-done.3.from_prev, f32[512,1]{1,0:T(8,128)S(1)} %copy.23.share, ...), custom_call_target="tpu_custom_call" | custom-call | flops 786432000 | bytes 1572864 | tf_op jit(solution)/shard_map/pallas_call | solution.py:47
  58.4 2.1 %collective-permute-done.4.got = bf16[2560,128]{1,0:T(8,128)(2,1)S(1)} collective-permute-done((bf16[2560,128]{1,0:T(8,128)(2,1)S(1)}, bf16[2560,128]{1,0:T(8,128)(2,1)S(1)}, u32[]{:S(2)}, u32[]{:S(2)}) %collective-permute-start.4) | collective-permute-done | bytes 655392 | tf_op jit(solution)/shard_map/ppermute | solution.py:304
  60.5 0.1 shard_map.175
  60.6 28.6 %all_to_all.20.got = bf16[16,176,128]{2,1,0:T(8,128)(2,1)S(1)} all-to-all(bf16[16,176,128]{2,1,0:T(8,128)(2,1)S(1)} %shard_map.175), channel_id=1, replica_groups=mesh['enc'=16,'blk'=16] {'enc'}, dimensions={0} | all-to-all | bytes 1441792 | tf_op jit(solution)/shard_map/all_to_all | solution.py:242
  89.1 0.3 shard_map.176
  89.4 15.2 %all_to_all.21.got = bf16[8,208,128]{2,1,0:T(8,128)(2,1)S(1)} all-to-all(bf16[8,208,128]{2,1,0:T(8,128)(2,1)S(1)} %shard_map.176), channel_id=1, replica_groups={{0,2,4,6,8,10,12,14},{1,3,5,7,9,11,13,15},{16,18,20,22,24,26,28,30},{17..., dimensions={0} | all-to-all | bytes 851968 | tf_op jit(solution)/shard_map/all_to_all | solution.py:242
  104.7 1.0 shard_map.177
  105.7 13.9 %all_to_all.22 = bf16[16,144,128]{2,1,0:T(8,128)(2,1)S(1)} all-to-all(bf16[16,144,128]{2,1,0:T(8,128)(2,1)S(1)} %get-tuple-element.28), channel_id=1, replica_groups=mesh['enc'=16,'blk'=16] {'enc'}, dimensions={0} | all-to-all | bytes 1179648 | tf_op jit(solution)/shard_map/all_to_all | solution.py:242
  119.6 3.9 %collective-permute-start.5 = (bf16[2304,128]{1,0:T(8,128)(2,1)S(1)}, bf16[2304,128]{1,0:T(8,128)(2,1)S(1)}, u32[]{:S(2)}, u32[]{:S(2)}) collective-permute-start(bf16[2304,128]{1,0:T(8,128)(2,1)S(1)} %bitcast.18), channel_id=1, source_target_pairs={{0,1},{1,0},{2,3},{3,2},{4,5},{5,4},{6,7},{7,6},{8,9},{9,8},{10,11... | collective-permute-start | bytes 1769480 | tf_op jit(solution)/shard_map/ppermute | solution.py:328
  123.5 1.6 %collective-permute-done.5.theirs = bf16[2304,128]{1,0:T(8,128)(2,1)S(1)} collective-permute-done((bf16[2304,128]{1,0:T(8,128)(2,1)S(1)}, bf16[2304,128]{1,0:T(8,128)(2,1)S(1)}, u32[]{:S(2)}, u32[]{:S(2)}) %collective-permute-start.5) | collective-permute-done | bytes 589856 | tf_op jit(solution)/shard_map/ppermute | solution.py:328
  125.1 2.1 %shard_map.178 = (f32[128,512]{1,0:T(8,128)}, f32[512,512]{1,0:T(8,128)}, f32[512,512]{1,0:T(8,128)}) custom-call(f32[2]{0:T(128)S(1)} %copy-done.10, s32[1]{0:T(128)} %bitcast.2.core, bf16[2304,128]{1,0:T(8,128)(2,1)S(1)} %bitcast.19, bf16[2304,128]{1,0:T(8,128)(2,1)S(1)} %collective-permute-done.5.theirs), custom_call_target="tpu_custom_call" | custom-call | flops 2359296 | bytes 3538944 | tf_op jit(solution)/shard_map/pallas_call | solution.py:47
  (24 shorter events, 0.2 us)
Async XLA Ops:
  0.6 28.5 %all-to-all-start = ((bf16[256,2,128]{2,1,0:T(2,128)(2,1)}), bf16[256,2,128]{2,1,0:T(2,128)(2,1)S(1)}, u32[]{:S(2)}, u32[]{:S(2)}) async-start(bf16[256,2,128]{2,1,0:T(2,128)(2,1)} %bitcast.24), calls=%async_computation | async-start | bytes 262144 | tf_op jit(solution)/shard_map/all_to_all | solution.py:242
  18.9 10.3 %copy-start.5 = (bf16[512,512]{1,0:T(8,128)(2,1)S(1)}, bf16[512,512]{1,0:T(8,128)(2,1)}, u32[]{:S(2)}) copy-start(bf16[512,512]{1,0:T(8,128)(2,1)} %w_out_far.1) | copy-start | bytes 1572868
  18.9 10.3 %copy-start.7 = (bf16[128,512]{1,0:T(8,128)(2,1)S(1)}, bf16[128,512]{1,0:T(8,128)(2,1)}, u32[]{:S(2)}) copy-start(bf16[128,512]{1,0:T(8,128)(2,1)} %w_in_far.1) | copy-start | bytes 393220
  29.2 12.3 %copy-start.3 = (bf16[256,1440]{1,0:T(8,128)(2,1)S(1)}, bf16[256,1440]{1,0:T(8,128)(2,1)}, u32[]{:S(2)}) copy-start(bf16[256,1440]{1,0:T(8,128)(2,1)} %constant.33.clone.table) | copy-start | bytes 2211844
  29.2 12.3 %copy-start.4 = (bf16[1440,256]{1,0:T(8,128)(2,1)S(1)}, bf16[1440,256]{1,0:T(8,128)(2,1)}, u32[]{:S(2)}) copy-start(bf16[1440,256]{1,0:T(8,128)(2,1)} %constant.34.clone.table_t) | copy-start | bytes 2211844
  29.8 11.7 %copy-start = (f32[256,512]{1,0:T(8,128)S(1)}, f32[256,512]{1,0:T(8,128)}, u32[]{:S(2)}) copy-start(f32[256,512]{1,0:T(8,128)} %w_spec_far.1) | copy-start | bytes 1572868
  29.8 11.7 %copy-start.1 = (bf16[512,512]{1,0:T(8,128)(2,1)S(1)}, bf16[512,512]{1,0:T(8,128)(2,1)}, u32[]{:S(2)}) copy-start(bf16[512,512]{1,0:T(8,128)(2,1)} %w_mix_far.1) | copy-start | bytes 1572868
  29.8 11.7 %copy-start.2 = (bf16[1,1440,512]{2,1,0:T(8,128)(2,1)S(1)}, bf16[1,1440,512]{2,1,0:T(8,128)(2,1)}, u32[]{:S(2)}) copy-start(bf16[1,1440,512]{2,1,0:T(8,128)(2,1)} %param.23) | copy-start | bytes 4423684
  29.8 11.7 %copy-start.6 = (f32[256,1]{1,0:T(8,128)S(1)}, f32[256,1]{1,0:T(8,128)}, u32[]{:S(2)}) copy-start(f32[256,1]{1,0:T(8,128)} %constant.35.clone.weight) | copy-start | bytes 3076
  29.8 11.7 %copy-start.8 = (f32[1,512]{1,0:T(1,128)S(1)}, f32[1,512]{1,0:T(1,128)}, u32[]{:S(2)}) copy-start(f32[1,512]{1,0:T(1,128)} %north.1) | copy-start | bytes 6148
  29.9 11.7 %copy-start.9 = (f32[1,512]{1,0:T(1,128)S(1)}, f32[1,512]{1,0:T(1,128)}, u32[]{:S(2)}) copy-start(f32[1,512]{1,0:T(1,128)} %south.1) | copy-start | bytes 6148
  30.2 6.9 %collective-permute-start = (bf16[256,512]{1,0:T(8,128)(2,1)S(1)}, bf16[256,512]{1,0:T(8,128)(2,1)S(1)}, u32[]{:S(2)}, u32[]{:S(2)}) collective-permute-start(bf16[256,512]{1,0:T(8,128)(2,1)S(1)} %get-tuple-element.33), channel_id=1, source_target_pairs={{0,1},{1,2},{2,3},{3,4},{4,5},{5,6},{6,7},{7,8},{8,9},{9,10},{10,1... | collective-permute-start | bytes 786440 | tf_op jit(solution)/shard_map/ppermute | solution.py:238
  33.8 7.7 %collective-permute-start.1 = (bf16[256,512]{1,0:T(8,128)(2,1)S(1)}, bf16[256,512]{1,0:T(8,128)(2,1)S(1)}, u32[]{:S(2)}, u32[]{:S(2)}) collective-permute-start(bf16[256,512]{1,0:T(8,128)(2,1)S(1)} %get-tuple-element.33), channel_id=1, source_target_pairs={{1,0},{2,1},{3,2},{4,3},{5,4},{6,5},{7,6},{8,7},{9,8},{10,9},{11,1... | collective-permute-start | bytes 786440 | tf_op jit(solution)/shard_map/ppermute | solution.py:238
  45.7 7.7 %collective-permute-start.2 = (bf16[256,512]{1,0:T(8,128)(2,1)S(1)}, bf16[256,512]{1,0:T(8,128)(2,1)S(1)}, u32[]{:S(2)}, u32[]{:S(2)}) collective-permute-start(bf16[256,512]{1,0:T(8,128)(2,1)S(1)} %get-tuple-element.22), channel_id=1, source_target_pairs={{1,0},{2,1},{3,2},{4,3},{5,4},{6,5},{7,6},{8,7},{9,8},{10,9},{11,1... | collective-permute-start | bytes 786440 | tf_op jit(solution)/shard_map/ppermute | solution.py:238
  47.6 6.9 %collective-permute-start.3 = (bf16[256,512]{1,0:T(8,128)(2,1)S(1)}, bf16[256,512]{1,0:T(8,128)(2,1)S(1)}, u32[]{:S(2)}, u32[]{:S(2)}) collective-permute-start(bf16[256,512]{1,0:T(8,128)(2,1)S(1)} %get-tuple-element.23), channel_id=1, source_target_pairs={{0,1},{1,2},{2,3},{3,4},{4,5},{5,6},{6,7},{7,8},{8,9},{9,10},{10,1... | collective-permute-start | bytes 786440 | tf_op jit(solution)/shard_map/ppermute | solution.py:238
  58.3 2.2 %collective-permute-start.4 = (bf16[2560,128]{1,0:T(8,128)(2,1)S(1)}, bf16[2560,128]{1,0:T(8,128)(2,1)S(1)}, u32[]{:S(2)}, u32[]{:S(2)}) collective-permute-start(bf16[2560,128]{1,0:T(8,128)(2,1)S(1)} %get-tuple-element.27), channel_id=1, source_target_pairs={{0,1},{1,0},{2,3},{3,2},{4,5},{5,4},{6,7},{7,6},{8,9},{9,8},{10,11... | collective-permute-start | bytes 1966088 | tf_op jit(solution)/shard_map/ppermute | solution.py:304
  89.4 35.7 %copy-start.10 = (f32[2]{0:T(128)S(1)}, f32[2]{0:T(128)}, u32[]{:S(2)}) copy-start(f32[2]{0:T(128)} %constant.36.clone.factors) | copy-start | bytes 28
  119.6 5.5 %collective-permute-start.5 = (bf16[2304,128]{1,0:T(8,128)(2,1)S(1)}, bf16[2304,128]{1,0:T(8,128)(2,1)S(1)}, u32[]{:S(2)}, u32[]{:S(2)}) collective-permute-start(bf16[2304,128]{1,0:T(8,128)(2,1)S(1)} %bitcast.18), channel_id=1, source_target_pairs={{0,1},{1,0},{2,3},{3,2},{4,5},{5,4},{6,7},{7,6},{8,9},{9,8},{10,11... | collective-permute-start | bytes 1769480 | tf_op jit(solution)/shard_map/ppermute | solution.py:328

commit v4 on v3

--- a/solution.py
+++ b/solution.py
@@ -35,38 +35,26 @@
     return 0.5 * jnp.tanh(0.5 * values) + 0.5
 
 
-def local_kernel(body, out_shape, flops, moved, *operands, smem=(), hbm=(), hbm_out=(), room=6):
+def local_kernel(body, out_shape, flops, moved, *operands, smem=(), room=6, held=(), aliases=None):
     vmem = pl.BlockSpec(memory_space=pltpu.VMEM)
-    far = pl.BlockSpec(memory_space=pltpu.HBM)
-    scalar = pl.BlockSpec(memory_space=pltpu.SMEM)
-    in_specs = [scalar if i in smem else far if i in hbm else vmem for i in range(len(operands))]
+    in_specs = [pl.BlockSpec(memory_space=pltpu.SMEM) if i in smem else vmem for i in range(len(operands))]
     single = not isinstance(out_shape, (tuple, list))
-    copies = len(hbm) + len(hbm_out)
-    held = [pltpu.VMEM(operands[i].shape, operands[i].dtype) for i in hbm]
-    held += [pltpu.VMEM(out_shape[i].shape, out_shape[i].dtype) for i in hbm_out]
+    far = pl.BlockSpec(memory_space=pl.ANY)
+    aliases = aliases or {}
+    in_specs = [far if i in aliases else spec for i, spec in enumerate(in_specs)]
+    out = far if held else vmem
     return pl.pallas_call(
         body,
         out_shape=out_shape,
         in_specs=in_specs,
-        out_specs=vmem if single else [far if i in hbm_out else vmem for i in range(len(out_shape))],
-        scratch_shapes=held + ([pltpu.SemaphoreType.DMA((copies,))] if copies else []),
+        out_specs=out if single else [out] * len(out_shape),
+        scratch_shapes=[pltpu.VMEM(dims, F32) for dims in held] + ([pltpu.SemaphoreType.DMA((len(held),))] if held else []),
+        input_output_aliases=aliases,
         compiler_params=pltpu.CompilerParams(vmem_limit_bytes=room * 1024 * 1024),
         cost_estimate=pl.CostEstimate(flops=flops, bytes_accessed=moved, transcendentals=0),
     )(*operands)
 
 
-def fetch(sources, held, sems):
-    copies = [pltpu.make_async_copy(source, held[i], sems.at[i]) for i, source in enumerate(sources)]
-    for copy in copies:
-        copy.start()
-
-    def get(i):
-        copies[i].wait()
-        return held[i][...]
-
-    return get
-
-
 def shape(dims, dtype):
     return jax.ShapeDtypeStruct(dims, dtype)
 
@@ -82,8 +70,8 @@
 
 
 def mix_body(
-    spectrum, prev, following, w_spec, north, south, w_mix, weight, table_t, table, onehot, latent, cotangent,
-    state, pair_out, to_prev, to_next, pair, sems,
+    spectrum, prev, following, w_spec, north, south, w_mix, weight, table_t, table, cotangent,
+    pair, coeffs_out, to_prev, to_next,
 ):
     north_row, south_row = north[...], south[...]
     scale = weight[...]
@@ -92,47 +80,46 @@
     ).astype(BF16)
     pair[: mix.shape[0], :] = mix
     coeffs = (dot(mix, w_mix[...]) * scale).astype(BF16)
+    coeffs_out[...] = coeffs
     total = jnp.zeros(spectrum.shape, F32)
     for low, size in TILES:
         part = pl.ds(low, size)
         pre_act = dot(table_t[part, :], coeffs)
         gate = logistic(pre_act)
-        silu = pre_act * gate
-        state[part, :] = (dot(onehot[part, :], latent[...]) + silu).astype(BF16)
-        grad_pre = (cotangent[part, :].astype(F32) * (gate + silu * (1.0 - gate))).astype(BF16)
+        slope = gate * (1.0 + pre_act * (1.0 - gate))
+        grad_pre = (cotangent[part, :].astype(F32) * slope).astype(BF16)
         total += dot(table[:, part], grad_pre)
     grad_coeffs = (total * scale).astype(BF16)
     pair[mix.shape[0] :, :] = grad_coeffs
-    saved = pltpu.make_async_copy(pair, pair_out, sems.at[0])
-    saved.start()
     grad_mix = dot_tb(grad_coeffs, w_mix[...])
     to_prev[...] = (north_row * grad_mix).astype(BF16)
     to_next[...] = (south_row * grad_mix).astype(BF16)
-    saved.wait()
+
+
+def state_body(table_t, coeffs, onehot, latent, state):
+    for low, size in TILES:
+        part = pl.ds(low, size)
+        pre_act = dot(table_t[part, :], coeffs[...])
+        state[part, :] = (dot(onehot[part, :], latent[...]) + pre_act * logistic(pre_act)).astype(BF16)
 
 
 def back_body(
-    core, from_next, from_prev, share, pair_far, w_mix_far, w_spec_far, rows_far, w_in_far, modes_far, cot_far, w_out_far,
-    sent, mine, kept, *held,
+    core, from_next, from_prev, share, pair, w_mix, w_spec, rows, w_in, slot_modes, slot_cot, w_out,
+    sent, mine, kept,
 ):
-    get = fetch(
-        (pair_far, w_mix_far, w_spec_far, rows_far, w_in_far, modes_far, cot_far, w_out_far), held[:-1], held[-1]
-    )
     first = core[0] == 0
-    pair = get(0)
     count = pair.shape[0] // 2
-    mix, coeffs = pair[:count], pair[count:]
-    grad_mix = dot_tb(coeffs, get(1))
-    grad_spec = (get(2) * grad_mix + from_next[...].astype(F32) + from_prev[...].astype(F32)).astype(BF16)
-    rows, w_in = get(3), get(4)
-    pre1 = dot(rows, w_in)
+    mix, coeffs = pair[:count, :], pair[count:, :]
+    grad_mix = dot_tb(coeffs, w_mix[...])
+    grad_spec = (w_spec[...] * grad_mix + from_next[...].astype(F32) + from_prev[...].astype(F32)).astype(BF16)
+    pre1 = dot(rows[...], w_in[...])
     gate = logistic(pre1)
     hidden = (pre1 * gate).astype(BF16)
     slope = gate * (1.0 + pre1 * (1.0 - gate))
-    from_modes = dot_ta(get(5), grad_spec)
-    grad_latent = ((get(6).astype(F32) + from_modes) * share[...]).astype(BF16)
-    grad_pre1 = (dot_tb(grad_latent, get(7)) * slope).astype(BF16)
-    row_slope = dot_tb(grad_pre1, w_in).astype(BF16)
+    from_modes = dot_ta(slot_modes[...], grad_spec)
+    grad_latent = ((slot_cot[...].astype(F32) + from_modes) * share[...]).astype(BF16)
+    grad_pre1 = (dot_tb(grad_latent, w_out[...]) * slope).astype(BF16)
+    row_slope = dot_tb(grad_pre1, w_in[...]).astype(BF16)
     half = row_slope.shape[0] // 2
 
     def source(at):
@@ -145,7 +132,7 @@
     sent[mine.shape[0] :, :] = ordered[half:]
     at = 0
     depth = mine.shape[0] // 2
-    for left, right in ((hidden, grad_latent), (mix, coeffs), (rows, grad_pre1)):
+    for left, right in ((hidden, grad_latent), (mix, coeffs), (rows[...], grad_pre1)):
         width = right.shape[1] // 2
         low, high = right[:, :width], right[:, width:]
         near = dot_ta(left, jnp.where(first, low, high))
@@ -190,11 +177,19 @@
         out[i, more:, :] = total
 
 
-def gather_body(core, got, out, slope):
+def spread_body(few, got, out):
+    total = got[0, few:, :].astype(F32)
+    for i in range(1, got.shape[0]):
+        total += got[i, few:, :].astype(F32)
+    total = total.astype(BF16)
+    for i in range(out.shape[0]):
+        out[i, :, :] = total
+
+
+def return_body(encs, core, got, slope):
     sources = got.shape[0]
     slots = slope.shape[0]
     few = slots // sources
-    encs = out.shape[0]
 
     def source(at):
         enc, rest = split(at, slots // encs)
@@ -202,28 +197,29 @@
         which, slot = split(rest, CAP)
         return ((z * encs + enc) * 2 + ((which + core[0]) & 1)) * CAP + slot
 
-    total = got[0, few:, :].astype(F32)
-    for i in range(1, sources):
-        total += got[i, few:, :].astype(F32)
-    total = total.astype(BF16)
-    for i in range(out.shape[0]):
-        out[i, :, :] = total
     ordered = dot(order_rows(slots, source), jnp.concatenate([got[i, :few, :] for i in range(sources)], 0))
     slope[...] = ordered.astype(BF16)
 
 
-def final_body(factors, core, whole, theirs, entry, exit_, blend):
-    first = core[0] == 0
-    depth = whole.shape[0] // 2
-    for piece in range(2):
-        at = piece * depth
-        for out, factor in ((exit_, factors[0]), (blend, factors[1]), (entry, factors[0])):
-            size = out.shape[0]
-            ours = whole[at : at + size, :].astype(F32) * factor
-            other = theirs[at : at + size, :].astype(F32) * factor
-            out[:, piece * LANES : (piece + 1) * LANES] = jnp.where(first, ours, other)
-            out[:, (2 + piece) * LANES : (3 + piece) * LANES] = jnp.where(first, other, ours)
-            at += size
+def final_body(other, factors, core, half, *refs):
+    outs, held, sems = refs[-7:-4], refs[-4:-1], refs[-1]
+    side = (core[0] + 1) & 1 if other else core[0]
+    width = held[0].shape[1]
+    pieces = width // LANES
+    depth = half.shape[0] // pieces
+    at = 0
+    copies = []
+    for i, index in enumerate((1, 2, 0)):
+        size = held[index].shape[0]
+        for piece in range(pieces):
+            part = slice(piece * depth + at, piece * depth + at + size)
+            held[index][:, piece * LANES : (piece + 1) * LANES] = half[part, :].astype(F32) * factors[i & 1]
+        at += size
+        target = outs[index].at[:, pl.ds(pl.multiple_of(side * width, width), width)]
+        copies.append(pltpu.make_async_copy(held[index], target, sems.at[index]))
+        copies[-1].start()
+    for copy in copies:
+        copy.wait()
 
 
 def phase_tables():
@@ -279,17 +275,25 @@
     prev = neighbour(outgoing, devices, 1)
     following = neighbour(outgoing, devices, -1)
 
-    state, pair, to_prev, to_next = local_kernel(
+    pair, coeffs, to_prev, to_next = local_kernel(
         mix_body,
-        [shape((LON, code), BF16), shape((4 * MODES, code), BF16), shape(modes, BF16), shape(modes, BF16)],
-        2 * LON * code * (4 * MODES + slots),
-        8 * LON * code,
-        spectrum, prev, following, w_spec, north, south, w_mix, weight, table_t, table, onehot, latent, cotangent,
-        hbm_out=(1,),
+        [shape((4 * MODES, code), BF16), shape(modes, BF16), shape(modes, BF16), shape(modes, BF16)],
+        2 * LON * code * 4 * MODES,
+        6 * LON * code,
+        spectrum, prev, following, w_spec, north, south, w_mix, weight, table_t, table, cotangent,
         room=12,
+    )
+    state = local_kernel(
+        state_body,
+        shape((LON, code), BF16),
+        2 * LON * code * (2 * MODES + slots),
+        6 * LON * code,
+        table_t, coeffs, onehot, latent,
+        room=8,
     )
     from_next = neighbour(to_prev, devices, -1)
     from_prev = neighbour(to_next, devices, 1)
+    state, pair = lax.optimization_barrier((state, pair))
     depth = hid + code + channels
     sent, mine, kept = local_kernel(
         back_body,
@@ -298,8 +302,7 @@
         6 * slots * code,
         core_arg, from_next, from_prev, share, pair, w_mix, w_spec, rows, w_in, slot_modes, slot_cot, w_out,
         smem=(0,),
-        hbm=(4, 5, 6, 7, 8, 9, 10, 11),
-        room=16,
+        room=12,
     )
     got = lax.ppermute(sent, "blk", swap)
     chunk = 2 * depth // encs
@@ -316,25 +319,34 @@
         parts,
     )
     parts = all_swap(parts, "blk", columns)
-    spread, observation_slope = local_kernel(
-        gather_body,
-        [shape((encs, chunk, LANES), BF16), shape((slots, LANES), BF16)],
-        10 * depth * LANES,
-        8 * depth * LANES,
+    spread = local_kernel(
+        functools.partial(spread_body, more), shape((encs, chunk, LANES), BF16), 10 * depth * LANES, 8 * depth * LANES, parts
+    )
+    observation_slope = local_kernel(
+        functools.partial(return_body, encs),
+        shape((slots, LANES), BF16),
+        2 * slots * slots * LANES,
+        4 * slots * LANES,
         core_arg, parts,
         smem=(0,),
     )
     whole = all_swap(spread, "enc").reshape(2 * depth, LANES)
     theirs = lax.ppermute(whole, "blk", swap)
     factors = jnp.array([1.0 / math.sqrt(devices * slots), 1.0 / math.sqrt(devices * LON)], F32)
-    entry, exit_, blend = local_kernel(
-        final_body,
-        [shape((channels, hid), F32), shape((hid, code), F32), shape((code, code), F32)],
-        4 * depth * code,
-        6 * depth * code,
-        factors, core_arg, whole, theirs,
-        smem=(0, 1),
-    )
+    sizes = ((channels, hid), (hid, code), (code, code))
+    outs = []
+    for other, half_rows in ((False, whole), (True, theirs)):
+        outs = local_kernel(
+            functools.partial(final_body, other),
+            [shape(dims, F32) for dims in sizes],
+            2 * depth * code,
+            4 * depth * code,
+            factors, core_arg, half_rows, *outs,
+            smem=(0, 1),
+            held=[(dims[0], dims[1] // 2) for dims in sizes],
+            aliases={3 + i: i for i in range(len(outs))},
+        )
+    entry, exit_, blend = outs
     return state[None], entry, exit_, blend, observation_slope
 
 

time: 128 us -> 119 us (0.930)
  waiting for transfers between devices: 19.3 us -> 13 us
  blocking collectives: 57.7 us -> 54.3 us
    ppermute x4, waiting for transfers between devices: 7.37 us -> 2.65 us  [neighbour(): return lax.ppermute(value, BOTH, pairs)]
    all_to_all x3, blocking collectives: 57.7 us -> 54.3 us  [all_swap(): lax.all_to_all(blocks, axis, split_axis=0, concat_axis=0, tiled=True, axi...]
    ppermute x1, waiting for transfers between devices: 1.63 us -> 0.01 us  [shards(): theirs = lax.ppermute(whole, 'blk', swap)]
    pallas_call x6 -> x9, Pallas kernels: 11.4 us -> 11.8 us  [local_kernel(): pl.pallas_call(body, out_shape=out_shape, in_specs=in_specs, out_specs=ou...]
  transfers between devices with their start and end apart: 7 -> 7, of which waited for: 7 -> 4; matrix products, arithmetic and copies ran while one was open for 5% -> 5% of each run, Pallas kernels for 0% -> 4%
where the time goes in v4:
time: 119 us
  blocking collectives  54.3 us (46%)
  starting transfers between devices  31.6 us (27%)
  waiting for transfers between devices  13 us (11%)
  Pallas kernels  11.8 us (10%)
  matrix products  3.81 us (3%)
  other arithmetic  3.05 us (3%)
    all_to_all x3, blocking collectives, all_swap(): lax.all_to_all(blocks, axis, split_axis=0, concat_axis=0, tiled=True, axi...  54.3 us
    all_to_all x1, starting transfers between devices, all_swap(): lax.all_to_all(blocks, axis, split_axis=0, concat_axis=0, tiled=True, axi...  15.7 us
    ppermute x4, starting transfers between devices, neighbour(): return lax.ppermute(value, BOTH, pairs)  12 us
    pallas_call x9, Pallas kernels, local_kernel(): pl.pallas_call(body, out_shape=out_shape, in_specs=in_specs, out_specs=ou...  11.8 us
    all_to_all x1, waiting for transfers between devices, all_swap(): lax.all_to_all(blocks, axis, split_axis=0, concat_axis=0, tiled=True, axi...  8.23 us
    ppermute x1, starting transfers between devices, shards(): theirs = lax.ppermute(whole, 'blk', swap)  3.86 us
    dot_general x3, matrix products, dot(): return jnp.dot(a, b, preferred_element_type=F32)  2.78 us
    ppermute x4, waiting for transfers between devices, neighbour(): return lax.ppermute(value, BOTH, pairs)  2.65 us
  transfers between devices with their start and end apart: 7, of which 4 were waited for; matrix products, arithmetic and copies ran while one was open for 5% of the time, Pallas kernels for 4%

profile of v4, /device:TPU:1, one launch (start us, length us, event | category | flops | bytes accessed | tf_op | source)
XLA Modules:
  0.0 118.8 jit_solution(1942628223536148258)
XLA Ops:
  0.6 15.7 %all-to-all-start = ((bf16[256,2,128]{2,1,0:T(2,128)(2,1)}), bf16[256,2,128]{2,1,0:T(2,128)(2,1)S(1)}, u32[]{:S(2)}, u32[]{:S(2)}) async-start(bf16[256,2,128]{2,1,0:T(2,128)(2,1)} %bitcast.25), calls=%async_computation | async-start | bytes 262144 | tf_op jit(solution)/shard_map/all_to_all | solution.py:238
  16.3 0.8 iota_compare_fusion.7
  17.1 0.1 lt.29
  17.3 0.7 broadcast_select_fusion
  17.9 0.9 convert_reduce_fusion
  18.9 0.1 copy.26.share
  19.1 1.9 %fusion.7 = bf16[512,256]{0,1:T(8,128)(2,1)S(1)} fusion(bf16[256,1440]{1,0:T(8,128)(2,1)} %constant.33.clone.table, s32[512]{0:T(512)S(1)} %broadcast_select_fusion), kind=kOutput, calls=%fused_computation.9 | convolution fusion | flops 378355712 | bytes 1001472 | tf_op jit(solution)/shard_map/dot_general | solution.py:23
  20.9 8.2 %all-to-all-done = bf16[256,2,128]{2,1,0:T(2,128)(2,1)S(1)} async-done(((bf16[256,2,128]{2,1,0:T(2,128)(2,1)}), bf16[256,2,128]{2,1,0:T(2,128)(2,1)S(1)}, u32[]{:S(2)}, u32[]{:S(2)}) %all-to-all-start) | async-done | bytes 131104 | tf_op jit(solution)/shard_map/all_to_all | solution.py:238
  29.2 0.6 fusion.6.latent
  29.9 0.3 fusion.11
  30.2 2.9 %collective-permute-start.1 = (bf16[256,512]{1,0:T(8,128)(2,1)S(1)}, bf16[256,512]{1,0:T(8,128)(2,1)S(1)}, u32[]{:S(2)}, u32[]{:S(2)}) collective-permute-start(bf16[256,512]{1,0:T(8,128)(2,1)S(1)} %get-tuple-element.39), channel_id=1, source_target_pairs={{1,0},{2,1},{3,2},{4,3},{5,4},{6,5},{7,6},{8,7},{9,8},{10,9},{11,1... | collective-permute-start | bytes 786440 | tf_op jit(solution)/shard_map/ppermute | solution.py:234
  33.1 2.8 %collective-permute-start = (bf16[256,512]{1,0:T(8,128)(2,1)S(1)}, bf16[256,512]{1,0:T(8,128)(2,1)S(1)}, u32[]{:S(2)}, u32[]{:S(2)}) collective-permute-start(bf16[256,512]{1,0:T(8,128)(2,1)S(1)} %get-tuple-element.39), channel_id=1, source_target_pairs={{0,1},{1,2},{2,3},{3,4},{4,5},{5,6},{6,7},{7,8},{8,9},{9,10},{10,1... | collective-permute-start | bytes 786440 | tf_op jit(solution)/shard_map/ppermute | solution.py:234
  35.9 0.6 fusion.1.onehot
  36.5 1.5 %collective-permute-done.1.following = bf16[256,512]{1,0:T(8,128)(2,1)S(1)} collective-permute-done((bf16[256,512]{1,0:T(8,128)(2,1)S(1)}, bf16[256,512]{1,0:T(8,128)(2,1)S(1)}, u32[]{:S(2)}, u32[]{:S(2)}) %collective-permute-start.1) | collective-permute-done | bytes 262176 | tf_op jit(solution)/shard_map/ppermute | solution.py:234
  38.0 1.2 collective-permute-done.prev
  39.2 2.5 %shard_map.173 = (bf16[512,512]{1,0:T(8,128)(2,1)S(1)}, bf16[256,512]{1,0:T(8,128)(2,1)S(1)}, bf16[256,512]{1,0:T(8,128)(2,1)S(1)}, bf16[256,512]{1,0:T(8,128)(2,1)S(1)}) custom-call(f32[256,512]{1,0:T(8,128)S(1)} %get-tuple-element.40.spectrum, bf16[256,512]{1,0:T(8,128)(2,1)S(1)} %collective-permute-done.prev, ...), custom_call_target="tpu_custom_call" | custom-call | flops 754974720 | bytes 4423680 | tf_op jit(solution)/shard_map/pallas_call | solution.py:46
  41.8 1.9 %collective-permute-start.2 = (bf16[256,512]{1,0:T(8,128)(2,1)S(1)}, bf16[256,512]{1,0:T(8,128)(2,1)S(1)}, u32[]{:S(2)}, u32[]{:S(2)}) collective-permute-start(bf16[256,512]{1,0:T(8,128)(2,1)S(1)} %get-tuple-element.27), channel_id=1, source_target_pairs={{1,0},{2,1},{3,2},{4,3},{5,4},{6,5},{7,6},{8,7},{9,8},{10,9},{11,1... | collective-permute-start | bytes 786440 | tf_op jit(solution)/shard_map/ppermute | solution.py:234
  43.7 4.4 %collective-permute-start.3 = (bf16[256,512]{1,0:T(8,128)(2,1)S(1)}, bf16[256,512]{1,0:T(8,128)(2,1)S(1)}, u32[]{:S(2)}, u32[]{:S(2)}) collective-permute-start(bf16[256,512]{1,0:T(8,128)(2,1)S(1)} %get-tuple-element.28), channel_id=1, source_target_pairs={{0,1},{1,2},{2,3},{3,4},{4,5},{5,6},{6,7},{7,8},{8,9},{9,10},{10,1... | collective-permute-start | bytes 786440 | tf_op jit(solution)/shard_map/ppermute | solution.py:234
  48.1 1.0 fusion.5.slot_cot
  49.1 2.5 %shard_map.174 = bf16[1440,512]{1,0:T(8,128)(2,1)} custom-call(bf16[1440,256]{1,0:T(8,128)(2,1)S(1)} %copy-done, bf16[256,512]{1,0:T(8,128)(2,1)S(1)} %get-tuple-element.23.coeffs, bf16[1440,512]{1,0:T(8,128)(2,1)S(1)} %fusion.1.onehot, bf16[512,512]{1,0:T(8,128)(2,1)S(1)} %fusion.6.latent), custom_call_target="tpu_custom_call" | custom-call | flops 1132462080 | bytes 4423680 | tf_op jit(solution)/shard_map/pallas_call | solution.py:46
  51.6 2.1 %shard_map.175 = (bf16[2560,128]{1,0:T(8,128)(2,1)S(1)}, f32[2304,128]{1,0:T(8,128)S(1)}, bf16[256,128]{1,0:T(8,128)(2,1)S(1)}) custom-call(s32[1]{0:T(128)} %bitcast.2.core, bf16[256,512]{1,0:T(8,128)(2,1)S(1)} %collective-permute-done.2.from_next, bf16[256,512]{1,0:T(8,128)(2,1)S(1)} %collective-permute-done.3.from_prev, f32[512,1]{1,0:T(8,128)S(1)} %copy.26.share, ...), custom_call_target="tpu_custom_call" | custom-call | flops 786432000 | bytes 1572864 | tf_op jit(solution)/shard_map/pallas_call | solution.py:46
  53.7 0.1 collective-permute-start.4
  53.8 2.1 %collective-permute-done.4.got = bf16[2560,128]{1,0:T(8,128)(2,1)S(1)} collective-permute-done((bf16[2560,128]{1,0:T(8,128)(2,1)S(1)}, bf16[2560,128]{1,0:T(8,128)(2,1)S(1)}, u32[]{:S(2)}, u32[]{:S(2)}) %collective-permute-start.4) | collective-permute-done | bytes 655392 | tf_op jit(solution)/shard_map/ppermute | solution.py:307
  55.9 0.1 shard_map.176
  56.0 25.1 %all_to_all.20.got = bf16[16,176,128]{2,1,0:T(8,128)(2,1)S(1)} all-to-all(bf16[16,176,128]{2,1,0:T(8,128)(2,1)S(1)} %shard_map.176), channel_id=1, replica_groups=mesh['enc'=16,'blk'=16] {'enc'}, dimensions={0} | all-to-all | bytes 1441792 | tf_op jit(solution)/shard_map/all_to_all | solution.py:238
  81.2 0.3 shard_map.177
  81.5 15.2 %all_to_all.21.got = bf16[8,208,128]{2,1,0:T(8,128)(2,1)S(1)} all-to-all(bf16[8,208,128]{2,1,0:T(8,128)(2,1)S(1)} %shard_map.177), channel_id=1, replica_groups={{0,2,4,6,8,10,12,14},{1,3,5,7,9,11,13,15},{16,18,20,22,24,26,28,30},{17..., dimensions={0} | all-to-all | bytes 851968 | tf_op jit(solution)/shard_map/all_to_all | solution.py:238
  96.8 13.9 %all_to_all.22 = bf16[16,144,128]{2,1,0:T(8,128)(2,1)S(1)} all-to-all(bf16[16,144,128]{2,1,0:T(8,128)(2,1)S(1)} %shard_map.178), channel_id=1, replica_groups=mesh['enc'=16,'blk'=16] {'enc'}, dimensions={0} | all-to-all | bytes 1179648 | tf_op jit(solution)/shard_map/all_to_all | solution.py:238
  110.7 3.9 %collective-permute-start.5 = (bf16[2304,128]{1,0:T(8,128)(2,1)S(1)}, bf16[2304,128]{1,0:T(8,128)(2,1)S(1)}, u32[]{:S(2)}, u32[]{:S(2)}) collective-permute-start(bf16[2304,128]{1,0:T(8,128)(2,1)S(1)} %bitcast.18), channel_id=1, source_target_pairs={{0,1},{1,0},{2,3},{3,2},{4,5},{5,4},{6,7},{7,6},{8,9},{9,8},{10,11... | collective-permute-start | bytes 1769480 | tf_op jit(solution)/shard_map/ppermute | solution.py:334
  114.5 1.0 shard_map.181
  115.5 1.6 %shard_map.179 = (f32[128,512]{1,0:T(8,128)}, f32[512,512]{1,0:T(8,128)}, f32[512,512]{1,0:T(8,128)}) custom-call(f32[2]{0:T(128)S(1)} %copy-done.10, s32[1]{0:T(128)} %bitcast.2.core, bf16[2304,128]{1,0:T(8,128)(2,1)S(1)} %bitcast.19), custom_call_target="tpu_custom_call" | custom-call | flops 1179648 | bytes 2359296 | tf_op jit(solution)/shard_map/pallas_call | solution.py:46
  117.1 1.6 %shard_map.180 = (f32[128,512]{1,0:T(8,128)}, f32[512,512]{1,0:T(8,128)}, f32[512,512]{1,0:T(8,128)}) custom-call(f32[2]{0:T(128)S(1)} %copy-done.10, s32[1]{0:T(128)} %bitcast.2.core, bf16[2304,128]{1,0:T(8,128)(2,1)S(1)} %collective-permute-done.5.half, ...), custom_call_target="tpu_custom_call", output_to_operand_aliasing={{0}: (3, {}), {1}: (4, {}), {2}: (5, {})} | custom-call | flops 1179648 | bytes 2359296 | tf_op jit(solution)/shard_map/pallas_call | solution.py:46
  (27 shorter events, 0.1 us)
Async XLA Ops:
  0.6 28.5 %all-to-all-start = ((bf16[256,2,128]{2,1,0:T(2,128)(2,1)}), bf16[256,2,128]{2,1,0:T(2,128)(2,1)S(1)}, u32[]{:S(2)}, u32[]{:S(2)}) async-start(bf16[256,2,128]{2,1,0:T(2,128)(2,1)} %bitcast.25), calls=%async_computation | async-start | bytes 262144 | tf_op jit(solution)/shard_map/all_to_all | solution.py:238
  18.9 10.3 %copy-start.5 = (bf16[512,512]{1,0:T(8,128)(2,1)S(1)}, bf16[512,512]{1,0:T(8,128)(2,1)}, u32[]{:S(2)}) copy-start(bf16[512,512]{1,0:T(8,128)(2,1)} %w_out.1) | copy-start | bytes 1572868
  18.9 10.3 %copy-start.6 = (bf16[128,512]{1,0:T(8,128)(2,1)S(1)}, bf16[128,512]{1,0:T(8,128)(2,1)}, u32[]{:S(2)}) copy-start(bf16[128,512]{1,0:T(8,128)(2,1)} %w_in.1) | copy-start | bytes 393220
  29.2 10.0 %copy-start.3 = (bf16[1,1440,512]{2,1,0:T(8,128)(2,1)S(1)}, bf16[1,1440,512]{2,1,0:T(8,128)(2,1)}, u32[]{:S(2)}) copy-start(bf16[1,1440,512]{2,1,0:T(8,128)(2,1)} %param.23) | copy-start | bytes 4423684
  29.8 9.4 %copy-start = (bf16[1440,256]{1,0:T(8,128)(2,1)S(1)}, bf16[1440,256]{1,0:T(8,128)(2,1)}, u32[]{:S(2)}) copy-start(bf16[1440,256]{1,0:T(8,128)(2,1)} %constant.34.clone.table_t) | copy-start | bytes 2211844
  29.8 9.4 %copy-start.1 = (f32[256,512]{1,0:T(8,128)S(1)}, f32[256,512]{1,0:T(8,128)}, u32[]{:S(2)}) copy-start(f32[256,512]{1,0:T(8,128)} %w_spec.3) | copy-start | bytes 1572868
  29.8 9.4 %copy-start.2 = (bf16[512,512]{1,0:T(8,128)(2,1)S(1)}, bf16[512,512]{1,0:T(8,128)(2,1)}, u32[]{:S(2)}) copy-start(bf16[512,512]{1,0:T(8,128)(2,1)} %w_mix.3) | copy-start | bytes 1572868
  29.8 9.4 %copy-start.4 = (bf16[256,1440]{1,0:T(8,128)(2,1)S(1)}, bf16[256,1440]{1,0:T(8,128)(2,1)}, u32[]{:S(2)}) copy-start(bf16[256,1440]{1,0:T(8,128)(2,1)} %constant.33.clone.table) | copy-start | bytes 2211844
  29.8 9.4 %copy-start.7 = (f32[256,1]{1,0:T(8,128)S(1)}, f32[256,1]{1,0:T(8,128)}, u32[]{:S(2)}) copy-start(f32[256,1]{1,0:T(8,128)} %constant.35.clone.weight) | copy-start | bytes 3076
  29.8 9.4 %copy-start.8 = (f32[1,512]{1,0:T(1,128)S(1)}, f32[1,512]{1,0:T(1,128)}, u32[]{:S(2)}) copy-start(f32[1,512]{1,0:T(1,128)} %north.1) | copy-start | bytes 6148
  29.9 9.4 %copy-start.9 = (f32[1,512]{1,0:T(1,128)S(1)}, f32[1,512]{1,0:T(1,128)}, u32[]{:S(2)}) copy-start(f32[1,512]{1,0:T(1,128)} %south.1) | copy-start | bytes 6148
  30.2 7.8 %collective-permute-start.1 = (bf16[256,512]{1,0:T(8,128)(2,1)S(1)}, bf16[256,512]{1,0:T(8,128)(2,1)S(1)}, u32[]{:S(2)}, u32[]{:S(2)}) collective-permute-start(bf16[256,512]{1,0:T(8,128)(2,1)S(1)} %get-tuple-element.39), channel_id=1, source_target_pairs={{1,0},{2,1},{3,2},{4,3},{5,4},{6,5},{7,6},{8,7},{9,8},{10,9},{11,1... | collective-permute-start | bytes 786440 | tf_op jit(solution)/shard_map/ppermute | solution.py:234
  33.1 6.1 %collective-permute-start = (bf16[256,512]{1,0:T(8,128)(2,1)S(1)}, bf16[256,512]{1,0:T(8,128)(2,1)S(1)}, u32[]{:S(2)}, u32[]{:S(2)}) collective-permute-start(bf16[256,512]{1,0:T(8,128)(2,1)S(1)} %get-tuple-element.39), channel_id=1, source_target_pairs={{0,1},{1,2},{2,3},{3,4},{4,5},{5,6},{6,7},{7,8},{8,9},{9,10},{10,1... | collective-permute-start | bytes 786440 | tf_op jit(solution)/shard_map/ppermute | solution.py:234
  41.8 9.9 %collective-permute-start.2 = (bf16[256,512]{1,0:T(8,128)(2,1)S(1)}, bf16[256,512]{1,0:T(8,128)(2,1)S(1)}, u32[]{:S(2)}, u32[]{:S(2)}) collective-permute-start(bf16[256,512]{1,0:T(8,128)(2,1)S(1)} %get-tuple-element.27), channel_id=1, source_target_pairs={{1,0},{2,1},{3,2},{4,3},{5,4},{6,5},{7,6},{8,7},{9,8},{10,9},{11,1... | collective-permute-start | bytes 786440 | tf_op jit(solution)/shard_map/ppermute | solution.py:234
  43.7 8.0 %collective-permute-start.3 = (bf16[256,512]{1,0:T(8,128)(2,1)S(1)}, bf16[256,512]{1,0:T(8,128)(2,1)S(1)}, u32[]{:S(2)}, u32[]{:S(2)}) collective-permute-start(bf16[256,512]{1,0:T(8,128)(2,1)S(1)} %get-tuple-element.28), channel_id=1, source_target_pairs={{0,1},{1,2},{2,3},{3,4},{4,5},{5,6},{6,7},{7,8},{8,9},{9,10},{10,1... | collective-permute-start | bytes 786440 | tf_op jit(solution)/shard_map/ppermute | solution.py:234
  53.7 2.2 %collective-permute-start.4 = (bf16[2560,128]{1,0:T(8,128)(2,1)S(1)}, bf16[2560,128]{1,0:T(8,128)(2,1)S(1)}, u32[]{:S(2)}, u32[]{:S(2)}) collective-permute-start(bf16[2560,128]{1,0:T(8,128)(2,1)S(1)} %get-tuple-element.32), channel_id=1, source_target_pairs={{0,1},{1,0},{2,3},{3,2},{4,5},{5,4},{6,7},{7,6},{8,9},{9,8},{10,11... | collective-permute-start | bytes 1966088 | tf_op jit(solution)/shard_map/ppermute | solution.py:307
  96.7 18.8 %copy-start.10 = (f32[2]{0:T(128)S(1)}, f32[2]{0:T(128)}, u32[]{:S(2)}) copy-start(f32[2]{0:T(128)} %constant.36.clone.factors) | copy-start | bytes 28
  110.7 6.5 %collective-permute-start.5 = (bf16[2304,128]{1,0:T(8,128)(2,1)S(1)}, bf16[2304,128]{1,0:T(8,128)(2,1)S(1)}, u32[]{:S(2)}, u32[]{:S(2)}) collective-permute-start(bf16[2304,128]{1,0:T(8,128)(2,1)S(1)} %bitcast.18), channel_id=1, source_target_pairs={{0,1},{1,0},{2,3},{3,2},{4,5},{5,4},{6,7},{7,6},{8,9},{9,8},{10,11... | collective-permute-start | bytes 1769480 | tf_op jit(solution)/shard_map/ppermute | solution.py:334

commit v5 on v4

--- a/solution.py
+++ b/solution.py
@@ -70,13 +70,15 @@
 
 
 def mix_body(
-    spectrum, prev, following, w_spec, north, south, w_mix, weight, table_t, table, cotangent,
-    pair, coeffs_out, to_prev, to_next,
+    core, spectrum, inside, beyond, w_spec, north, south, w_mix, weight, table_t, table, cotangent,
+    pair, coeffs_out, to_beyond, to_inside,
 ):
-    north_row, south_row = north[...], south[...]
+    first = core[0] == 0
+    near_row = jnp.where(first, south[...], north[...])
+    far_row = jnp.where(first, north[...], south[...])
     scale = weight[...]
     mix = (
-        spectrum[...] * w_spec[...] + north_row * prev[...].astype(F32) + south_row * following[...].astype(F32)
+        spectrum[...] * w_spec[...] + near_row * inside[...].astype(F32) + far_row * beyond[...].astype(F32)
     ).astype(BF16)
     pair[: mix.shape[0], :] = mix
     coeffs = (dot(mix, w_mix[...]) * scale).astype(BF16)
@@ -92,8 +94,8 @@
     grad_coeffs = (total * scale).astype(BF16)
     pair[mix.shape[0] :, :] = grad_coeffs
     grad_mix = dot_tb(grad_coeffs, w_mix[...])
-    to_prev[...] = (north_row * grad_mix).astype(BF16)
-    to_next[...] = (south_row * grad_mix).astype(BF16)
+    to_beyond[...] = (far_row * grad_mix).astype(BF16)
+    to_inside[...] = (near_row * grad_mix).astype(BF16)
 
 
 def state_body(table_t, coeffs, onehot, latent, state):
@@ -104,14 +106,14 @@
 
 
 def back_body(
-    core, from_next, from_prev, share, pair, w_mix, w_spec, rows, w_in, slot_modes, slot_cot, w_out,
+    core, from_beyond, from_inside, share, pair, w_mix, w_spec, rows, w_in, slot_modes, slot_cot, w_out,
     sent, mine, kept,
 ):
     first = core[0] == 0
     count = pair.shape[0] // 2
     mix, coeffs = pair[:count, :], pair[count:, :]
     grad_mix = dot_tb(coeffs, w_mix[...])
-    grad_spec = (w_spec[...] * grad_mix + from_next[...].astype(F32) + from_prev[...].astype(F32)).astype(BF16)
+    grad_spec = (w_spec[...] * grad_mix + from_inside[...].astype(F32) + from_beyond[...].astype(F32)).astype(BF16)
     pre1 = dot(rows[...], w_in[...])
     gate = logistic(pre1)
     hidden = (pre1 * gate).astype(BF16)
@@ -229,9 +231,11 @@
     return jnp.asarray(table, BF16), jnp.asarray(np.ascontiguousarray(table.T), BF16)
 
 
-def neighbour(value, count, step):
-    pairs = [(i, i + step) for i in range(count) if 0 <= i + step < count]
-    return lax.ppermute(value, BOTH, pairs)
+def trade(near, far, count):
+    links = [(i, i + 1) for i in range(1, count - 1, 2)]
+    beyond = lax.ppermute(far, BOTH, links + [(j, i) for i, j in links])
+    inside = lax.ppermute(near, BOTH, [(i, i ^ 1) for i in range(count)])
+    return inside, beyond
 
 
 def all_swap(blocks, axis, groups=None):
@@ -272,15 +276,15 @@
     latent = (dot(hidden, w_out) * share).astype(BF16)
     spectrum = dot(slot_modes, latent)
     outgoing = spectrum.astype(BF16)
-    prev = neighbour(outgoing, devices, 1)
-    following = neighbour(outgoing, devices, -1)
-
-    pair, coeffs, to_prev, to_next = local_kernel(
+    inside, beyond = trade(outgoing, outgoing, devices)
+
+    pair, coeffs, to_beyond, to_inside = local_kernel(
         mix_body,
         [shape((4 * MODES, code), BF16), shape(modes, BF16), shape(modes, BF16), shape(modes, BF16)],
         2 * LON * code * 4 * MODES,
         6 * LON * code,
-        spectrum, prev, following, w_spec, north, south, w_mix, weight, table_t, table, cotangent,
+        core_arg, spectrum, inside, beyond, w_spec, north, south, w_mix, weight, table_t, table, cotangent,
+        smem=(0,),
         room=12,
     )
     state = local_kernel(
@@ -291,8 +295,7 @@
         table_t, coeffs, onehot, latent,
         room=8,
     )
-    from_next = neighbour(to_prev, devices, -1)
-    from_prev = neighbour(to_next, devices, 1)
+    from_inside, from_beyond = trade(to_inside, to_beyond, devices)
     state, pair = lax.optimization_barrier((state, pair))
     depth = hid + code + channels
     sent, mine, kept = local_kernel(
@@ -300,7 +303,7 @@
         [shape((2 * depth + half, LANES), BF16), shape((2 * depth, LANES), F32), shape((half, LANES), BF16)],
         2 * slots * code * 1500,
         6 * slots * code,
-        core_arg, from_next, from_prev, share, pair, w_mix, w_spec, rows, w_in, slot_modes, slot_cot, w_out,
+        core_arg, from_beyond, from_inside, share, pair, w_mix, w_spec, rows, w_in, slot_modes, slot_cot, w_out,
         smem=(0,),
         room=12,
     )

time: 119 us -> 114 us (0.958)
  starting transfers between devices: 31.6 us -> 26.9 us
  blocking collectives: 54.3 us -> 52.6 us
  waiting for transfers between devices: 13 us -> 14.3 us
    ppermute x4, starting transfers between devices: 12 us -> 7.32 us  [the longest x2 7.14 us: trade(): beyond = lax.ppermute(far, BOTH, links + [(j, i) for i, j in links])]
    all_to_all x3, blocking collectives: 54.3 us -> 52.6 us  [all_swap(): lax.all_to_all(blocks, axis, split_axis=0, concat_axis=0, tiled=True, axi...]
    ppermute x4, waiting for transfers between devices: 2.65 us -> 3.98 us  [the longest x2 3.97 us: trade(): beyond = lax.ppermute(far, BOTH, links + [(j, i) for i, j in links])]
where the time goes in v5:
time: 114 us
  blocking collectives  52.6 us (46%)
  starting transfers between devices  26.9 us (24%)
  waiting for transfers between devices  14.3 us (13%)
  Pallas kernels  11.8 us (10%)
  matrix products  3.81 us (3%)
  other arithmetic  3.05 us (3%)
    all_to_all x3, blocking collectives, all_swap(): lax.all_to_all(blocks, axis, split_axis=0, concat_axis=0, tiled=True, axi...  52.6 us
    all_to_all x1, starting transfers between devices, all_swap(): lax.all_to_all(blocks, axis, split_axis=0, concat_axis=0, tiled=True, axi...  15.7 us
    pallas_call x9, Pallas kernels, local_kernel(): pl.pallas_call(body, out_shape=out_shape, in_specs=in_specs, out_specs=ou...  11.8 us
    all_to_all x1, waiting for transfers between devices, all_swap(): lax.all_to_all(blocks, axis, split_axis=0, concat_axis=0, tiled=True, axi...  8.23 us
    ppermute x2, starting transfers between devices, trade(): beyond = lax.ppermute(far, BOTH, links + [(j, i) for i, j in links])  7.14 us
    ppermute x2, waiting for transfers between devices, trade(): beyond = lax.ppermute(far, BOTH, links + [(j, i) for i, j in links])  3.97 us
    ppermute x1, starting transfers between devices, shards(): theirs = lax.ppermute(whole, 'blk', swap)  3.86 us
    dot_general x3, matrix products, dot(): return jnp.dot(a, b, preferred_element_type=F32)  2.78 us
  transfers between devices with their start and end apart: 7, of which 4 were waited for; matrix products, arithmetic and copies ran while one was open for 5% of the time, Pallas kernels for 4%

profile of v5, /device:TPU:1, one launch (start us, length us, event | category | flops | bytes accessed | tf_op | source)
XLA Modules:
  0.0 113.7 jit_solution(16151301691201296934)
XLA Ops:
  0.6 15.7 %all-to-all-start = ((bf16[256,2,128]{2,1,0:T(2,128)(2,1)}), bf16[256,2,128]{2,1,0:T(2,128)(2,1)S(1)}, u32[]{:S(2)}, u32[]{:S(2)}) async-start(bf16[256,2,128]{2,1,0:T(2,128)(2,1)} %bitcast.25), calls=%async_computation | async-start | bytes 262144 | tf_op jit(solution)/shard_map/all_to_all | solution.py:242
  16.3 0.8 iota_compare_fusion.7
  17.1 0.1 lt.29
  17.3 0.7 broadcast_select_fusion
  17.9 0.9 convert_reduce_fusion
  18.9 0.1 copy.26.share
  19.1 1.9 %fusion.7 = bf16[512,256]{0,1:T(8,128)(2,1)S(1)} fusion(bf16[256,1440]{1,0:T(8,128)(2,1)} %constant.33.clone.table, s32[512]{0:T(512)S(1)} %broadcast_select_fusion), kind=kOutput, calls=%fused_computation.9 | convolution fusion | flops 378355712 | bytes 1001472 | tf_op jit(solution)/shard_map/dot_general | solution.py:23
  20.9 8.2 %all-to-all-done = bf16[256,2,128]{2,1,0:T(2,128)(2,1)S(1)} async-done(((bf16[256,2,128]{2,1,0:T(2,128)(2,1)}), bf16[256,2,128]{2,1,0:T(2,128)(2,1)S(1)}, u32[]{:S(2)}, u32[]{:S(2)}) %all-to-all-start) | async-done | bytes 131104 | tf_op jit(solution)/shard_map/all_to_all | solution.py:242
  29.2 0.6 fusion.6.latent
  29.9 0.3 fusion.11
  30.2 3.6 %collective-permute-start.1 = (bf16[256,512]{1,0:T(8,128)(2,1)S(1)}, bf16[256,512]{1,0:T(8,128)(2,1)S(1)}, u32[]{:S(2)}, u32[]{:S(2)}) collective-permute-start(bf16[256,512]{1,0:T(8,128)(2,1)S(1)} %get-tuple-element.39), channel_id=1, source_target_pairs={{1,2},{3,4},{5,6},{7,8},{9,10},{11,12},{13,14},{15,16},{17,18},{19... | collective-permute-start | bytes 786440 | tf_op jit(solution)/shard_map/ppermute | solution.py:236
  33.8 0.1 collective-permute-start
  33.9 0.6 fusion.1.onehot
  34.6 3.4 %collective-permute-done.1.beyond = bf16[256,512]{1,0:T(8,128)(2,1)S(1)} collective-permute-done((bf16[256,512]{1,0:T(8,128)(2,1)S(1)}, bf16[256,512]{1,0:T(8,128)(2,1)S(1)}, u32[]{:S(2)}, u32[]{:S(2)}) %collective-permute-start.1) | collective-permute-done | bytes 262176 | tf_op jit(solution)/shard_map/ppermute | solution.py:236
  38.1 2.5 %shard_map.173 = (bf16[512,512]{1,0:T(8,128)(2,1)S(1)}, bf16[256,512]{1,0:T(8,128)(2,1)S(1)}, bf16[256,512]{1,0:T(8,128)(2,1)S(1)}, bf16[256,512]{1,0:T(8,128)(2,1)S(1)}) custom-call(s32[1]{0:T(128)} %bitcast.2.core, f32[256,512]{1,0:T(8,128)S(1)} %get-tuple-element.40.spectrum, bf16[256,512]{1,0:T(8,128)(2,1)S(1)} %collective-permute-done.inside, ...), custom_call_target="tpu_custom_call" | custom-call | flops 754974720 | bytes 4423680 | tf_op jit(solution)/shard_map/pallas_call | solution.py:46
  40.6 3.5 %collective-permute-start.2 = (bf16[256,512]{1,0:T(8,128)(2,1)S(1)}, bf16[256,512]{1,0:T(8,128)(2,1)S(1)}, u32[]{:S(2)}, u32[]{:S(2)}) collective-permute-start(bf16[256,512]{1,0:T(8,128)(2,1)S(1)} %get-tuple-element.27), channel_id=1, source_target_pairs={{1,2},{3,4},{5,6},{7,8},{9,10},{11,12},{13,14},{15,16},{17,18},{19... | collective-permute-start | bytes 786440 | tf_op jit(solution)/shard_map/ppermute | solution.py:236
  44.1 0.1 collective-permute-start.3
  44.2 1.0 fusion.5.slot_cot
  45.2 2.5 %shard_map.174 = bf16[1440,512]{1,0:T(8,128)(2,1)} custom-call(bf16[1440,256]{1,0:T(8,128)(2,1)S(1)} %copy-done, bf16[256,512]{1,0:T(8,128)(2,1)S(1)} %get-tuple-element.24.coeffs, bf16[1440,512]{1,0:T(8,128)(2,1)S(1)} %fusion.1.onehot, bf16[512,512]{1,0:T(8,128)(2,1)S(1)} %fusion.6.latent), custom_call_target="tpu_custom_call" | custom-call | flops 1132462080 | bytes 4423680 | tf_op jit(solution)/shard_map/pallas_call | solution.py:46
  47.7 0.5 collective-permute-done.2.from_beyond
  48.3 2.1 %shard_map.175 = (bf16[2560,128]{1,0:T(8,128)(2,1)S(1)}, f32[2304,128]{1,0:T(8,128)S(1)}, bf16[256,128]{1,0:T(8,128)(2,1)S(1)}) custom-call(s32[1]{0:T(128)} %bitcast.2.core, bf16[256,512]{1,0:T(8,128)(2,1)S(1)} %collective-permute-done.2.from_beyond, bf16[256,512]{1,0:T(8,128)(2,1)S(1)} %collective-permute-done.3.from_inside, f32[512,1]{1,0:T(8,128)S(1)} %copy.26.share, ...), custom_call_target="tpu_custom_call" | custom-call | flops 786432000 | bytes 1572864 | tf_op jit(solution)/shard_map/pallas_call | solution.py:46
  50.4 0.1 collective-permute-start.4
  50.5 2.1 %collective-permute-done.4.got = bf16[2560,128]{1,0:T(8,128)(2,1)S(1)} collective-permute-done((bf16[2560,128]{1,0:T(8,128)(2,1)S(1)}, bf16[2560,128]{1,0:T(8,128)(2,1)S(1)}, u32[]{:S(2)}, u32[]{:S(2)}) %collective-permute-start.4) | collective-permute-done | bytes 655392 | tf_op jit(solution)/shard_map/ppermute | solution.py:310
  52.6 0.1 shard_map.176
  52.7 23.4 %all_to_all.20.got = bf16[16,176,128]{2,1,0:T(8,128)(2,1)S(1)} all-to-all(bf16[16,176,128]{2,1,0:T(8,128)(2,1)S(1)} %shard_map.176), channel_id=1, replica_groups=mesh['enc'=16,'blk'=16] {'enc'}, dimensions={0} | all-to-all | bytes 1441792 | tf_op jit(solution)/shard_map/all_to_all | solution.py:242
  76.1 0.3 shard_map.177
  76.5 15.2 %all_to_all.21.got = bf16[8,208,128]{2,1,0:T(8,128)(2,1)S(1)} all-to-all(bf16[8,208,128]{2,1,0:T(8,128)(2,1)S(1)} %shard_map.177), channel_id=1, replica_groups={{0,2,4,6,8,10,12,14},{1,3,5,7,9,11,13,15},{16,18,20,22,24,26,28,30},{17..., dimensions={0} | all-to-all | bytes 851968 | tf_op jit(solution)/shard_map/all_to_all | solution.py:242
  91.7 13.9 %all_to_all.22 = bf16[16,144,128]{2,1,0:T(8,128)(2,1)S(1)} all-to-all(bf16[16,144,128]{2,1,0:T(8,128)(2,1)S(1)} %shard_map.178), channel_id=1, replica_groups=mesh['enc'=16,'blk'=16] {'enc'}, dimensions={0} | all-to-all | bytes 1179648 | tf_op jit(solution)/shard_map/all_to_all | solution.py:242
  105.6 3.9 %collective-permute-start.5 = (bf16[2304,128]{1,0:T(8,128)(2,1)S(1)}, bf16[2304,128]{1,0:T(8,128)(2,1)S(1)}, u32[]{:S(2)}, u32[]{:S(2)}) collective-permute-start(bf16[2304,128]{1,0:T(8,128)(2,1)S(1)} %bitcast.18), channel_id=1, source_target_pairs={{0,1},{1,0},{2,3},{3,2},{4,5},{5,4},{6,7},{7,6},{8,9},{9,8},{10,11... | collective-permute-start | bytes 1769480 | tf_op jit(solution)/shard_map/ppermute | solution.py:337
  109.5 1.0 shard_map.181
  110.5 1.6 %shard_map.179 = (f32[128,512]{1,0:T(8,128)}, f32[512,512]{1,0:T(8,128)}, f32[512,512]{1,0:T(8,128)}) custom-call(f32[2]{0:T(128)S(1)} %copy-done.10, s32[1]{0:T(128)} %bitcast.2.core, bf16[2304,128]{1,0:T(8,128)(2,1)S(1)} %bitcast.19), custom_call_target="tpu_custom_call" | custom-call | flops 1179648 | bytes 2359296 | tf_op jit(solution)/shard_map/pallas_call | solution.py:46
  112.1 1.6 %shard_map.180 = (f32[128,512]{1,0:T(8,128)}, f32[512,512]{1,0:T(8,128)}, f32[512,512]{1,0:T(8,128)}) custom-call(f32[2]{0:T(128)S(1)} %copy-done.10, s32[1]{0:T(128)} %bitcast.2.core, bf16[2304,128]{1,0:T(8,128)(2,1)S(1)} %collective-permute-done.5.half, ...), custom_call_target="tpu_custom_call", output_to_operand_aliasing={{0}: (3, {}), {1}: (4, {}), {2}: (5, {})} | custom-call | flops 1179648 | bytes 2359296 | tf_op jit(solution)/shard_map/pallas_call | solution.py:46
  (27 shorter events, 0.1 us)
Async XLA Ops:
  0.6 28.5 %all-to-all-start = ((bf16[256,2,128]{2,1,0:T(2,128)(2,1)}), bf16[256,2,128]{2,1,0:T(2,128)(2,1)S(1)}, u32[]{:S(2)}, u32[]{:S(2)}) async-start(bf16[256,2,128]{2,1,0:T(2,128)(2,1)} %bitcast.25), calls=%async_computation | async-start | bytes 262144 | tf_op jit(solution)/shard_map/all_to_all | solution.py:242
  18.9 10.3 %copy-start.5 = (bf16[512,512]{1,0:T(8,128)(2,1)S(1)}, bf16[512,512]{1,0:T(8,128)(2,1)}, u32[]{:S(2)}) copy-start(bf16[512,512]{1,0:T(8,128)(2,1)} %w_out.1) | copy-start | bytes 1572868
  18.9 10.3 %copy-start.6 = (bf16[128,512]{1,0:T(8,128)(2,1)S(1)}, bf16[128,512]{1,0:T(8,128)(2,1)}, u32[]{:S(2)}) copy-start(bf16[128,512]{1,0:T(8,128)(2,1)} %w_in.1) | copy-start | bytes 393220
  29.2 8.8 %copy-start.3 = (bf16[1,1440,512]{2,1,0:T(8,128)(2,1)S(1)}, bf16[1,1440,512]{2,1,0:T(8,128)(2,1)}, u32[]{:S(2)}) copy-start(bf16[1,1440,512]{2,1,0:T(8,128)(2,1)} %param.23) | copy-start | bytes 4423684
  29.8 8.2 %copy-start = (bf16[1440,256]{1,0:T(8,128)(2,1)S(1)}, bf16[1440,256]{1,0:T(8,128)(2,1)}, u32[]{:S(2)}) copy-start(bf16[1440,256]{1,0:T(8,128)(2,1)} %constant.34.clone.table_t) | copy-start | bytes 2211844
  29.8 8.2 %copy-start.1 = (f32[256,512]{1,0:T(8,128)S(1)}, f32[256,512]{1,0:T(8,128)}, u32[]{:S(2)}) copy-start(f32[256,512]{1,0:T(8,128)} %w_spec.3) | copy-start | bytes 1572868
  29.8 8.2 %copy-start.2 = (bf16[512,512]{1,0:T(8,128)(2,1)S(1)}, bf16[512,512]{1,0:T(8,128)(2,1)}, u32[]{:S(2)}) copy-start(bf16[512,512]{1,0:T(8,128)(2,1)} %w_mix.3) | copy-start | bytes 1572868
  29.8 8.2 %copy-start.4 = (bf16[256,1440]{1,0:T(8,128)(2,1)S(1)}, bf16[256,1440]{1,0:T(8,128)(2,1)}, u32[]{:S(2)}) copy-start(bf16[256,1440]{1,0:T(8,128)(2,1)} %constant.33.clone.table) | copy-start | bytes 2211844
  29.8 8.2 %copy-start.7 = (f32[256,1]{1,0:T(8,128)S(1)}, f32[256,1]{1,0:T(8,128)}, u32[]{:S(2)}) copy-start(f32[256,1]{1,0:T(8,128)} %constant.35.clone.weight) | copy-start | bytes 3076
  29.8 8.2 %copy-start.8 = (f32[1,512]{1,0:T(1,128)S(1)}, f32[1,512]{1,0:T(1,128)}, u32[]{:S(2)}) copy-start(f32[1,512]{1,0:T(1,128)} %north.1) | copy-start | bytes 6148
  29.9 8.2 %copy-start.9 = (f32[1,512]{1,0:T(1,128)S(1)}, f32[1,512]{1,0:T(1,128)}, u32[]{:S(2)}) copy-start(f32[1,512]{1,0:T(1,128)} %south.1) | copy-start | bytes 6148
  30.2 7.8 %collective-permute-start.1 = (bf16[256,512]{1,0:T(8,128)(2,1)S(1)}, bf16[256,512]{1,0:T(8,128)(2,1)S(1)}, u32[]{:S(2)}, u32[]{:S(2)}) collective-permute-start(bf16[256,512]{1,0:T(8,128)(2,1)S(1)} %get-tuple-element.39), channel_id=1, source_target_pairs={{1,2},{3,4},{5,6},{7,8},{9,10},{11,12},{13,14},{15,16},{17,18},{19... | collective-permute-start | bytes 786440 | tf_op jit(solution)/shard_map/ppermute | solution.py:236
  33.8 4.2 %collective-permute-start = (bf16[256,512]{1,0:T(8,128)(2,1)S(1)}, bf16[256,512]{1,0:T(8,128)(2,1)S(1)}, u32[]{:S(2)}, u32[]{:S(2)}) collective-permute-start(bf16[256,512]{1,0:T(8,128)(2,1)S(1)} %get-tuple-element.39), channel_id=1, source_target_pairs={{0,1},{1,0},{2,3},{3,2},{4,5},{5,4},{6,7},{7,6},{8,9},{9,8},{10,11... | collective-permute-start | bytes 786440 | tf_op jit(solution)/shard_map/ppermute | solution.py:237
  40.6 7.7 %collective-permute-start.2 = (bf16[256,512]{1,0:T(8,128)(2,1)S(1)}, bf16[256,512]{1,0:T(8,128)(2,1)S(1)}, u32[]{:S(2)}, u32[]{:S(2)}) collective-permute-start(bf16[256,512]{1,0:T(8,128)(2,1)S(1)} %get-tuple-element.27), channel_id=1, source_target_pairs={{1,2},{3,4},{5,6},{7,8},{9,10},{11,12},{13,14},{15,16},{17,18},{19... | collective-permute-start | bytes 786440 | tf_op jit(solution)/shard_map/ppermute | solution.py:236
  44.1 4.2 %collective-permute-start.3 = (bf16[256,512]{1,0:T(8,128)(2,1)S(1)}, bf16[256,512]{1,0:T(8,128)(2,1)S(1)}, u32[]{:S(2)}, u32[]{:S(2)}) collective-permute-start(bf16[256,512]{1,0:T(8,128)(2,1)S(1)} %get-tuple-element.28), channel_id=1, source_target_pairs={{0,1},{1,0},{2,3},{3,2},{4,5},{5,4},{6,7},{7,6},{8,9},{9,8},{10,11... | collective-permute-start | bytes 786440 | tf_op jit(solution)/shard_map/ppermute | solution.py:237
  50.4 2.2 %collective-permute-start.4 = (bf16[2560,128]{1,0:T(8,128)(2,1)S(1)}, bf16[2560,128]{1,0:T(8,128)(2,1)S(1)}, u32[]{:S(2)}, u32[]{:S(2)}) collective-permute-start(bf16[2560,128]{1,0:T(8,128)(2,1)S(1)} %get-tuple-element.32), channel_id=1, source_target_pairs={{0,1},{1,0},{2,3},{3,2},{4,5},{5,4},{6,7},{7,6},{8,9},{9,8},{10,11... | collective-permute-start | bytes 1966088 | tf_op jit(solution)/shard_map/ppermute | solution.py:310
  91.7 18.8 %copy-start.10 = (f32[2]{0:T(128)S(1)}, f32[2]{0:T(128)}, u32[]{:S(2)}) copy-start(f32[2]{0:T(128)} %constant.36.clone.factors) | copy-start | bytes 28
  105.6 6.5 %collective-permute-start.5 = (bf16[2304,128]{1,0:T(8,128)(2,1)S(1)}, bf16[2304,128]{1,0:T(8,128)(2,1)S(1)}, u32[]{:S(2)}, u32[]{:S(2)}) collective-permute-start(bf16[2304,128]{1,0:T(8,128)(2,1)S(1)} %bitcast.18), channel_id=1, source_target_pairs={{0,1},{1,0},{2,3},{3,2},{4,5},{5,4},{6,7},{7,6},{8,9},{9,8},{10,11... | collective-permute-start | bytes 1769480 | tf_op jit(solution)/shard_map/ppermute | solution.py:337

commit v6 on v5

--- a/solution.py
+++ b/solution.py
@@ -334,6 +334,7 @@
         smem=(0,),
     )
     whole = all_swap(spread, "enc").reshape(2 * depth, LANES)
+    whole, observation_slope = lax.optimization_barrier((whole, observation_slope))
     theirs = lax.ppermute(whole, "blk", swap)
     factors = jnp.array([1.0 / math.sqrt(devices * slots), 1.0 / math.sqrt(devices * LON)], F32)
     sizes = ((channels, hid), (hid, code), (code, code))

time: 114 us -> 114 us (level)
  blocking collectives: 52.6 us -> 38.7 us
  waiting for transfers between devices: 14.3 us -> 22.9 us
  starting transfers between devices: 26.9 us -> 31.4 us
    all_to_all x3 -> x2, blocking collectives: 52.6 us -> 38.7 us  [all_swap(): lax.all_to_all(blocks, axis, split_axis=0, concat_axis=0, tiled=True, axi...]
    all_to_all x1 -> x2, waiting for transfers between devices: 8.23 us -> 16.8 us  [all_swap(): lax.all_to_all(blocks, axis, split_axis=0, concat_axis=0, tiled=True, axi...]
    all_to_all x1 -> x2, starting transfers between devices: 15.7 us -> 20.3 us  [all_swap(): lax.all_to_all(blocks, axis, split_axis=0, concat_axis=0, tiled=True, axi...]
  transfers between devices with their start and end apart: 7 -> 8, of which waited for: 4 -> 5; matrix products, arithmetic and copies ran while one was open for 5% -> 5% of each run, Pallas kernels for 4% -> 4%
where the time goes in v6:
time: 114 us
  blocking collectives  38.7 us (34%)
  starting transfers between devices  31.4 us (28%)
  waiting for transfers between devices  22.9 us (20%)
  Pallas kernels  12.6 us (11%)
  matrix products  3.81 us (3%)
  other arithmetic  3.05 us (3%)
    all_to_all x2, blocking collectives, all_swap(): lax.all_to_all(blocks, axis, split_axis=0, concat_axis=0, tiled=True, axi...  38.7 us
    all_to_all x2, starting transfers between devices, all_swap(): lax.all_to_all(blocks, axis, split_axis=0, concat_axis=0, tiled=True, axi...  20.3 us
    all_to_all x2, waiting for transfers between devices, all_swap(): lax.all_to_all(blocks, axis, split_axis=0, concat_axis=0, tiled=True, axi...  16.8 us
    pallas_call x9, Pallas kernels, local_kernel(): pl.pallas_call(body, out_shape=out_shape, in_specs=in_specs, out_specs=ou...  12.6 us
    ppermute x2, starting transfers between devices, trade(): beyond = lax.ppermute(far, BOTH, links + [(j, i) for i, j in links])  7.14 us
    ppermute x2, waiting for transfers between devices, trade(): beyond = lax.ppermute(far, BOTH, links + [(j, i) for i, j in links])  3.97 us
    ppermute x1, starting transfers between devices, shards(): theirs = lax.ppermute(whole, 'blk', swap)  3.73 us
    dot_general x3, matrix products, dot(): return jnp.dot(a, b, preferred_element_type=F32)  2.78 us
  transfers between devices with their start and end apart: 8, of which 5 were waited for; matrix products, arithmetic and copies ran while one was open for 5% of the time, Pallas kernels for 4%

profile of v6, /device:TPU:1, one launch (start us, length us, event | category | flops | bytes accessed | tf_op | source)
XLA Modules:
  0.0 113.7 jit_solution(1959648623569080015)
XLA Ops:
  0.6 15.7 %all-to-all-start = ((bf16[256,2,128]{2,1,0:T(2,128)(2,1)}), bf16[256,2,128]{2,1,0:T(2,128)(2,1)S(1)}, u32[]{:S(2)}, u32[]{:S(2)}) async-start(bf16[256,2,128]{2,1,0:T(2,128)(2,1)} %bitcast.25), calls=%async_computation | async-start | bytes 262144 | tf_op jit(solution)/shard_map/all_to_all | solution.py:242
  16.3 0.8 iota_compare_fusion.7
  17.1 0.1 lt.29
  17.3 0.7 broadcast_select_fusion
  17.9 0.9 convert_reduce_fusion
  18.9 0.1 copy.26.share
  19.1 1.9 %fusion.7 = bf16[512,256]{0,1:T(8,128)(2,1)S(1)} fusion(bf16[256,1440]{1,0:T(8,128)(2,1)} %constant.33.clone.table, s32[512]{0:T(512)S(1)} %broadcast_select_fusion), kind=kOutput, calls=%fused_computation.9 | convolution fusion | flops 378355712 | bytes 1001472 | tf_op jit(solution)/shard_map/dot_general | solution.py:23
  20.9 8.2 %all-to-all-done = bf16[256,2,128]{2,1,0:T(2,128)(2,1)S(1)} async-done(((bf16[256,2,128]{2,1,0:T(2,128)(2,1)}), bf16[256,2,128]{2,1,0:T(2,128)(2,1)S(1)}, u32[]{:S(2)}, u32[]{:S(2)}) %all-to-all-start) | async-done | bytes 131104 | tf_op jit(solution)/shard_map/all_to_all | solution.py:242
  29.2 0.6 fusion.6.latent
  29.9 0.3 fusion.11
  30.2 3.6 %collective-permute-start.1 = (bf16[256,512]{1,0:T(8,128)(2,1)S(1)}, bf16[256,512]{1,0:T(8,128)(2,1)S(1)}, u32[]{:S(2)}, u32[]{:S(2)}) collective-permute-start(bf16[256,512]{1,0:T(8,128)(2,1)S(1)} %get-tuple-element.43), channel_id=1, source_target_pairs={{1,2},{3,4},{5,6},{7,8},{9,10},{11,12},{13,14},{15,16},{17,18},{19... | collective-permute-start | bytes 786440 | tf_op jit(solution)/shard_map/ppermute | solution.py:236
  33.8 0.1 collective-permute-start
  33.9 0.6 fusion.1.onehot
  34.6 3.4 %collective-permute-done.1.beyond = bf16[256,512]{1,0:T(8,128)(2,1)S(1)} collective-permute-done((bf16[256,512]{1,0:T(8,128)(2,1)S(1)}, bf16[256,512]{1,0:T(8,128)(2,1)S(1)}, u32[]{:S(2)}, u32[]{:S(2)}) %collective-permute-start.1) | collective-permute-done | bytes 262176 | tf_op jit(solution)/shard_map/ppermute | solution.py:236
  38.1 2.5 %shard_map.173 = (bf16[512,512]{1,0:T(8,128)(2,1)S(1)}, bf16[256,512]{1,0:T(8,128)(2,1)S(1)}, bf16[256,512]{1,0:T(8,128)(2,1)S(1)}, bf16[256,512]{1,0:T(8,128)(2,1)S(1)}) custom-call(s32[1]{0:T(128)} %bitcast.2.core, f32[256,512]{1,0:T(8,128)S(1)} %get-tuple-element.44.spectrum, bf16[256,512]{1,0:T(8,128)(2,1)S(1)} %collective-permute-done.inside, ...), custom_call_target="tpu_custom_call" | custom-call | flops 754974720 | bytes 4423680 | tf_op jit(solution)/shard_map/pallas_call | solution.py:46
  40.6 3.5 %collective-permute-start.2 = (bf16[256,512]{1,0:T(8,128)(2,1)S(1)}, bf16[256,512]{1,0:T(8,128)(2,1)S(1)}, u32[]{:S(2)}, u32[]{:S(2)}) collective-permute-start(bf16[256,512]{1,0:T(8,128)(2,1)S(1)} %get-tuple-element.29), channel_id=1, source_target_pairs={{1,2},{3,4},{5,6},{7,8},{9,10},{11,12},{13,14},{15,16},{17,18},{19... | collective-permute-start | bytes 786440 | tf_op jit(solution)/shard_map/ppermute | solution.py:236
  44.2 1.0 fusion.5.slot_cot
  45.2 2.5 %shard_map.174 = bf16[1440,512]{1,0:T(8,128)(2,1)} custom-call(bf16[1440,256]{1,0:T(8,128)(2,1)S(1)} %copy-done, bf16[256,512]{1,0:T(8,128)(2,1)S(1)} %get-tuple-element.26.coeffs, bf16[1440,512]{1,0:T(8,128)(2,1)S(1)} %fusion.1.onehot, bf16[512,512]{1,0:T(8,128)(2,1)S(1)} %fusion.6.latent), custom_call_target="tpu_custom_call" | custom-call | flops 1132462080 | bytes 4423680 | tf_op jit(solution)/shard_map/pallas_call | solution.py:46
  47.7 0.5 collective-permute-done.2.from_beyond
  48.3 2.1 %shard_map.175 = (bf16[2560,128]{1,0:T(8,128)(2,1)S(1)}, f32[2304,128]{1,0:T(8,128)S(1)}, bf16[256,128]{1,0:T(8,128)(2,1)S(1)}) custom-call(s32[1]{0:T(128)} %bitcast.2.core, bf16[256,512]{1,0:T(8,128)(2,1)S(1)} %collective-permute-done.2.from_beyond, bf16[256,512]{1,0:T(8,128)(2,1)S(1)} %collective-permute-done.3.from_inside, f32[512,1]{1,0:T(8,128)S(1)} %copy.26.share, ...), custom_call_target="tpu_custom_call" | custom-call | flops 786432000 | bytes 1572864 | tf_op jit(solution)/shard_map/pallas_call | solution.py:46
  50.5 2.1 %collective-permute-done.4.got = bf16[2560,128]{1,0:T(8,128)(2,1)S(1)} collective-permute-done((bf16[2560,128]{1,0:T(8,128)(2,1)S(1)}, bf16[2560,128]{1,0:T(8,128)(2,1)S(1)}, u32[]{:S(2)}, u32[]{:S(2)}) %collective-permute-start.4) | collective-permute-done | bytes 655392 | tf_op jit(solution)/shard_map/ppermute | solution.py:310
  52.6 0.1 shard_map.176
  52.7 23.4 %all_to_all.20.got = bf16[16,176,128]{2,1,0:T(8,128)(2,1)S(1)} all-to-all(bf16[16,176,128]{2,1,0:T(8,128)(2,1)S(1)} %shard_map.176), channel_id=1, replica_groups=mesh['enc'=16,'blk'=16] {'enc'}, dimensions={0} | all-to-all | bytes 1441792 | tf_op jit(solution)/shard_map/all_to_all | solution.py:242
  76.1 0.3 shard_map.177
  76.5 15.2 %all_to_all.21.got = bf16[8,208,128]{2,1,0:T(8,128)(2,1)S(1)} all-to-all(bf16[8,208,128]{2,1,0:T(8,128)(2,1)S(1)} %shard_map.177), channel_id=1, replica_groups={{0,2,4,6,8,10,12,14},{1,3,5,7,9,11,13,15},{16,18,20,22,24,26,28,30},{17..., dimensions={0} | all-to-all | bytes 851968 | tf_op jit(solution)/shard_map/all_to_all | solution.py:242
  91.7 0.9 shard_map.178
  92.6 4.6 %all-to-all-start.3 = ((bf16[16,144,128]{2,1,0:T(8,128)(2,1)}), bf16[16,144,128]{2,1,0:T(8,128)(2,1)S(1)}, u32[]{:S(2)}, u32[]{:S(2)}) async-start(bf16[16,144,128]{2,1,0:T(8,128)(2,1)} %shard_map.178), calls=%async_computation.3 | async-start | bytes 1179648 | tf_op jit(solution)/shard_map/all_to_all | solution.py:242
  97.2 1.0 shard_map.179
  98.1 8.6 %all-to-all-done.3 = bf16[16,144,128]{2,1,0:T(8,128)(2,1)S(1)} async-done(((bf16[16,144,128]{2,1,0:T(8,128)(2,1)}), bf16[16,144,128]{2,1,0:T(8,128)(2,1)S(1)}, u32[]{:S(2)}, u32[]{:S(2)}) %all-to-all-start.3) | async-done | bytes 589856 | tf_op jit(solution)/shard_map/all_to_all | solution.py:242
  106.8 3.7 %collective-permute-start.5 = (bf16[2304,128]{1,0:T(8,128)(2,1)S(1)}, bf16[2304,128]{1,0:T(8,128)(2,1)S(1)}, u32[]{:S(2)}, u32[]{:S(2)}) collective-permute-start(bf16[2304,128]{1,0:T(8,128)(2,1)S(1)} %bitcast.18), channel_id=1, source_target_pairs={{0,1},{1,0},{2,3},{3,2},{4,5},{5,4},{6,7},{7,6},{8,9},{9,8},{10,11... | collective-permute-start | bytes 1769480 | tf_op jit(solution)/shard_map/ppermute | solution.py:338
  110.5 1.6 %shard_map.180 = (f32[128,512]{1,0:T(8,128)}, f32[512,512]{1,0:T(8,128)}, f32[512,512]{1,0:T(8,128)}) custom-call(f32[2]{0:T(128)S(1)} %copy-done.10, s32[1]{0:T(128)} %bitcast.2.core, bf16[2304,128]{1,0:T(8,128)(2,1)S(1)} %bitcast.19), custom_call_target="tpu_custom_call" | custom-call | flops 1179648 | bytes 2359296 | tf_op jit(solution)/shard_map/pallas_call | solution.py:46
  112.1 1.6 %shard_map.181 = (f32[128,512]{1,0:T(8,128)}, f32[512,512]{1,0:T(8,128)}, f32[512,512]{1,0:T(8,128)}) custom-call(f32[2]{0:T(128)S(1)} %copy-done.10, s32[1]{0:T(128)} %bitcast.2.core, bf16[2304,128]{1,0:T(8,128)(2,1)S(1)} %collective-permute-done.5.half, ...), custom_call_target="tpu_custom_call", output_to_operand_aliasing={{0}: (3, {}), {1}: (4, {}), {2}: (5, {})} | custom-call | flops 1179648 | bytes 2359296 | tf_op jit(solution)/shard_map/pallas_call | solution.py:46
  (28 shorter events, 0.3 us)
Async XLA Ops:
  0.6 28.5 %all-to-all-start = ((bf16[256,2,128]{2,1,0:T(2,128)(2,1)}), bf16[256,2,128]{2,1,0:T(2,128)(2,1)S(1)}, u32[]{:S(2)}, u32[]{:S(2)}) async-start(bf16[256,2,128]{2,1,0:T(2,128)(2,1)} %bitcast.25), calls=%async_computation | async-start | bytes 262144 | tf_op jit(solution)/shard_map/all_to_all | solution.py:242
  18.9 10.3 %copy-start.5 = (bf16[512,512]{1,0:T(8,128)(2,1)S(1)}, bf16[512,512]{1,0:T(8,128)(2,1)}, u32[]{:S(2)}) copy-start(bf16[512,512]{1,0:T(8,128)(2,1)} %w_out.1) | copy-start | bytes 1572868
  18.9 10.3 %copy-start.6 = (bf16[128,512]{1,0:T(8,128)(2,1)S(1)}, bf16[128,512]{1,0:T(8,128)(2,1)}, u32[]{:S(2)}) copy-start(bf16[128,512]{1,0:T(8,128)(2,1)} %w_in.1) | copy-start | bytes 393220
  29.2 8.8 %copy-start.3 = (bf16[1,1440,512]{2,1,0:T(8,128)(2,1)S(1)}, bf16[1,1440,512]{2,1,0:T(8,128)(2,1)}, u32[]{:S(2)}) copy-start(bf16[1,1440,512]{2,1,0:T(8,128)(2,1)} %param.23) | copy-start | bytes 4423684
  29.8 8.2 %copy-start = (bf16[1440,256]{1,0:T(8,128)(2,1)S(1)}, bf16[1440,256]{1,0:T(8,128)(2,1)}, u32[]{:S(2)}) copy-start(bf16[1440,256]{1,0:T(8,128)(2,1)} %constant.34.clone.table_t) | copy-start | bytes 2211844
  29.8 8.2 %copy-start.1 = (f32[256,512]{1,0:T(8,128)S(1)}, f32[256,512]{1,0:T(8,128)}, u32[]{:S(2)}) copy-start(f32[256,512]{1,0:T(8,128)} %w_spec.3) | copy-start | bytes 1572868
  29.8 8.2 %copy-start.2 = (bf16[512,512]{1,0:T(8,128)(2,1)S(1)}, bf16[512,512]{1,0:T(8,128)(2,1)}, u32[]{:S(2)}) copy-start(bf16[512,512]{1,0:T(8,128)(2,1)} %w_mix.3) | copy-start | bytes 1572868
  29.8 8.2 %copy-start.4 = (bf16[256,1440]{1,0:T(8,128)(2,1)S(1)}, bf16[256,1440]{1,0:T(8,128)(2,1)}, u32[]{:S(2)}) copy-start(bf16[256,1440]{1,0:T(8,128)(2,1)} %constant.33.clone.table) | copy-start | bytes 2211844
  29.8 8.2 %copy-start.7 = (f32[256,1]{1,0:T(8,128)S(1)}, f32[256,1]{1,0:T(8,128)}, u32[]{:S(2)}) copy-start(f32[256,1]{1,0:T(8,128)} %constant.35.clone.weight) | copy-start | bytes 3076
  29.8 8.2 %copy-start.8 = (f32[1,512]{1,0:T(1,128)S(1)}, f32[1,512]{1,0:T(1,128)}, u32[]{:S(2)}) copy-start(f32[1,512]{1,0:T(1,128)} %north.1) | copy-start | bytes 6148
  29.9 8.2 %copy-start.9 = (f32[1,512]{1,0:T(1,128)S(1)}, f32[1,512]{1,0:T(1,128)}, u32[]{:S(2)}) copy-start(f32[1,512]{1,0:T(1,128)} %south.1) | copy-start | bytes 6148
  30.2 7.8 %collective-permute-start.1 = (bf16[256,512]{1,0:T(8,128)(2,1)S(1)}, bf16[256,512]{1,0:T(8,128)(2,1)S(1)}, u32[]{:S(2)}, u32[]{:S(2)}) collective-permute-start(bf16[256,512]{1,0:T(8,128)(2,1)S(1)} %get-tuple-element.43), channel_id=1, source_target_pairs={{1,2},{3,4},{5,6},{7,8},{9,10},{11,12},{13,14},{15,16},{17,18},{19... | collective-permute-start | bytes 786440 | tf_op jit(solution)/shard_map/ppermute | solution.py:236
  33.8 4.2 %collective-permute-start = (bf16[256,512]{1,0:T(8,128)(2,1)S(1)}, bf16[256,512]{1,0:T(8,128)(2,1)S(1)}, u32[]{:S(2)}, u32[]{:S(2)}) collective-permute-start(bf16[256,512]{1,0:T(8,128)(2,1)S(1)} %get-tuple-element.43), channel_id=1, source_target_pairs={{0,1},{1,0},{2,3},{3,2},{4,5},{5,4},{6,7},{7,6},{8,9},{9,8},{10,11... | collective-permute-start | bytes 786440 | tf_op jit(solution)/shard_map/ppermute | solution.py:237
  40.6 7.7 %collective-permute-start.2 = (bf16[256,512]{1,0:T(8,128)(2,1)S(1)}, bf16[256,512]{1,0:T(8,128)(2,1)S(1)}, u32[]{:S(2)}, u32[]{:S(2)}) collective-permute-start(bf16[256,512]{1,0:T(8,128)(2,1)S(1)} %get-tuple-element.29), channel_id=1, source_target_pairs={{1,2},{3,4},{5,6},{7,8},{9,10},{11,12},{13,14},{15,16},{17,18},{19... | collective-permute-start | bytes 786440 | tf_op jit(solution)/shard_map/ppermute | solution.py:236
  44.1 4.2 %collective-permute-start.3 = (bf16[256,512]{1,0:T(8,128)(2,1)S(1)}, bf16[256,512]{1,0:T(8,128)(2,1)S(1)}, u32[]{:S(2)}, u32[]{:S(2)}) collective-permute-start(bf16[256,512]{1,0:T(8,128)(2,1)S(1)} %get-tuple-element.30), channel_id=1, source_target_pairs={{0,1},{1,0},{2,3},{3,2},{4,5},{5,4},{6,7},{7,6},{8,9},{9,8},{10,11... | collective-permute-start | bytes 786440 | tf_op jit(solution)/shard_map/ppermute | solution.py:237
  50.4 2.2 %collective-permute-start.4 = (bf16[2560,128]{1,0:T(8,128)(2,1)S(1)}, bf16[2560,128]{1,0:T(8,128)(2,1)S(1)}, u32[]{:S(2)}, u32[]{:S(2)}) collective-permute-start(bf16[2560,128]{1,0:T(8,128)(2,1)S(1)} %get-tuple-element.34), channel_id=1, source_target_pairs={{0,1},{1,0},{2,3},{3,2},{4,5},{5,4},{6,7},{7,6},{8,9},{9,8},{10,11... | collective-permute-start | bytes 1966088 | tf_op jit(solution)/shard_map/ppermute | solution.py:310
  91.7 18.8 %copy-start.10 = (f32[2]{0:T(128)S(1)}, f32[2]{0:T(128)}, u32[]{:S(2)}) copy-start(f32[2]{0:T(128)} %constant.36.clone.factors) | copy-start | bytes 28
  92.6 14.2 %all-to-all-start.3 = ((bf16[16,144,128]{2,1,0:T(8,128)(2,1)}), bf16[16,144,128]{2,1,0:T(8,128)(2,1)S(1)}, u32[]{:S(2)}, u32[]{:S(2)}) async-start(bf16[16,144,128]{2,1,0:T(8,128)(2,1)} %shard_map.178), calls=%async_computation.3 | async-start | bytes 1179648 | tf_op jit(solution)/shard_map/all_to_all | solution.py:242
  106.8 5.4 %collective-permute-start.5 = (bf16[2304,128]{1,0:T(8,128)(2,1)S(1)}, bf16[2304,128]{1,0:T(8,128)(2,1)S(1)}, u32[]{:S(2)}, u32[]{:S(2)}) collective-permute-start(bf16[2304,128]{1,0:T(8,128)(2,1)S(1)} %bitcast.18), channel_id=1, source_target_pairs={{0,1},{1,0},{2,3},{3,2},{4,5},{5,4},{6,7},{7,6},{8,9},{9,8},{10,11... | collective-permute-start | bytes 1769480 | tf_op jit(solution)/shard_map/ppermute | solution.py:338

commit v7 on v6

--- a/solution.py
+++ b/solution.py
@@ -98,7 +98,24 @@
     to_inside[...] = (near_row * grad_mix).astype(BF16)
 
 
-def state_body(table_t, coeffs, onehot, latent, state):
+def halves(core, right):
+    width = right.shape[1] // 2
+    low, high = right[:, :width], right[:, width:]
+    first = core[0] == 0
+    return jnp.where(first, low, high), jnp.where(first, high, low)
+
+
+def put(out, at, depth, value):
+    for piece in range(value.shape[1] // LANES):
+        start = piece * depth + at
+        out[start : start + value.shape[0], :] = value[:, piece * LANES : (piece + 1) * LANES]
+
+
+def state_body(core, table_t, coeffs, onehot, latent, pair, state, blend_near, blend_far):
+    count = pair.shape[0] // 2
+    near, far = halves(core, pair[count:, :])
+    put(blend_near, 0, blend_near.shape[0] // 2, dot_ta(pair[:count, :], near))
+    put(blend_far, 0, blend_far.shape[0] // 2, dot_ta(pair[:count, :], far).astype(BF16))
     for low, size in TILES:
         part = pl.ds(low, size)
         pre_act = dot(table_t[part, :], coeffs[...])
@@ -109,10 +126,8 @@
     core, from_beyond, from_inside, share, pair, w_mix, w_spec, rows, w_in, slot_modes, slot_cot, w_out,
     sent, mine, kept,
 ):
-    first = core[0] == 0
     count = pair.shape[0] // 2
-    mix, coeffs = pair[:count, :], pair[count:, :]
-    grad_mix = dot_tb(coeffs, w_mix[...])
+    grad_mix = dot_tb(pair[count:, :], w_mix[...])
     grad_spec = (w_spec[...] * grad_mix + from_inside[...].astype(F32) + from_beyond[...].astype(F32)).astype(BF16)
     pre1 = dot(rows[...], w_in[...])
     gate = logistic(pre1)
@@ -134,28 +149,25 @@
     sent[mine.shape[0] :, :] = ordered[half:]
     at = 0
     depth = mine.shape[0] // 2
-    for left, right in ((hidden, grad_latent), (mix, coeffs), (rows[...], grad_pre1)):
-        width = right.shape[1] // 2
-        low, high = right[:, :width], right[:, width:]
-        near = dot_ta(left, jnp.where(first, low, high))
-        far = dot_ta(left, jnp.where(first, high, low)).astype(BF16)
-        size = near.shape[0]
-        for piece in range(2):
-            lanes = slice(piece * LANES, (piece + 1) * LANES)
-            mine[piece * depth + at : piece * depth + at + size, :] = near[:, lanes]
-            sent[piece * depth + at : piece * depth + at + size, :] = far[:, lanes]
-        at += size
-
-
-def scatter_body(mine, kept, got, out):
+    for left, right in ((hidden, grad_latent), (rows[...], grad_pre1)):
+        near, far = halves(core, right)
+        put(mine, at, depth, dot_ta(left, near))
+        put(sent, at, depth, dot_ta(left, far).astype(BF16))
+        at += left.shape[1]
+
+
+def scatter_body(mine, kept, got, blend_near, blend_got, out):
     count = out.shape[0]
-    size = mine.shape[0] // count
     few = kept.shape[0] // count
     for i in range(count):
         out[i, :few, :] = kept[i * few : (i + 1) * few, :]
         out[i, few : 2 * few, :] = got[mine.shape[0] + i * few : mine.shape[0] + (i + 1) * few, :]
-        part = slice(i * size, (i + 1) * size)
-        out[i, 2 * few :, :] = (mine[part, :] + got[part, :].astype(F32)).astype(BF16)
+        at = 2 * few
+        for ours, theirs in ((mine, got), (blend_near, blend_got)):
+            size = ours.shape[0] // count
+            part = slice(i * size, (i + 1) * size)
+            out[i, at : at + size, :] = (ours[part, :] + theirs[part, :].astype(F32)).astype(BF16)
+            at += size
 
 
 def relay_body(slots, got, out):
@@ -203,23 +215,39 @@
     slope[...] = ordered.astype(BF16)
 
 
-def final_body(other, factors, core, half, *refs):
+def final_body(other, blocks, factors, core, half, *refs):
     outs, held, sems = refs[-7:-4], refs[-4:-1], refs[-1]
+    entry, exit_, blend = held
     side = (core[0] + 1) & 1 if other else core[0]
-    width = held[0].shape[1]
-    pieces = width // LANES
-    depth = half.shape[0] // pieces
-    at = 0
+    width = blend.shape[1]
+    chunk = half.shape[0] // blocks
+    late = 2 * blend.shape[0] // blocks
+    early = chunk - late
     copies = []
-    for i, index in enumerate((1, 2, 0)):
-        size = held[index].shape[0]
-        for piece in range(pieces):
-            part = slice(piece * depth + at, piece * depth + at + size)
-            held[index][:, piece * LANES : (piece + 1) * LANES] = half[part, :].astype(F32) * factors[i & 1]
-        at += size
+
+    def send(index):
         target = outs[index].at[:, pl.ds(pl.multiple_of(side * width, width), width)]
         copies.append(pltpu.make_async_copy(held[index], target, sems.at[index]))
         copies[-1].start()
+
+    for i in range(blocks):
+        piece, at = divmod(i, blocks // 2)
+        lanes = slice(piece * LANES, (piece + 1) * LANES)
+        values = half[i * chunk + early : (i + 1) * chunk, :].astype(F32)
+        blend[at * late : (at + 1) * late, lanes] = values * factors[1]
+    send(2)
+    for i in range(blocks):
+        piece, at = divmod(i, blocks // 2)
+        lanes = slice(piece * LANES, (piece + 1) * LANES)
+        values = half[i * chunk : i * chunk + early, :].astype(F32) * factors[0]
+        start, end = at * early, (at + 1) * early
+        count = min(max(exit_.shape[0] - start, 0), early)
+        if count:
+            exit_[start : start + count, lanes] = values[:count]
+        if count < early:
+            entry[start + count - exit_.shape[0] : end - exit_.shape[0], lanes] = values[count:]
+    send(1)
+    send(0)
     for copy in copies:
         copy.wait()
 
@@ -287,17 +315,19 @@
         smem=(0,),
         room=12,
     )
-    state = local_kernel(
+    state, blend_near, blend_far = local_kernel(
         state_body,
-        shape((LON, code), BF16),
+        [shape((LON, code), BF16), shape((2 * code, LANES), F32), shape((2 * code, LANES), BF16)],
         2 * LON * code * (2 * MODES + slots),
         6 * LON * code,
-        table_t, coeffs, onehot, latent,
-        room=8,
+        core_arg, table_t, coeffs, onehot, latent, pair,
+        smem=(0,),
+        room=10,
     )
     from_inside, from_beyond = trade(to_inside, to_beyond, devices)
-    state, pair = lax.optimization_barrier((state, pair))
-    depth = hid + code + channels
+    blend_got = lax.ppermute(blend_far, "blk", swap)
+    state, pair, blend_got = lax.optimization_barrier((state, pair, blend_got))
+    depth = hid + channels
     sent, mine, kept = local_kernel(
         back_body,
         [shape((2 * depth + half, LANES), BF16), shape((2 * depth, LANES), F32), shape((half, LANES), BF16)],
@@ -308,10 +338,12 @@
         room=12,
     )
     got = lax.ppermute(sent, "blk", swap)
+    depth += code
     chunk = 2 * depth // encs
     few, more = slots // encs, slots // deep
     parts = local_kernel(
-        scatter_body, shape((encs, few + chunk, LANES), BF16), depth * LANES, 16 * depth * LANES, mine, kept, got
+        scatter_body, shape((encs, few + chunk, LANES), BF16), depth * LANES, 16 * depth * LANES, mine, kept, got,
+        blend_near, blend_got,
     )
     parts = all_swap(parts, "enc")
     parts = local_kernel(
@@ -341,7 +373,7 @@
     outs = []
     for other, half_rows in ((False, whole), (True, theirs)):
         outs = local_kernel(
-            functools.partial(final_body, other),
+            functools.partial(final_body, other, encs),
             [shape(dims, F32) for dims in sizes],
             2 * depth * code,
             4 * depth * code,

time: 114 us -> 114 us (level)
  transfers between devices with their start and end apart: 8 -> 9, of which waited for: 5 -> 5; matrix products, arithmetic and copies ran while one was open for 5% -> 6% of each run, Pallas kernels for 4% -> 5%
where the time goes in v7:
time: 114 us; the launch traced here: 113 us
  blocking collectives  38.5 us (34%)
  starting transfers between devices  32.3 us (28%)
  waiting for transfers between devices  21.8 us (19%)
  Pallas kernels  12.6 us (11%)
  matrix products  3.81 us (3%)
  other arithmetic  3.05 us (3%)
    all_to_all x2, blocking collectives, all_swap(): lax.all_to_all(blocks, axis, split_axis=0, concat_axis=0, tiled=True, axi...  38.5 us
    all_to_all x2, starting transfers between devices, all_swap(): lax.all_to_all(blocks, axis, split_axis=0, concat_axis=0, tiled=True, axi...  20.3 us
    all_to_all x2, waiting for transfers between devices, all_swap(): lax.all_to_all(blocks, axis, split_axis=0, concat_axis=0, tiled=True, axi...  16.8 us
    pallas_call x9, Pallas kernels, local_kernel(): pl.pallas_call(body, out_shape=out_shape, in_specs=in_specs, out_specs=ou...  12.6 us
    ppermute x2, starting transfers between devices, trade(): beyond = lax.ppermute(far, BOTH, links + [(j, i) for i, j in links])  7.13 us
    ppermute x1, starting transfers between devices, shards(): theirs = lax.ppermute(whole, 'blk', swap)  3.73 us
    ppermute x2, waiting for transfers between devices, trade(): beyond = lax.ppermute(far, BOTH, links + [(j, i) for i, j in links])  3.43 us
    dot_general x3, matrix products, dot(): return jnp.dot(a, b, preferred_element_type=F32)  2.78 us
  transfers between devices with their start and end apart: 9, of which 5 were waited for; matrix products, arithmetic and copies ran while one was open for 6% of the time, Pallas kernels for 5%

profile of v7, /device:TPU:1, one launch (start us, length us, event | category | flops | bytes accessed | tf_op | source)
XLA Modules:
  0.0 113.2 jit_solution(12576689897972648849)
XLA Ops:
  0.6 15.7 %all-to-all-start = ((bf16[256,2,128]{2,1,0:T(2,128)(2,1)}), bf16[256,2,128]{2,1,0:T(2,128)(2,1)S(1)}, u32[]{:S(2)}, u32[]{:S(2)}) async-start(bf16[256,2,128]{2,1,0:T(2,128)(2,1)} %bitcast.24), calls=%async_computation | async-start | bytes 262144 | tf_op jit(solution)/shard_map/all_to_all | solution.py:270
  16.3 0.8 iota_compare_fusion.7
  17.1 0.1 lt.29
  17.3 0.7 broadcast_select_fusion
  17.9 0.9 convert_reduce_fusion
  18.9 0.1 copy.26.share
  19.1 1.9 %fusion.7 = bf16[512,256]{0,1:T(8,128)(2,1)S(1)} fusion(bf16[256,1440]{1,0:T(8,128)(2,1)} %constant.33.clone.table, s32[512]{0:T(512)S(1)} %broadcast_select_fusion), kind=kOutput, calls=%fused_computation.9 | convolution fusion | flops 378355712 | bytes 1001472 | tf_op jit(solution)/shard_map/dot_general | solution.py:23
  20.9 8.2 %all-to-all-done = bf16[256,2,128]{2,1,0:T(2,128)(2,1)S(1)} async-done(((bf16[256,2,128]{2,1,0:T(2,128)(2,1)}), bf16[256,2,128]{2,1,0:T(2,128)(2,1)S(1)}, u32[]{:S(2)}, u32[]{:S(2)}) %all-to-all-start) | async-done | bytes 131104 | tf_op jit(solution)/shard_map/all_to_all | solution.py:270
  29.2 0.6 fusion.6.latent
  29.9 0.3 fusion.11
  30.2 3.6 %collective-permute-start.1 = (bf16[256,512]{1,0:T(8,128)(2,1)S(1)}, bf16[256,512]{1,0:T(8,128)(2,1)S(1)}, u32[]{:S(2)}, u32[]{:S(2)}) collective-permute-start(bf16[256,512]{1,0:T(8,128)(2,1)S(1)} %get-tuple-element.51), channel_id=1, source_target_pairs={{1,2},{3,4},{5,6},{7,8},{9,10},{11,12},{13,14},{15,16},{17,18},{19... | collective-permute-start | bytes 786440 | tf_op jit(solution)/shard_map/ppermute | solution.py:264
  33.9 0.6 fusion.1.onehot
  34.6 3.4 %collective-permute-done.1.beyond = bf16[256,512]{1,0:T(8,128)(2,1)S(1)} collective-permute-done((bf16[256,512]{1,0:T(8,128)(2,1)S(1)}, bf16[256,512]{1,0:T(8,128)(2,1)S(1)}, u32[]{:S(2)}, u32[]{:S(2)}) %collective-permute-start.1) | collective-permute-done | bytes 262176 | tf_op jit(solution)/shard_map/ppermute | solution.py:264
  38.1 2.6 %shard_map.173 = (bf16[512,512]{1,0:T(8,128)(2,1)S(1)}, bf16[256,512]{1,0:T(8,128)(2,1)S(1)}, bf16[256,512]{1,0:T(8,128)(2,1)S(1)}, bf16[256,512]{1,0:T(8,128)(2,1)S(1)}) custom-call(s32[1]{0:T(128)} %bitcast.2.core, f32[256,512]{1,0:T(8,128)S(1)} %get-tuple-element.52.spectrum, bf16[256,512]{1,0:T(8,128)(2,1)S(1)} %collective-permute-done.inside, ...), custom_call_target="tpu_custom_call" | custom-call | flops 754974720 | bytes 4423680 | tf_op jit(solution)/shard_map/pallas_call | solution.py:46
  40.6 3.5 %collective-permute-start.3 = (bf16[256,512]{1,0:T(8,128)(2,1)S(1)}, bf16[256,512]{1,0:T(8,128)(2,1)S(1)}, u32[]{:S(2)}, u32[]{:S(2)}) collective-permute-start(bf16[256,512]{1,0:T(8,128)(2,1)S(1)} %get-tuple-element.35), channel_id=1, source_target_pairs={{1,2},{3,4},{5,6},{7,8},{9,10},{11,12},{13,14},{15,16},{17,18},{19... | collective-permute-start | bytes 786440 | tf_op jit(solution)/shard_map/ppermute | solution.py:264
  44.2 2.6 %shard_map.174 = (bf16[1440,512]{1,0:T(8,128)(2,1)}, f32[1024,128]{1,0:T(8,128)S(1)}, bf16[1024,128]{1,0:T(8,128)(2,1)S(1)}) custom-call(s32[1]{0:T(128)} %bitcast.2.core, bf16[1440,256]{1,0:T(8,128)(2,1)S(1)} %copy-done.4, bf16[256,512]{1,0:T(8,128)(2,1)S(1)} %get-tuple-element.30.coeffs, bf16[1440,512]{1,0:T(8,128)(2,1)S(1)} %fusion.1.onehot, ...), custom_call_target="tpu_custom_call" | custom-call | flops 1132462080 | bytes 4423680 | tf_op jit(solution)/shard_map/pallas_call | solution.py:46
  46.9 0.5 collective-permute-start.2
  47.4 1.0 fusion.5.slot_cot
  48.4 0.1 collective-permute-done.2.blend_got
  48.5 2.0 %shard_map.175 = (bf16[1536,128]{1,0:T(8,128)(2,1)S(1)}, f32[1280,128]{1,0:T(8,128)S(1)}, bf16[256,128]{1,0:T(8,128)(2,1)S(1)}) custom-call(s32[1]{0:T(128)} %bitcast.2.core, bf16[256,512]{1,0:T(8,128)(2,1)S(1)} %collective-permute-done.3.from_beyond, bf16[256,512]{1,0:T(8,128)(2,1)S(1)} %collective-permute-done.4.from_inside, f32[512,1]{1,0:T(8,128)S(1)} %copy.26.share, ...), custom_call_target="tpu_custom_call" | custom-call | flops 786432000 | bytes 1572864 | tf_op jit(solution)/shard_map/pallas_call | solution.py:46
  50.5 0.5 collective-permute-start.5
  51.0 1.4 %collective-permute-done.5.got = bf16[1536,128]{1,0:T(8,128)(2,1)S(1)} collective-permute-done((bf16[1536,128]{1,0:T(8,128)(2,1)S(1)}, bf16[1536,128]{1,0:T(8,128)(2,1)S(1)}, u32[]{:S(2)}, u32[]{:S(2)}) %collective-permute-start.5) | collective-permute-done | bytes 393248 | tf_op jit(solution)/shard_map/ppermute | solution.py:340
  52.4 23.2 %all_to_all.20.got = bf16[16,176,128]{2,1,0:T(8,128)(2,1)S(1)} all-to-all(bf16[16,176,128]{2,1,0:T(8,128)(2,1)S(1)} %shard_map.176), channel_id=1, replica_groups=mesh['enc'=16,'blk'=16] {'enc'}, dimensions={0} | all-to-all | bytes 1441792 | tf_op jit(solution)/shard_map/all_to_all | solution.py:270
  75.7 0.3 shard_map.177
  76.0 15.2 %all_to_all.21.got = bf16[8,208,128]{2,1,0:T(8,128)(2,1)S(1)} all-to-all(bf16[8,208,128]{2,1,0:T(8,128)(2,1)S(1)} %shard_map.177), channel_id=1, replica_groups={{0,2,4,6,8,10,12,14},{1,3,5,7,9,11,13,15},{16,18,20,22,24,26,28,30},{17..., dimensions={0} | all-to-all | bytes 851968 | tf_op jit(solution)/shard_map/all_to_all | solution.py:270
  91.2 0.9 shard_map.178
  92.1 4.6 %all-to-all-start.3 = ((bf16[16,144,128]{2,1,0:T(8,128)(2,1)}), bf16[16,144,128]{2,1,0:T(8,128)(2,1)S(1)}, u32[]{:S(2)}, u32[]{:S(2)}) async-start(bf16[16,144,128]{2,1,0:T(8,128)(2,1)} %shard_map.178), calls=%async_computation.3 | async-start | bytes 1179648 | tf_op jit(solution)/shard_map/all_to_all | solution.py:270
  96.7 1.0 shard_map.179
  97.7 8.6 %all-to-all-done.3 = bf16[16,144,128]{2,1,0:T(8,128)(2,1)S(1)} async-done(((bf16[16,144,128]{2,1,0:T(8,128)(2,1)}), bf16[16,144,128]{2,1,0:T(8,128)(2,1)S(1)}, u32[]{:S(2)}, u32[]{:S(2)}) %all-to-all-start.3) | async-done | bytes 589856 | tf_op jit(solution)/shard_map/all_to_all | solution.py:270
  106.3 3.7 %collective-permute-start.6 = (bf16[2304,128]{1,0:T(8,128)(2,1)S(1)}, bf16[2304,128]{1,0:T(8,128)(2,1)S(1)}, u32[]{:S(2)}, u32[]{:S(2)}) collective-permute-start(bf16[2304,128]{1,0:T(8,128)(2,1)S(1)} %bitcast.18), channel_id=1, source_target_pairs={{0,1},{1,0},{2,3},{3,2},{4,5},{5,4},{6,7},{7,6},{8,9},{9,8},{10,11... | collective-permute-start | bytes 1769480 | tf_op jit(solution)/shard_map/ppermute | solution.py:370
  110.0 1.6 %shard_map.180 = (f32[128,512]{1,0:T(8,128)}, f32[512,512]{1,0:T(8,128)}, f32[512,512]{1,0:T(8,128)}) custom-call(f32[2]{0:T(128)S(1)} %copy-done.10, s32[1]{0:T(128)} %bitcast.2.core, bf16[2304,128]{1,0:T(8,128)(2,1)S(1)} %bitcast.19), custom_call_target="tpu_custom_call" | custom-call | flops 1179648 | bytes 2359296 | tf_op jit(solution)/shard_map/pallas_call | solution.py:46
  111.6 1.6 %shard_map.181 = (f32[128,512]{1,0:T(8,128)}, f32[512,512]{1,0:T(8,128)}, f32[512,512]{1,0:T(8,128)}) custom-call(f32[2]{0:T(128)S(1)} %copy-done.10, s32[1]{0:T(128)} %bitcast.2.core, bf16[2304,128]{1,0:T(8,128)(2,1)S(1)} %collective-permute-done.6.half, ...), custom_call_target="tpu_custom_call", output_to_operand_aliasing={{0}: (3, {}), {1}: (4, {}), {2}: (5, {})} | custom-call | flops 1179648 | bytes 2359296 | tf_op jit(solution)/shard_map/pallas_call | solution.py:46
  (30 shorter events, 0.4 us)
Async XLA Ops:
  0.6 28.5 %all-to-all-start = ((bf16[256,2,128]{2,1,0:T(2,128)(2,1)}), bf16[256,2,128]{2,1,0:T(2,128)(2,1)S(1)}, u32[]{:S(2)}, u32[]{:S(2)}) async-start(bf16[256,2,128]{2,1,0:T(2,128)(2,1)} %bitcast.24), calls=%async_computation | async-start | bytes 262144 | tf_op jit(solution)/shard_map/all_to_all | solution.py:270
  18.9 10.3 %copy-start.5 = (bf16[512,512]{1,0:T(8,128)(2,1)S(1)}, bf16[512,512]{1,0:T(8,128)(2,1)}, u32[]{:S(2)}) copy-start(bf16[512,512]{1,0:T(8,128)(2,1)} %w_out.1) | copy-start | bytes 1572868
  18.9 10.3 %copy-start.6 = (bf16[128,512]{1,0:T(8,128)(2,1)S(1)}, bf16[128,512]{1,0:T(8,128)(2,1)}, u32[]{:S(2)}) copy-start(bf16[128,512]{1,0:T(8,128)(2,1)} %w_in.1) | copy-start | bytes 393220
  29.2 8.8 %copy-start.3 = (bf16[256,1440]{1,0:T(8,128)(2,1)S(1)}, bf16[256,1440]{1,0:T(8,128)(2,1)}, u32[]{:S(2)}) copy-start(bf16[256,1440]{1,0:T(8,128)(2,1)} %constant.33.clone.table) | copy-start | bytes 2211844
  29.2 8.8 %copy-start.4 = (bf16[1440,256]{1,0:T(8,128)(2,1)S(1)}, bf16[1440,256]{1,0:T(8,128)(2,1)}, u32[]{:S(2)}) copy-start(bf16[1440,256]{1,0:T(8,128)(2,1)} %constant.34.clone.table_t) | copy-start | bytes 2211844
  29.8 8.2 %copy-start = (f32[256,512]{1,0:T(8,128)S(1)}, f32[256,512]{1,0:T(8,128)}, u32[]{:S(2)}) copy-start(f32[256,512]{1,0:T(8,128)} %w_spec.3) | copy-start | bytes 1572868
  29.8 8.2 %copy-start.1 = (bf16[512,512]{1,0:T(8,128)(2,1)S(1)}, bf16[512,512]{1,0:T(8,128)(2,1)}, u32[]{:S(2)}) copy-start(bf16[512,512]{1,0:T(8,128)(2,1)} %w_mix.3) | copy-start | bytes 1572868
  29.8 8.2 %copy-start.2 = (bf16[1,1440,512]{2,1,0:T(8,128)(2,1)S(1)}, bf16[1,1440,512]{2,1,0:T(8,128)(2,1)}, u32[]{:S(2)}) copy-start(bf16[1,1440,512]{2,1,0:T(8,128)(2,1)} %param.23) | copy-start | bytes 4423684
  29.8 8.2 %copy-start.7 = (f32[256,1]{1,0:T(8,128)S(1)}, f32[256,1]{1,0:T(8,128)}, u32[]{:S(2)}) copy-start(f32[256,1]{1,0:T(8,128)} %constant.35.clone.weight) | copy-start | bytes 3076
  29.8 8.2 %copy-start.8 = (f32[1,512]{1,0:T(1,128)S(1)}, f32[1,512]{1,0:T(1,128)}, u32[]{:S(2)}) copy-start(f32[1,512]{1,0:T(1,128)} %north.1) | copy-start | bytes 6148
  29.9 8.2 %copy-start.9 = (f32[1,512]{1,0:T(1,128)S(1)}, f32[1,512]{1,0:T(1,128)}, u32[]{:S(2)}) copy-start(f32[1,512]{1,0:T(1,128)} %south.1) | copy-start | bytes 6148
  30.2 7.8 %collective-permute-start.1 = (bf16[256,512]{1,0:T(8,128)(2,1)S(1)}, bf16[256,512]{1,0:T(8,128)(2,1)S(1)}, u32[]{:S(2)}, u32[]{:S(2)}) collective-permute-start(bf16[256,512]{1,0:T(8,128)(2,1)S(1)} %get-tuple-element.51), channel_id=1, source_target_pairs={{1,2},{3,4},{5,6},{7,8},{9,10},{11,12},{13,14},{15,16},{17,18},{19... | collective-permute-start | bytes 786440 | tf_op jit(solution)/shard_map/ppermute | solution.py:264
  33.8 4.2 %collective-permute-start = (bf16[256,512]{1,0:T(8,128)(2,1)S(1)}, bf16[256,512]{1,0:T(8,128)(2,1)S(1)}, u32[]{:S(2)}, u32[]{:S(2)}) collective-permute-start(bf16[256,512]{1,0:T(8,128)(2,1)S(1)} %get-tuple-element.51), channel_id=1, source_target_pairs={{0,1},{1,0},{2,3},{3,2},{4,5},{5,4},{6,7},{7,6},{8,9},{9,8},{10,11... | collective-permute-start | bytes 786440 | tf_op jit(solution)/shard_map/ppermute | solution.py:265
  40.6 7.9 %collective-permute-start.3 = (bf16[256,512]{1,0:T(8,128)(2,1)S(1)}, bf16[256,512]{1,0:T(8,128)(2,1)S(1)}, u32[]{:S(2)}, u32[]{:S(2)}) collective-permute-start(bf16[256,512]{1,0:T(8,128)(2,1)S(1)} %get-tuple-element.35), channel_id=1, source_target_pairs={{1,2},{3,4},{5,6},{7,8},{9,10},{11,12},{13,14},{15,16},{17,18},{19... | collective-permute-start | bytes 786440 | tf_op jit(solution)/shard_map/ppermute | solution.py:264
  44.1 4.4 %collective-permute-start.4 = (bf16[256,512]{1,0:T(8,128)(2,1)S(1)}, bf16[256,512]{1,0:T(8,128)(2,1)S(1)}, u32[]{:S(2)}, u32[]{:S(2)}) collective-permute-start(bf16[256,512]{1,0:T(8,128)(2,1)S(1)} %get-tuple-element.36), channel_id=1, source_target_pairs={{0,1},{1,0},{2,3},{3,2},{4,5},{5,4},{6,7},{7,6},{8,9},{9,8},{10,11... | collective-permute-start | bytes 786440 | tf_op jit(solution)/shard_map/ppermute | solution.py:265
  46.9 1.7 %collective-permute-start.2 = (bf16[1024,128]{1,0:T(8,128)(2,1)S(1)}, bf16[1024,128]{1,0:T(8,128)(2,1)S(1)}, u32[]{:S(2)}, u32[]{:S(2)}) collective-permute-start(bf16[1024,128]{1,0:T(8,128)(2,1)S(1)} %get-tuple-element.33), channel_id=1, source_target_pairs={{0,1},{1,0},{2,3},{3,2},{4,5},{5,4},{6,7},{7,6},{8,9},{9,8},{10,11... | collective-permute-start | bytes 786440 | tf_op jit(solution)/shard_map/ppermute | solution.py:328
  50.5 1.8 %collective-permute-start.5 = (bf16[1536,128]{1,0:T(8,128)(2,1)S(1)}, bf16[1536,128]{1,0:T(8,128)(2,1)S(1)}, u32[]{:S(2)}, u32[]{:S(2)}) collective-permute-start(bf16[1536,128]{1,0:T(8,128)(2,1)S(1)} %get-tuple-element.40), channel_id=1, source_target_pairs={{0,1},{1,0},{2,3},{3,2},{4,5},{5,4},{6,7},{7,6},{8,9},{9,8},{10,11... | collective-permute-start | bytes 1179656 | tf_op jit(solution)/shard_map/ppermute | solution.py:340
  91.2 18.8 %copy-start.10 = (f32[2]{0:T(128)S(1)}, f32[2]{0:T(128)}, u32[]{:S(2)}) copy-start(f32[2]{0:T(128)} %constant.36.clone.factors) | copy-start | bytes 28
  92.1 14.2 %all-to-all-start.3 = ((bf16[16,144,128]{2,1,0:T(8,128)(2,1)}), bf16[16,144,128]{2,1,0:T(8,128)(2,1)S(1)}, u32[]{:S(2)}, u32[]{:S(2)}) async-start(bf16[16,144,128]{2,1,0:T(8,128)(2,1)} %shard_map.178), calls=%async_computation.3 | async-start | bytes 1179648 | tf_op jit(solution)/shard_map/all_to_all | solution.py:270
  106.3 5.4 %collective-permute-start.6 = (bf16[2304,128]{1,0:T(8,128)(2,1)S(1)}, bf16[2304,128]{1,0:T(8,128)(2,1)S(1)}, u32[]{:S(2)}, u32[]{:S(2)}) collective-permute-start(bf16[2304,128]{1,0:T(8,128)(2,1)S(1)} %bitcast.18), channel_id=1, source_target_pairs={{0,1},{1,0},{2,3},{3,2},{4,5},{5,4},{6,7},{7,6},{8,9},{9,8},{10,11... | collective-permute-start | bytes 1769480 | tf_op jit(solution)/shard_map/ppermute | solution.py:370

commit v8 on v7

--- a/solution.py
+++ b/solution.py
@@ -87,11 +87,12 @@
     for low, size in TILES:
         part = pl.ds(low, size)
         pre_act = dot(table_t[part, :], coeffs)
-        gate = logistic(pre_act)
-        slope = gate * (1.0 + pre_act * (1.0 - gate))
+        half = 0.5 * pre_act
+        bend = jnp.tanh(half)
+        slope = 1.0 + bend + half * (1.0 - bend * bend)
         grad_pre = (cotangent[part, :].astype(F32) * slope).astype(BF16)
         total += dot(table[:, part], grad_pre)
-    grad_coeffs = (total * scale).astype(BF16)
+    grad_coeffs = (total * (0.5 * scale)).astype(BF16)
     pair[mix.shape[0] :, :] = grad_coeffs
     grad_mix = dot_tb(grad_coeffs, w_mix[...])
     to_beyond[...] = (far_row * grad_mix).astype(BF16)

time: 114 us -> 114 us (level)
  no operation moved by 1% of the time
where the time goes in v8:
time: 114 us; the launch traced here: 113 us
  blocking collectives  38.4 us (34%)
  starting transfers between devices  32.3 us (28%)
  waiting for transfers between devices  21.8 us (19%)
  Pallas kernels  12.6 us (11%)
  matrix products  3.81 us (3%)
  other arithmetic  3.05 us (3%)
    all_to_all x2, blocking collectives, all_swap(): lax.all_to_all(blocks, axis, split_axis=0, concat_axis=0, tiled=True, axi...  38.4 us
    all_to_all x2, starting transfers between devices, all_swap(): lax.all_to_all(blocks, axis, split_axis=0, concat_axis=0, tiled=True, axi...  20.3 us
    all_to_all x2, waiting for transfers between devices, all_swap(): lax.all_to_all(blocks, axis, split_axis=0, concat_axis=0, tiled=True, axi...  16.8 us
    pallas_call x9, Pallas kernels, local_kernel(): pl.pallas_call(body, out_shape=out_shape, in_specs=in_specs, out_specs=ou...  12.6 us
    ppermute x2, starting transfers between devices, trade(): beyond = lax.ppermute(far, BOTH, links + [(j, i) for i, j in links])  7.14 us
    ppermute x1, starting transfers between devices, shards(): theirs = lax.ppermute(whole, 'blk', swap)  3.73 us
    ppermute x2, waiting for transfers between devices, trade(): beyond = lax.ppermute(far, BOTH, links + [(j, i) for i, j in links])  3.43 us
    dot_general x3, matrix products, dot(): return jnp.dot(a, b, preferred_element_type=F32)  2.78 us
  transfers between devices with their start and end apart: 9, of which 5 were waited for; matrix products, arithmetic and copies ran while one was open for 6% of the time, Pallas kernels for 5%

profile of v8, /device:TPU:1, one launch (start us, length us, event | category | flops | bytes accessed | tf_op | source)
XLA Modules:
  0.0 113.2 jit_solution(7483464538780087719)
XLA Ops:
  0.6 15.7 %all-to-all-start = ((bf16[256,2,128]{2,1,0:T(2,128)(2,1)}), bf16[256,2,128]{2,1,0:T(2,128)(2,1)S(1)}, u32[]{:S(2)}, u32[]{:S(2)}) async-start(bf16[256,2,128]{2,1,0:T(2,128)(2,1)} %bitcast.24), calls=%async_computation | async-start | bytes 262144 | tf_op jit(solution)/shard_map/all_to_all | solution.py:271
  16.3 0.8 iota_compare_fusion.7
  17.1 0.1 lt.29
  17.3 0.7 broadcast_select_fusion
  17.9 0.9 convert_reduce_fusion
  18.9 0.1 copy.26.share
  19.1 1.9 %fusion.7 = bf16[512,256]{0,1:T(8,128)(2,1)S(1)} fusion(bf16[256,1440]{1,0:T(8,128)(2,1)} %constant.33.clone.table, s32[512]{0:T(512)S(1)} %broadcast_select_fusion), kind=kOutput, calls=%fused_computation.9 | convolution fusion | flops 378355712 | bytes 1001472 | tf_op jit(solution)/shard_map/dot_general | solution.py:23
  20.9 8.2 %all-to-all-done = bf16[256,2,128]{2,1,0:T(2,128)(2,1)S(1)} async-done(((bf16[256,2,128]{2,1,0:T(2,128)(2,1)}), bf16[256,2,128]{2,1,0:T(2,128)(2,1)S(1)}, u32[]{:S(2)}, u32[]{:S(2)}) %all-to-all-start) | async-done | bytes 131104 | tf_op jit(solution)/shard_map/all_to_all | solution.py:271
  29.2 0.6 fusion.6.latent
  29.9 0.3 fusion.11
  30.2 3.6 %collective-permute-start.1 = (bf16[256,512]{1,0:T(8,128)(2,1)S(1)}, bf16[256,512]{1,0:T(8,128)(2,1)S(1)}, u32[]{:S(2)}, u32[]{:S(2)}) collective-permute-start(bf16[256,512]{1,0:T(8,128)(2,1)S(1)} %get-tuple-element.51), channel_id=1, source_target_pairs={{1,2},{3,4},{5,6},{7,8},{9,10},{11,12},{13,14},{15,16},{17,18},{19... | collective-permute-start | bytes 786440 | tf_op jit(solution)/shard_map/ppermute | solution.py:265
  33.9 0.6 fusion.1.onehot
  34.6 3.4 %collective-permute-done.1.beyond = bf16[256,512]{1,0:T(8,128)(2,1)S(1)} collective-permute-done((bf16[256,512]{1,0:T(8,128)(2,1)S(1)}, bf16[256,512]{1,0:T(8,128)(2,1)S(1)}, u32[]{:S(2)}, u32[]{:S(2)}) %collective-permute-start.1) | collective-permute-done | bytes 262176 | tf_op jit(solution)/shard_map/ppermute | solution.py:265
  38.1 2.5 %shard_map.173 = (bf16[512,512]{1,0:T(8,128)(2,1)S(1)}, bf16[256,512]{1,0:T(8,128)(2,1)S(1)}, bf16[256,512]{1,0:T(8,128)(2,1)S(1)}, bf16[256,512]{1,0:T(8,128)(2,1)S(1)}) custom-call(s32[1]{0:T(128)} %bitcast.2.core, f32[256,512]{1,0:T(8,128)S(1)} %get-tuple-element.52.spectrum, bf16[256,512]{1,0:T(8,128)(2,1)S(1)} %collective-permute-done.inside, ...), custom_call_target="tpu_custom_call" | custom-call | flops 754974720 | bytes 4423680 | tf_op jit(solution)/shard_map/pallas_call | solution.py:46
  40.6 3.5 %collective-permute-start.3 = (bf16[256,512]{1,0:T(8,128)(2,1)S(1)}, bf16[256,512]{1,0:T(8,128)(2,1)S(1)}, u32[]{:S(2)}, u32[]{:S(2)}) collective-permute-start(bf16[256,512]{1,0:T(8,128)(2,1)S(1)} %get-tuple-element.35), channel_id=1, source_target_pairs={{1,2},{3,4},{5,6},{7,8},{9,10},{11,12},{13,14},{15,16},{17,18},{19... | collective-permute-start | bytes 786440 | tf_op jit(solution)/shard_map/ppermute | solution.py:265
  44.2 2.6 %shard_map.174 = (bf16[1440,512]{1,0:T(8,128)(2,1)}, f32[1024,128]{1,0:T(8,128)S(1)}, bf16[1024,128]{1,0:T(8,128)(2,1)S(1)}) custom-call(s32[1]{0:T(128)} %bitcast.2.core, bf16[1440,256]{1,0:T(8,128)(2,1)S(1)} %copy-done.4, bf16[256,512]{1,0:T(8,128)(2,1)S(1)} %get-tuple-element.30.coeffs, bf16[1440,512]{1,0:T(8,128)(2,1)S(1)} %fusion.1.onehot, ...), custom_call_target="tpu_custom_call" | custom-call | flops 1132462080 | bytes 4423680 | tf_op jit(solution)/shard_map/pallas_call | solution.py:46
  46.9 0.5 collective-permute-start.2
  47.4 1.0 fusion.5.slot_cot
  48.4 0.1 collective-permute-done.2.blend_got
  48.5 2.0 %shard_map.175 = (bf16[1536,128]{1,0:T(8,128)(2,1)S(1)}, f32[1280,128]{1,0:T(8,128)S(1)}, bf16[256,128]{1,0:T(8,128)(2,1)S(1)}) custom-call(s32[1]{0:T(128)} %bitcast.2.core, bf16[256,512]{1,0:T(8,128)(2,1)S(1)} %collective-permute-done.3.from_beyond, bf16[256,512]{1,0:T(8,128)(2,1)S(1)} %collective-permute-done.4.from_inside, f32[512,1]{1,0:T(8,128)S(1)} %copy.26.share, ...), custom_call_target="tpu_custom_call" | custom-call | flops 786432000 | bytes 1572864 | tf_op jit(solution)/shard_map/pallas_call | solution.py:46
  50.5 0.5 collective-permute-start.5
  51.0 1.3 %collective-permute-done.5.got = bf16[1536,128]{1,0:T(8,128)(2,1)S(1)} collective-permute-done((bf16[1536,128]{1,0:T(8,128)(2,1)S(1)}, bf16[1536,128]{1,0:T(8,128)(2,1)S(1)}, u32[]{:S(2)}, u32[]{:S(2)}) %collective-permute-start.5) | collective-permute-done | bytes 393248 | tf_op jit(solution)/shard_map/ppermute | solution.py:341
  52.4 23.2 %all_to_all.20.got = bf16[16,176,128]{2,1,0:T(8,128)(2,1)S(1)} all-to-all(bf16[16,176,128]{2,1,0:T(8,128)(2,1)S(1)} %shard_map.176), channel_id=1, replica_groups=mesh['enc'=16,'blk'=16] {'enc'}, dimensions={0} | all-to-all | bytes 1441792 | tf_op jit(solution)/shard_map/all_to_all | solution.py:271
  75.6 0.3 shard_map.177
  76.0 15.2 %all_to_all.21.got = bf16[8,208,128]{2,1,0:T(8,128)(2,1)S(1)} all-to-all(bf16[8,208,128]{2,1,0:T(8,128)(2,1)S(1)} %shard_map.177), channel_id=1, replica_groups={{0,2,4,6,8,10,12,14},{1,3,5,7,9,11,13,15},{16,18,20,22,24,26,28,30},{17..., dimensions={0} | all-to-all | bytes 851968 | tf_op jit(solution)/shard_map/all_to_all | solution.py:271
  91.2 0.9 shard_map.178
  92.1 4.6 %all-to-all-start.3 = ((bf16[16,144,128]{2,1,0:T(8,128)(2,1)}), bf16[16,144,128]{2,1,0:T(8,128)(2,1)S(1)}, u32[]{:S(2)}, u32[]{:S(2)}) async-start(bf16[16,144,128]{2,1,0:T(8,128)(2,1)} %shard_map.178), calls=%async_computation.3 | async-start | bytes 1179648 | tf_op jit(solution)/shard_map/all_to_all | solution.py:271
  96.7 1.0 shard_map.179
  97.6 8.6 %all-to-all-done.3 = bf16[16,144,128]{2,1,0:T(8,128)(2,1)S(1)} async-done(((bf16[16,144,128]{2,1,0:T(8,128)(2,1)}), bf16[16,144,128]{2,1,0:T(8,128)(2,1)S(1)}, u32[]{:S(2)}, u32[]{:S(2)}) %all-to-all-start.3) | async-done | bytes 589856 | tf_op jit(solution)/shard_map/all_to_all | solution.py:271
  106.3 3.7 %collective-permute-start.6 = (bf16[2304,128]{1,0:T(8,128)(2,1)S(1)}, bf16[2304,128]{1,0:T(8,128)(2,1)S(1)}, u32[]{:S(2)}, u32[]{:S(2)}) collective-permute-start(bf16[2304,128]{1,0:T(8,128)(2,1)S(1)} %bitcast.18), channel_id=1, source_target_pairs={{0,1},{1,0},{2,3},{3,2},{4,5},{5,4},{6,7},{7,6},{8,9},{9,8},{10,11... | collective-permute-start | bytes 1769480 | tf_op jit(solution)/shard_map/ppermute | solution.py:371
  110.0 1.6 %shard_map.180 = (f32[128,512]{1,0:T(8,128)}, f32[512,512]{1,0:T(8,128)}, f32[512,512]{1,0:T(8,128)}) custom-call(f32[2]{0:T(128)S(1)} %copy-done.10, s32[1]{0:T(128)} %bitcast.2.core, bf16[2304,128]{1,0:T(8,128)(2,1)S(1)} %bitcast.19), custom_call_target="tpu_custom_call" | custom-call | flops 1179648 | bytes 2359296 | tf_op jit(solution)/shard_map/pallas_call | solution.py:46
  111.6 1.6 %shard_map.181 = (f32[128,512]{1,0:T(8,128)}, f32[512,512]{1,0:T(8,128)}, f32[512,512]{1,0:T(8,128)}) custom-call(f32[2]{0:T(128)S(1)} %copy-done.10, s32[1]{0:T(128)} %bitcast.2.core, bf16[2304,128]{1,0:T(8,128)(2,1)S(1)} %collective-permute-done.6.half, ...), custom_call_target="tpu_custom_call", output_to_operand_aliasing={{0}: (3, {}), {1}: (4, {}), {2}: (5, {})} | custom-call | flops 1179648 | bytes 2359296 | tf_op jit(solution)/shard_map/pallas_call | solution.py:46
  (30 shorter events, 0.4 us)
Async XLA Ops:
  0.6 28.5 %all-to-all-start = ((bf16[256,2,128]{2,1,0:T(2,128)(2,1)}), bf16[256,2,128]{2,1,0:T(2,128)(2,1)S(1)}, u32[]{:S(2)}, u32[]{:S(2)}) async-start(bf16[256,2,128]{2,1,0:T(2,128)(2,1)} %bitcast.24), calls=%async_computation | async-start | bytes 262144 | tf_op jit(solution)/shard_map/all_to_all | solution.py:271
  18.9 10.3 %copy-start.5 = (bf16[512,512]{1,0:T(8,128)(2,1)S(1)}, bf16[512,512]{1,0:T(8,128)(2,1)}, u32[]{:S(2)}) copy-start(bf16[512,512]{1,0:T(8,128)(2,1)} %w_out.1) | copy-start | bytes 1572868
  18.9 10.3 %copy-start.6 = (bf16[128,512]{1,0:T(8,128)(2,1)S(1)}, bf16[128,512]{1,0:T(8,128)(2,1)}, u32[]{:S(2)}) copy-start(bf16[128,512]{1,0:T(8,128)(2,1)} %w_in.1) | copy-start | bytes 393220
  29.2 8.8 %copy-start.3 = (bf16[256,1440]{1,0:T(8,128)(2,1)S(1)}, bf16[256,1440]{1,0:T(8,128)(2,1)}, u32[]{:S(2)}) copy-start(bf16[256,1440]{1,0:T(8,128)(2,1)} %constant.33.clone.table) | copy-start | bytes 2211844
  29.2 8.8 %copy-start.4 = (bf16[1440,256]{1,0:T(8,128)(2,1)S(1)}, bf16[1440,256]{1,0:T(8,128)(2,1)}, u32[]{:S(2)}) copy-start(bf16[1440,256]{1,0:T(8,128)(2,1)} %constant.34.clone.table_t) | copy-start | bytes 2211844
  29.8 8.2 %copy-start = (f32[256,512]{1,0:T(8,128)S(1)}, f32[256,512]{1,0:T(8,128)}, u32[]{:S(2)}) copy-start(f32[256,512]{1,0:T(8,128)} %w_spec.3) | copy-start | bytes 1572868
  29.8 8.2 %copy-start.1 = (bf16[512,512]{1,0:T(8,128)(2,1)S(1)}, bf16[512,512]{1,0:T(8,128)(2,1)}, u32[]{:S(2)}) copy-start(bf16[512,512]{1,0:T(8,128)(2,1)} %w_mix.3) | copy-start | bytes 1572868
  29.8 8.2 %copy-start.2 = (bf16[1,1440,512]{2,1,0:T(8,128)(2,1)S(1)}, bf16[1,1440,512]{2,1,0:T(8,128)(2,1)}, u32[]{:S(2)}) copy-start(bf16[1,1440,512]{2,1,0:T(8,128)(2,1)} %param.23) | copy-start | bytes 4423684
  29.8 8.2 %copy-start.7 = (f32[256,1]{1,0:T(8,128)S(1)}, f32[256,1]{1,0:T(8,128)}, u32[]{:S(2)}) copy-start(f32[256,1]{1,0:T(8,128)} %constant.35.clone.weight) | copy-start | bytes 3076
  29.8 8.2 %copy-start.8 = (f32[1,512]{1,0:T(1,128)S(1)}, f32[1,512]{1,0:T(1,128)}, u32[]{:S(2)}) copy-start(f32[1,512]{1,0:T(1,128)} %north.1) | copy-start | bytes 6148
  29.9 8.2 %copy-start.9 = (f32[1,512]{1,0:T(1,128)S(1)}, f32[1,512]{1,0:T(1,128)}, u32[]{:S(2)}) copy-start(f32[1,512]{1,0:T(1,128)} %south.1) | copy-start | bytes 6148
  30.2 7.8 %collective-permute-start.1 = (bf16[256,512]{1,0:T(8,128)(2,1)S(1)}, bf16[256,512]{1,0:T(8,128)(2,1)S(1)}, u32[]{:S(2)}, u32[]{:S(2)}) collective-permute-start(bf16[256,512]{1,0:T(8,128)(2,1)S(1)} %get-tuple-element.51), channel_id=1, source_target_pairs={{1,2},{3,4},{5,6},{7,8},{9,10},{11,12},{13,14},{15,16},{17,18},{19... | collective-permute-start | bytes 786440 | tf_op jit(solution)/shard_map/ppermute | solution.py:265
  33.8 4.2 %collective-permute-start = (bf16[256,512]{1,0:T(8,128)(2,1)S(1)}, bf16[256,512]{1,0:T(8,128)(2,1)S(1)}, u32[]{:S(2)}, u32[]{:S(2)}) collective-permute-start(bf16[256,512]{1,0:T(8,128)(2,1)S(1)} %get-tuple-element.51), channel_id=1, source_target_pairs={{0,1},{1,0},{2,3},{3,2},{4,5},{5,4},{6,7},{7,6},{8,9},{9,8},{10,11... | collective-permute-start | bytes 786440 | tf_op jit(solution)/shard_map/ppermute | solution.py:266
  40.6 7.9 %collective-permute-start.3 = (bf16[256,512]{1,0:T(8,128)(2,1)S(1)}, bf16[256,512]{1,0:T(8,128)(2,1)S(1)}, u32[]{:S(2)}, u32[]{:S(2)}) collective-permute-start(bf16[256,512]{1,0:T(8,128)(2,1)S(1)} %get-tuple-element.35), channel_id=1, source_target_pairs={{1,2},{3,4},{5,6},{7,8},{9,10},{11,12},{13,14},{15,16},{17,18},{19... | collective-permute-start | bytes 786440 | tf_op jit(solution)/shard_map/ppermute | solution.py:265
  44.1 4.4 %collective-permute-start.4 = (bf16[256,512]{1,0:T(8,128)(2,1)S(1)}, bf16[256,512]{1,0:T(8,128)(2,1)S(1)}, u32[]{:S(2)}, u32[]{:S(2)}) collective-permute-start(bf16[256,512]{1,0:T(8,128)(2,1)S(1)} %get-tuple-element.36), channel_id=1, source_target_pairs={{0,1},{1,0},{2,3},{3,2},{4,5},{5,4},{6,7},{7,6},{8,9},{9,8},{10,11... | collective-permute-start | bytes 786440 | tf_op jit(solution)/shard_map/ppermute | solution.py:266
  46.9 1.7 %collective-permute-start.2 = (bf16[1024,128]{1,0:T(8,128)(2,1)S(1)}, bf16[1024,128]{1,0:T(8,128)(2,1)S(1)}, u32[]{:S(2)}, u32[]{:S(2)}) collective-permute-start(bf16[1024,128]{1,0:T(8,128)(2,1)S(1)} %get-tuple-element.33), channel_id=1, source_target_pairs={{0,1},{1,0},{2,3},{3,2},{4,5},{5,4},{6,7},{7,6},{8,9},{9,8},{10,11... | collective-permute-start | bytes 786440 | tf_op jit(solution)/shard_map/ppermute | solution.py:329
  50.5 1.8 %collective-permute-start.5 = (bf16[1536,128]{1,0:T(8,128)(2,1)S(1)}, bf16[1536,128]{1,0:T(8,128)(2,1)S(1)}, u32[]{:S(2)}, u32[]{:S(2)}) collective-permute-start(bf16[1536,128]{1,0:T(8,128)(2,1)S(1)} %get-tuple-element.40), channel_id=1, source_target_pairs={{0,1},{1,0},{2,3},{3,2},{4,5},{5,4},{6,7},{7,6},{8,9},{9,8},{10,11... | collective-permute-start | bytes 1179656 | tf_op jit(solution)/shard_map/ppermute | solution.py:341
  91.2 18.8 %copy-start.10 = (f32[2]{0:T(128)S(1)}, f32[2]{0:T(128)}, u32[]{:S(2)}) copy-start(f32[2]{0:T(128)} %constant.36.clone.factors) | copy-start | bytes 28
  92.1 14.2 %all-to-all-start.3 = ((bf16[16,144,128]{2,1,0:T(8,128)(2,1)}), bf16[16,144,128]{2,1,0:T(8,128)(2,1)S(1)}, u32[]{:S(2)}, u32[]{:S(2)}) async-start(bf16[16,144,128]{2,1,0:T(8,128)(2,1)} %shard_map.178), calls=%async_computation.3 | async-start | bytes 1179648 | tf_op jit(solution)/shard_map/all_to_all | solution.py:271
  106.3 5.4 %collective-permute-start.6 = (bf16[2304,128]{1,0:T(8,128)(2,1)S(1)}, bf16[2304,128]{1,0:T(8,128)(2,1)S(1)}, u32[]{:S(2)}, u32[]{:S(2)}) collective-permute-start(bf16[2304,128]{1,0:T(8,128)(2,1)S(1)} %bitcast.18), channel_id=1, source_target_pairs={{0,1},{1,0},{2,3},{3,2},{4,5},{5,4},{6,7},{7,6},{8,9},{9,8},{10,11... | collective-permute-start | bytes 1769480 | tf_op jit(solution)/shard_map/ppermute | solution.py:371
